TPU v7x, 512 devices: a whole 4x8x8 slice. The times are simulated.
512 devices in a mesh: lat: 8 (over z_lo, x), lon: 16 (over y, core), head: 4 (over z_hi).
Axes of the slice: x: 4, y: 8, z: 8 (z_hi: 4, z_lo: 2; z = z_hi * 2 + z_lo), core: 2. Of those that a mesh axis runs over, the one named last changes fastest.
Arguments:
- inputs: bfloat16 [2, 48, 192, 512], P(None, 'lat', 'lon'), may hold values from -6 to 6
- cotangent: bfloat16 [2, 48, 192, 512], P(None, 'lat', 'lon'), may hold values from -6 to 6
- qkv_weight: bfloat16 [2, 512, 3, 512], P(None, None, None, 'head'), may hold values from -0.70710678 to 0.70710678
- proj_weight: bfloat16 [2, 512, 512], P(None, None, 'head'), may hold values from -0.25 to 0.25
- up_weight: bfloat16 [2, 512, 2048], P(None, None, 'head'), may hold values from -0.25 to 0.25
- down_weight: bfloat16 [2, 512, 2048], P(None, None, 'head'), may hold values from -0.125 to 0.125
- shift_labels: int32 [48, 192], P('lat', 'lon'), may hold values from 0 to 2
Outputs:
- layer_out: bfloat16 [2, 48, 192, 512], P(None, 'lat', 'lon')
- input_grad: bfloat16 [2, 48, 192, 512], P(None, 'lat', 'lon')
- qkv_grad: float32 [2, 512, 3, 512], P(None, ('lat', 'lon'), None, 'head')
- proj_grad: float32 [2, 512, 512], P(None, ('lat', 'lon'), 'head')
All inputs are finite; a program needn't handle non-finite values.
Results may differ from a plain program's by a relative error of at most 0.034.
Values may be sent and summed in bfloat16 or wider, within the bound.
No kernel may reach another device: no remote copies, remote signals or barrier semaphores. Data moves between devices by JAX's collectives and lax.ppermute only.
A program may use at most 64 MiB of HBM per device.

v0:
```python
from functools import partial

import jax
import jax.numpy as jnp
from jax import lax
from jax.sharding import PartitionSpec as P

HD = 64
WIN_LEV = 2
WIN_LAT = 6
WIN_LON = 12


EPSILON = 1e-05


def from_behind(shard, axis, by):
    peers = lax.axis_size(axis)
    return lax.ppermute(shard, axis, [(i, (i + by) % peers) for i in range(peers)])


def norm_rows(values):
    average = jnp.mean(values, axis=-1, keepdims=True)
    centred = values - average
    spread = jnp.mean(centred * centred, axis=-1, keepdims=True)
    return centred * lax.rsqrt(spread + EPSILON)


def norm_pull(stream, cotangent):
    _, pullback = jax.vjp(norm_rows, stream.astype(jnp.float32))
    return pullback(cotangent)[0]


def gelu_exact(values):
    return jax.nn.gelu(values, approximate=False)


def to_windows(grid_array):
    level_count, lat_rows, lon_cols, channels = grid_array.shape
    blocks = grid_array.reshape(
        level_count // WIN_LEV,
        WIN_LEV,
        lat_rows // WIN_LAT,
        WIN_LAT,
        lon_cols // WIN_LON,
        WIN_LON,
        channels,
    )
    blocks = blocks.transpose(0, 2, 4, 1, 3, 5, 6)
    return blocks.reshape(-1, WIN_LEV * WIN_LAT * WIN_LON, channels)


def from_windows(blocks, level_count, lat_rows, lon_cols):
    channels = blocks.shape[-1]
    grid_array = blocks.reshape(
        level_count // WIN_LEV,
        lat_rows // WIN_LAT,
        lon_cols // WIN_LON,
        WIN_LEV,
        WIN_LAT,
        WIN_LON,
        channels,
    )
    grid_array = grid_array.transpose(0, 3, 1, 4, 2, 5, 6)
    return grid_array.reshape(level_count, lat_rows, lon_cols, channels)


def attend(queries, keys_in, values, allowed):
    factor = queries.shape[-1] ** (-0.5)
    scores = (
        jnp.einsum("wqhd,wkhd->whqk", queries.astype(jnp.float32), keys_in.astype(jnp.float32))
        * factor
    )
    scores = jnp.where(allowed[:, None], scores, -1e30)
    highest = jnp.max(scores, axis=-1, keepdims=True)
    weights = jnp.exp(scores - highest)
    weights = weights / jnp.sum(weights, axis=-1, keepdims=True)
    rounded = lax.optimization_barrier(weights.astype(jnp.bfloat16)).astype(jnp.float32)
    return jnp.einsum("whqk,wkhd->wqhd", rounded, values.astype(jnp.float32))


def attention_map(packed, allowed):
    level_count, lat_rows, lon_cols, triple, head_width = packed.shape
    blocks = to_windows(packed.reshape(level_count, lat_rows, lon_cols, triple * head_width))
    blocks = blocks.reshape(blocks.shape[0], blocks.shape[1], triple, head_width // HD, HD)
    result = attend(blocks[:, :, 0], blocks[:, :, 1], blocks[:, :, 2], allowed)
    result = result.reshape(result.shape[0], result.shape[1], head_width)
    return from_windows(result, level_count, lat_rows, lon_cols)


def allowed_map(region, level_count):
    grid_array = jnp.broadcast_to(region[None, :, :, None], (level_count,) + region.shape + (1,))
    labels = to_windows(grid_array)[:, :, 0]
    return labels[:, :, None] == labels[:, None, :]


def to_extended(grid_array):
    lat_rows = grid_array.shape[1]
    lon_cols = grid_array.shape[2]
    rows_in = from_behind(grid_array[:, lat_rows - WIN_LAT // 2 :], "lat", 1)
    row_ext = jnp.concatenate([rows_in, grid_array[:, : lat_rows - WIN_LAT // 2]], axis=1)
    cols_in = from_behind(row_ext[:, :, lon_cols - WIN_LON // 2 :], "lon", 1)
    return jnp.concatenate([cols_in, row_ext[:, :, : lon_cols - WIN_LON // 2]], axis=2)


def from_extended(grid_array):
    cols_back = from_behind(grid_array[:, :, : WIN_LON // 2], "lon", -1)
    row_ext = jnp.concatenate([grid_array[:, :, WIN_LON // 2 :], cols_back], axis=2)
    rows_back = from_behind(row_ext[:, : WIN_LAT // 2], "lat", -1)
    return jnp.concatenate([row_ext[:, WIN_LAT // 2 :], rows_back], axis=1)


def head_reduce(partial_sum, finish, extras):
    summed = lax.psum(partial_sum.astype(jnp.bfloat16), "head").astype(jnp.float32)
    return finish(summed, extras)


def after_attention(summed, extras):
    middle = (extras[0].astype(jnp.float32) + summed).astype(jnp.bfloat16)
    return (middle, norm_rows(middle.astype(jnp.float32)).astype(jnp.bfloat16))


def after_mlp(summed, extras):
    return ((extras[0].astype(jnp.float32) + summed).astype(jnp.bfloat16),)


def after_norm(summed, extras):
    return ((extras[0].astype(jnp.float32) + norm_pull(extras[1], summed)).astype(jnp.bfloat16),)


def contract_last(left, right):
    return lax.dot_general(
        left, right, (((1,), (1,)), ((), ())), preferred_element_type=jnp.float32
    )


def contract_first(left, right):
    return lax.dot_general(
        left, right, (((0,), (0,)), ((), ())), preferred_element_type=jnp.float32
    )


def per_device(inputs, cotangent, qkv_weight, proj_weight, up_weight, down_weight, shift_labels):
    level_count, lat_rows, lon_cols, model_width = inputs.shape
    head_width = qkv_weight.shape[-1]
    edge_flag = ((jnp.arange(lat_rows) < WIN_LAT // 2) & (lax.axis_index("lat") == 0)).astype(
        jnp.int32
    )
    regions = (jnp.zeros((lat_rows, lon_cols), jnp.int32), shift_labels * 2 + edge_flag[:, None])
    stream_rows = inputs.reshape(-1, model_width)
    stores = []
    for layer_index in range(2):
        shifted = layer_index == 1
        pack_weight = qkv_weight[layer_index].reshape(model_width, 3 * head_width)
        normed = norm_rows(stream_rows.astype(jnp.float32)).astype(jnp.bfloat16)
        packed = jnp.dot(normed, pack_weight, preferred_element_type=jnp.float32).astype(
            jnp.bfloat16
        )
        if shifted:
            packed = to_extended(packed.reshape(level_count, lat_rows, lon_cols, 3 * head_width))
        packed = packed.reshape(level_count, lat_rows, lon_cols, 3, head_width)
        allowed = allowed_map(regions[layer_index], level_count)
        mixed_out = attention_map(packed, allowed).astype(jnp.bfloat16)
        if shifted:
            mixed_out = from_extended(mixed_out)
        mixed_rows = mixed_out.reshape(-1, head_width)
        partial_sum = contract_last(mixed_rows, proj_weight[layer_index])
        middle, second = head_reduce(partial_sum, after_attention, (stream_rows,))
        pre_act = jnp.dot(second, up_weight[layer_index], preferred_element_type=jnp.float32)
        activated = gelu_exact(pre_act).astype(jnp.bfloat16)
        partial_sum = contract_last(activated, down_weight[layer_index])
        (next_rows,) = head_reduce(partial_sum, after_mlp, (middle,))
        stores.append((stream_rows, normed, allowed, packed, mixed_rows, middle, pre_act))
        stream_rows = next_rows
    layer_out = stream_rows.reshape(inputs.shape)
    gradient = cotangent.reshape(-1, model_width)
    pack_list = [None, None]
    proj_list = [None, None]
    for layer_index in (1, 0):
        shifted = layer_index == 1
        entry_rows, normed, allowed, packed, mixed_rows, middle, pre_act = stores[layer_index]
        pack_weight = qkv_weight[layer_index].reshape(model_width, 3 * head_width)
        d_act = jnp.dot(gradient, down_weight[layer_index], preferred_element_type=jnp.float32)
        _, pullback = jax.vjp(gelu_exact, pre_act)
        d_pre = pullback(d_act)[0].astype(jnp.bfloat16)
        partial_sum = contract_last(d_pre, up_weight[layer_index])
        (mid_grad,) = head_reduce(partial_sum, after_norm, (gradient, middle))
        d_mixed = jnp.dot(
            mid_grad, proj_weight[layer_index], preferred_element_type=jnp.float32
        ).astype(jnp.bfloat16)
        proj_list[layer_index] = contract_first(mid_grad, mixed_rows)
        d_grid = d_mixed.reshape(level_count, lat_rows, lon_cols, head_width)
        if shifted:
            d_grid = to_extended(d_grid)
        _, pullback = jax.vjp(partial(attention_map, allowed=allowed), packed)
        d_pack = pullback(d_grid.astype(jnp.float32))[0]
        if shifted:
            d_pack = from_extended(d_pack.reshape(level_count, lat_rows, lon_cols, 3 * head_width))
        d_rows = d_pack.reshape(-1, 3 * head_width)
        pack_list[layer_index] = contract_first(normed, d_rows).reshape(model_width, 3, head_width)
        partial_sum = contract_last(d_rows, pack_weight)
        (gradient,) = head_reduce(partial_sum, after_norm, (mid_grad, entry_rows))
    token_total = level_count * lat_rows * lon_cols * lax.axis_size("lat") * lax.axis_size("lon")
    factor = float(token_total) ** (-0.5)
    pack_sum, proj_sum = (
        lax.psum_scatter(
            jnp.stack(pack_list, axis=0) * factor, ("lat", "lon"), scatter_dimension=1, tiled=True
        ),
        lax.psum_scatter(
            jnp.stack(proj_list, axis=0) * factor, ("lat", "lon"), scatter_dimension=1, tiled=True
        ),
    )
    return (layer_out, gradient.reshape(inputs.shape), pack_sum, proj_sum)


def solution(mesh):
    in_specs = (
        P(None, "lat", "lon", None),
        P(None, "lat", "lon", None),
        P(None, None, None, "head"),
        P(None, None, "head"),
        P(None, None, "head"),
        P(None, None, "head"),
        P("lat", "lon"),
    )
    out_specs = (
        P(None, "lat", "lon", None),
        P(None, "lat", "lon", None),
        P(None, ("lat", "lon"), None, "head"),
        P(None, ("lat", "lon"), "head"),
    )
    return jax.shard_map(
        per_device, mesh=mesh, in_specs=in_specs, out_specs=out_specs, check_vma=False
    )
```

profile of v0, /device:TPU:1, one launch (start us, length us, event | category | flops | bytes accessed | tf_op | source)
XLA Modules:
  0.0 1587.6 jit_solution(2668105444111213594)
XLA Ops:
  10.9 1.3 convert_reduce_fusion.3
  13.4 59.7 %all-reduce.19.cloned.1.call-done = bf16[144,512]{1,0:T(8,128)(2,1)} async-done(((bf16[144,512]{1,0:T(8,128)(2,1)}), bf16[144,512]{1,0:T(8,128)(2,1)}) %all-reduce.19.cloned.1.call-update) | async-done | bytes 147472 | tf_op jit(solution)/shard_map/psum | solution.py:114
  74.5 1.3 fusion.20
  76.5 1.5 convolution_convert_fusion.5
  78.3 54.1 %all-reduce.21.cloned.1.call-done = bf16[144,512]{1,0:T(8,128)(2,1)} async-done(((bf16[144,512]{1,0:T(8,128)(2,1)}), bf16[144,512]{1,0:T(8,128)(2,1)}) %all-reduce.21.cloned.1.call-update) | async-done | bytes 147472 | tf_op jit(solution)/shard_map/psum | solution.py:114
  134.2 3.1 collective-permute-start
  137.5 3.9 collective-permute-done
  141.4 4.9 collective-permute-start.1
  146.4 1.3 collective-permute-done.1
  149.0 1.3 convert_reduce_fusion.4
  150.9 2.5 collective-permute-start.2
  153.3 1.4 collective-permute-done.2
  154.8 2.4 collective-permute-start.3
  157.2 2.2 collective-permute-done.3
  161.3 51.7 %all-reduce.23.cloned.1.call-done = bf16[144,512]{1,0:T(8,128)(2,1)} async-done(((bf16[144,512]{1,0:T(8,128)(2,1)}), bf16[144,512]{1,0:T(8,128)(2,1)}) %all-reduce.23.cloned.1.call-update) | async-done | bytes 147472 | tf_op jit(solution)/shard_map/psum | solution.py:114
  214.3 2.0 fusion.14
  216.3 3.0 convolution_convert_fusion.3
  219.4 54.3 %all-reduce.25.cloned.1.call-done = bf16[144,512]{1,0:T(8,128)(2,1)} async-done(((bf16[144,512]{1,0:T(8,128)(2,1)}), bf16[144,512]{1,0:T(8,128)(2,1)}) %all-reduce.25.cloned.1.call-update) | async-done | bytes 147472 | tf_op jit(solution)/shard_map/psum | solution.py:114
  277.4 3.1 collective-permute-start.4
  280.5 3.6 collective-permute-done.4
  284.1 4.9 collective-permute-start.5
  295.6 2.4 collective-permute-start.6
  298.0 1.9 collective-permute-done.6
  300.0 2.4 collective-permute-start.7
  303.7 2.0 collective-permute-done.7
  306.8 2.6 convolution_convert_fusion.4
  309.4 49.3 %all-reduce.27.cloned.1.call-done = bf16[144,512]{1,0:T(8,128)(2,1)} async-done(((bf16[144,512]{1,0:T(8,128)(2,1)}), bf16[144,512]{1,0:T(8,128)(2,1)}) %all-reduce.27.cloned.1.call-update) | async-done | bytes 147472 | tf_op jit(solution)/shard_map/psum | solution.py:114
  362.2 2.9 convolution_convert_fusion.1
  366.1 53.4 %all-reduce.29.cloned.1.call-done = bf16[144,512]{1,0:T(8,128)(2,1)} async-done(((bf16[144,512]{1,0:T(8,128)(2,1)}), bf16[144,512]{1,0:T(8,128)(2,1)}) %all-reduce.29.cloned.1.call-update) | async-done | bytes 147472 | tf_op jit(solution)/shard_map/psum | solution.py:114
  432.4 50.6 %all-reduce.33.cloned.1.call-done = (bf16[144,512]{1,0:T(8,128)(2,1)}, bf16[144,512]{1,0:T(8,128)(2,1)}) async-done(((bf16[144,512]{1,0:T(8,128)(2,1)}, bf16[144,512]{1,0:T(8,128)(2,1)}), (bf16[144,512]{1,0:T(8,128)(2,1)}, bf16[144,512]{1,0:T(8,128)(2,1)})) %all-reduce.33.cloned.1.call-update) | async-done | bytes 294928 | tf_op jit(solution)/shard_map/psum | solution.py:114
  486.3 1091.9 %all-reduce.31.cloned.1.call-done = (f32[2,512,3,128]{3,1,2,0:T(8,128)}, f32[2,512,128]{2,1,0:T(8,128)}) async-done(((f32[2,512,3,128]{3,1,2,0:T(8,128)}, f32[2,512,128]{2,1,0:T(8,128)}), (f32[2,512,3,128]{3,1,2,0:T(8,128)}, f32[2,512,128]{2,1,0:T(8,128)})) %all-reduce.31.cloned.1.call-update) | async-done | bytes 2097168
  1578.1 1.3 constant_dynamic-slice_fusion.1
  (218 shorter events, 47.6 us)
Async XLA Ops:
  7.2 65.9 %all-reduce.19.cloned.1.call-start = ((), (), s32[]{:S(2)}) async-start(), calls=%async_computation | async-start | bytes 294912 | tf_op jit(solution)/shard_map/psum | solution.py:114
  12.4 63.4 %copy-start.7 = (bf16[2,64,144]{2,1,0:T(8,128)(2,1)}, bf16[2,64,144]{2,1,0:T(8,128)(2,1)S(1)}, u32[]{:S(2)}) copy-start(bf16[2,64,144]{2,1,0:T(8,128)(2,1)S(1)} %convolution_convert_fusion.19) | copy-start | bytes 110596
  13.3 119.1 %all-reduce.21.cloned.1.call-start = ((), (), s32[]{:S(2)}) async-start(), calls=%async_computation.1 | async-start | bytes 294912 | tf_op jit(solution)/shard_map/psum | solution.py:114
  73.1 3.4 copy-start.31
  74.4 3.5 copy-start.24
  74.4 3.5 copy-start.22
  78.0 59.3 %copy-start.30 = (s32[6,12]{1,0:T(8,128)S(1)}, s32[6,12]{1,0:T(8,128)}, u32[]{:S(2)}) copy-start(s32[6,12]{1,0:T(8,128)} %param.13) | copy-start | bytes 868
  78.0 135.0 %all-reduce.23.cloned.1.call-start = ((), (), s32[]{:S(2)}) async-start(), calls=%async_computation.2 | async-start | bytes 294912 | tf_op jit(solution)/shard_map/psum | solution.py:114
  133.6 14.6 copy-start.20
  134.2 7.2 collective-permute-start
  141.4 6.3 collective-permute-start.1
  150.9 3.9 collective-permute-start.2
  154.8 4.6 collective-permute-start.3
  160.3 113.4 %all-reduce.25.cloned.1.call-start = ((), (), s32[]{:S(2)}) async-start(), calls=%async_computation.3 | async-start | bytes 294912 | tf_op jit(solution)/shard_map/psum | solution.py:114
  161.3 58.0 %copy-start.4 = (bf16[144,512]{1,0:T(8,128)(2,1)}, bf16[144,512]{1,0:T(8,128)(2,1)S(1)}, u32[]{:S(2)}) copy-start(bf16[144,512]{1,0:T(8,128)(2,1)S(1)} %reshape.462) | copy-start | bytes 442372
  219.3 139.4 %all-reduce.27.cloned.1.call-start = ((), (), s32[]{:S(2)}) async-start(), calls=%async_computation.4 | async-start | bytes 294912 | tf_op jit(solution)/shard_map/psum | solution.py:114
  274.8 18.7 %copy-start.14 = (bf16[1,144,1,2,64]{1,4,3,2,0:T(8,128)(2,1)S(1)}, bf16[1,144,1,2,64]{1,4,3,2,0:T(8,128)(2,1)}, u32[]{:S(2)}) copy-start(bf16[1,144,1,2,64]{1,4,3,2,0:T(8,128)(2,1)} %copy-done.13) | copy-start | bytes 110596
  277.4 6.7 collective-permute-start.4
  284.1 5.8 collective-permute-start.5
  295.6 4.4 collective-permute-start.6
  300.0 5.7 collective-permute-start.7
  306.7 53.2 %copy-start.27 = (f32[144]{0:T(256)S(1)}, f32[144]{0:T(256)}, u32[]{:S(2)}) copy-start(f32[144]{0:T(256)} %copy-done.26) | copy-start | bytes 1732
  306.7 53.2 %copy-start.21 = (f32[144]{0:T(256)S(1)}, f32[144]{0:T(256)}, u32[]{:S(2)}) copy-start(f32[144]{0:T(256)} %copy-done.20) | copy-start | bytes 1732
  306.7 55.4 %copy-start.33 = (f32[144,512]{1,0:T(8,128)S(1)}, f32[144,512]{1,0:T(8,128)}, u32[]{:S(2)}) copy-start(f32[144,512]{1,0:T(8,128)} %copy-done.32) | copy-start | bytes 884740
  306.7 112.8 %all-reduce.29.cloned.1.call-start = ((), (), s32[]{:S(2)}) async-start(), calls=%async_computation.5 | async-start | bytes 294912 | tf_op jit(solution)/shard_map/psum | solution.py:114
  365.1 55.5 %copy-start.25 = (f32[144]{0:T(256)S(1)}, f32[144]{0:T(256)}, u32[]{:S(2)}) copy-start(f32[144]{0:T(256)} %copy-done.24) | copy-start | bytes 1732
  365.1 55.5 %copy-start.23 = (f32[144]{0:T(256)S(1)}, f32[144]{0:T(256)}, u32[]{:S(2)}) copy-start(f32[144]{0:T(256)} %copy-done.22) | copy-start | bytes 1732
  365.1 117.8 %all-reduce.33.cloned.1.call-start = ((), (), s32[]{:S(2)}) async-start(), calls=%async_computation.7 | async-start | bytes 589824 | tf_op jit(solution)/shard_map/psum | solution.py:114
  365.7 56.2 %copy-start.6 = (bf16[144,512]{1,0:T(8,128)(2,1)S(1)}, bf16[144,512]{1,0:T(8,128)(2,1)}, u32[]{:S(2)}) copy-start(bf16[144,512]{1,0:T(8,128)(2,1)} %copy-done.5) | copy-start | bytes 442372
  365.7 57.9 %copy-start.29 = (f32[2,144]{1,0:T(2,128)S(1)}, f32[2,144]{1,0:T(2,128)}, u32[]{:S(2)}) copy-start(f32[2,144]{1,0:T(2,128)} %multiply_divide_fusion) | copy-start | bytes 3460
  366.1 57.7 %copy-start.28 = (f32[2,144]{1,0:T(2,128)S(1)}, f32[2,144]{1,0:T(2,128)}, u32[]{:S(2)}) copy-start(f32[2,144]{1,0:T(2,128)} %get-tuple-element.22) | copy-start | bytes 3460
  426.8 1151.4 %all-reduce.31.cloned.1.call-start = ((), (), s32[]{:S(2)}) async-start(), calls=%async_computation.6 | async-start | bytes 4194304
  (18 other events, 34.2 us)
Sparse Core Ops, SparseCore 0:
  13.4 59.6 all-reduce.18
  78.1 54.2 all-reduce.20
  160.4 52.5 all-reduce.22
  219.4 54.2 all-reduce.24
  306.8 51.8 all-reduce.26
  365.3 54.2 all-reduce.28
  426.9 55.9 all-reduce.32
  485.9 1092.2 all-reduce.30
where the time goes:
time: 1590 us
  waiting for transfers between devices  1480 us (93%)
  starting transfers between devices  26.2 us (2%)
  other arithmetic  26.1 us (2%)
  matrix products  23.7 us (1%)
    unnamed x9, waiting for transfers between devices  1090 us
    psum x7, waiting for transfers between devices, head_reduce(): lax.psum(partial_sum.astype(jnp.bfloat16), 'head').astype(jnp.float32)  373 us
  transfers between devices with their start and end apart: 16, of which 16 were waited for; matrix products, arithmetic and copies ran while one was open for 1% of the time, Pallas kernels for 0%

commit v1 on v0

v1 whole, which is shorter than its diff:
```python
from functools import partial

import jax
import jax.numpy as jnp
import numpy as np
from jax import lax
from jax.experimental import pallas as pl
from jax.experimental.pallas import tpu as pltpu
from jax.sharding import PartitionSpec as P

HD = 64
EPSILON = 1e-05
PARTS = 4
BF = jnp.bfloat16
F32 = jnp.float32


def norm_rows(values):
    average = jnp.mean(values, axis=-1, keepdims=True)
    centred = values - average
    spread = jnp.mean(centred * centred, axis=-1, keepdims=True)
    return centred * lax.rsqrt(spread + EPSILON)


def norm_pull(stream, cotangent):
    stream = stream.astype(F32)
    average = jnp.mean(stream, axis=-1, keepdims=True)
    centred = stream - average
    spread = jnp.mean(centred * centred, axis=-1, keepdims=True)
    inverse = lax.rsqrt(spread + EPSILON)
    unit = centred * inverse
    mean_c = jnp.mean(cotangent, axis=-1, keepdims=True)
    mean_u = jnp.mean(cotangent * unit, axis=-1, keepdims=True)
    return inverse * (cotangent - mean_c - unit * mean_u)


def dot(left, right, left_dim, right_dim):
    return lax.dot_general(
        left, right, (((left_dim,), (right_dim,)), ((), ())), preferred_element_type=F32
    )


def gelu_and_slope(pre):
    cdf = 0.5 * (1.0 + lax.erf(pre * 0.7071067811865476))
    density = jnp.exp(-0.5 * pre * pre) * 0.3989422804014327
    return pre * cdf, cdf + pre * density


def quads(grid):
    channels = grid.shape[-1]
    return (
        grid.reshape(-1, 2, 3, 2, 6, channels).transpose(1, 3, 0, 2, 4, 5).reshape(PARTS, -1, channels)
    )


def unquads(rows):
    channels = rows.shape[-1]
    return (
        rows.reshape(2, 2, -1, 3, 6, channels)
        .transpose(2, 0, 3, 1, 4, 5)
        .reshape(-1, 6, 12, channels)
    )


def joint(sizes, move):
    pairs = []
    for source in np.ndindex(*sizes):
        target = [t % s for t, s in zip(move(*source), sizes)]
        pairs.append((int(np.ravel_multi_index(source, sizes)), int(np.ravel_multi_index(target, sizes))))
    return pairs


def after(value, *others):
    return lax.optimization_barrier((value,) + others)[0]


def send_quads(pieces, sign):
    sizes = (lax.axis_size("lat"), lax.axis_size("lon"))
    out = [pieces[0]]
    for q in (3, 2, 1):
        perm = joint(sizes, lambda a, b: (a + sign * (q // 2), b + sign * (q % 2)))
        out.insert(1, lax.ppermute(pieces[q], ("lat", "lon"), perm))
    return out


def lat_parts():
    lats = lax.axis_size("lat")
    return 2, lats // 2


def fetch_heads(shard, gate=()):
    low, ring = lat_parts()
    sizes = (low * ring, lax.axis_size("head"))
    shard = after(shard, *gate)

    def odd(hops):
        def move(a, h):
            low_now, x = divmod(a, ring)
            return ((1 - low_now) * ring + x, h + (hops if low_now else -hops))

        return joint(sizes, move)

    def even(a, h):
        return (a, h + (1 if a // ring else -1))

    three = lax.ppermute(shard, ("lat", "head"), odd(2))
    two = lax.ppermute(shard, ("lat", "head"), joint(sizes, even))
    one = lax.ppermute(shard, ("lat", "head"), odd(1))
    return one, two, three


def swap_cores(piece):
    size = lax.axis_size("lon")
    return lax.ppermute(piece, "lon", [(i, i ^ 1) for i in range(size)])


def ring_x(own, long_way, gates=((), ())):
    low, ring = lat_parts()
    size = lax.axis_size("lat")

    def pairs(by):
        return [(i, i // ring * ring + (i + by) % ring) for i in range(size)]

    blocks = {0: own}
    for sign, gate in zip((long_way, -long_way), gates):
        if ring > 2 or sign == long_way:
            sent = after(own, *gate)
            blocks[sign % ring] = lax.ppermute(sent, "lat", pairs(sign))
    if ring > 2:
        blocks[2] = lax.ppermute(blocks[long_way % ring], "lat", pairs(long_way))
    return [blocks[s] for s in range(ring)]


def shard_kernel(ring, qkv_ref, proj_ref, up_ref, down_ref, *refs):
    out_refs, sem = refs[:-1], refs[-1]
    rows, half = out_refs[0].shape
    side = lax.axis_index("lon") % 2
    start = pl.multiple_of(lax.axis_index("lat") % ring * rows, rows)
    width, hidden = proj_ref.shape[2], up_ref.shape[2]
    split = half - 4 * width

    def run(views):
        copies = []
        for layer, out_ref in enumerate(out_refs):
            at = 0
            for view in views(layer):
                target = out_ref.at[:, pl.ds(at, view.shape[1])]
                copies.append(pltpu.make_async_copy(view, target, sem.at[len(copies)]))
                at += view.shape[1]
        for copy in copies:
            copy.start()
        for copy in copies:
            copy.wait()

    @pl.when(side == 0)
    def _():
        run(
            lambda layer: [qkv_ref.at[layer, i, pl.ds(start, rows), :] for i in range(3)]
            + [proj_ref.at[layer, pl.ds(start, rows), :], up_ref.at[layer, pl.ds(start, rows), pl.ds(0, split)]]
        )

    @pl.when(side == 1)
    def _():
        run(
            lambda layer: [
                up_ref.at[layer, pl.ds(start, rows), pl.ds(split, hidden - split)],
                down_ref.at[layer, pl.ds(start, rows), :],
            ]
        )


def weight_shards(own):
    ring = lat_parts()[1]
    columns = 4 * own[1].shape[2] + 2 * own[2].shape[2]
    shard = jax.ShapeDtypeStruct((own[1].shape[1] // ring, columns // 2), BF)
    return pl.pallas_call(
        partial(shard_kernel, ring),
        out_shape=[shard] * 2,
        in_specs=hbm_specs(4),
        out_specs=vmem_specs(2),
        scratch_shapes=[pltpu.SemaphoreType.DMA((10,))],
        compiler_params=pltpu.CompilerParams(vmem_limit_bytes=58 * 1024 * 1024),
    )(*own)


def load_weights(layer, piece_refs, own_refs, w_ref, sem):
    ring = len(piece_refs) // 2
    rows, half = piece_refs[0].shape[1:]
    core = lax.axis_index("lon") % 2
    place = lax.axis_index("lat") % ring
    copies = []
    at = 0
    for ref in own_refs:
        views = [ref.at[layer, i] for i in range(3)] if len(ref.shape) == 4 else [ref.at[layer]]
        for view in views:
            copies.append((view, w_ref.at[0, :, pl.ds(at, view.shape[1])]))
            at += view.shape[1]
    for s in range(ring):
        start = pl.multiple_of((place - s + ring) % ring * rows, rows)
        for side, ref in ((core, piece_refs[s]), (1 - core, piece_refs[ring + s])):
            columns = pl.ds(pl.multiple_of(side * half, half), half)
            copies.append((ref, w_ref.at[pl.ds(1, PARTS - 1), pl.ds(start, rows), columns]))
    copies = [pltpu.make_async_copy(s, d, sem.at[i]) for i, (s, d) in enumerate(copies)]
    for copy in copies:
        copy.start()
    return copies


class Weights:
    def __init__(self, ref, ends):
        self.ref = ref
        self.ends = ends

    def get(self, k, which):
        return self.ref[k, :, self.ends[which] : self.ends[which + 1]]

    qkv = lambda self, k: self.get(k, 0)
    proj = lambda self, k: self.get(k, 1)
    up = lambda self, k: self.get(k, 2)
    down = lambda self, k: self.get(k, 3)


def head_parts(packed, a):
    width = packed.shape[1] // 3
    return tuple(packed[:, i * width + a * HD : i * width + (a + 1) * HD] for i in range(3))


def forward(x, weights, allowed, packed_ref, probs_ref, mixed_ref, slope_ref):
    normed = norm_rows(x).astype(BF)
    total = jnp.zeros(x.shape, F32)
    for k in range(PARTS):
        packed = dot(normed, weights.qkv(k), 1, 0).astype(BF)
        packed_ref[k] = packed
        count = packed.shape[1] // (3 * HD)
        outs = []
        for a in range(count):
            queries, keys, values = head_parts(packed, a)
            scores = dot(queries, keys, 1, 1) * HD**-0.5
            if allowed is not None:
                scores = jnp.where(allowed, scores, -1e30)
            exps = jnp.exp(scores - jnp.max(scores, axis=-1, keepdims=True))
            probs = exps / jnp.sum(exps, axis=-1, keepdims=True)
            probs_ref[k * count + a] = probs
            outs.append(dot(probs.astype(BF), values, 1, 0))
        mixed = jnp.concatenate(outs, axis=1).astype(BF)
        if k == 0:
            mixed_ref[...] = mixed
        total += dot(mixed, weights.proj(k), 1, 1)
    middle = (x + total).astype(BF)
    second = norm_rows(middle.astype(F32)).astype(BF)
    total = jnp.zeros(x.shape, F32)
    for k in range(PARTS):
        active, slope = gelu_and_slope(dot(second, weights.up(k), 1, 0))
        slope_ref[k] = slope
        total += dot(active.astype(BF), weights.down(k), 1, 1)
    return middle, (middle.astype(F32) + total).astype(BF)


def backward(x, middle, gradient, weights, factor, packed_ref, probs_ref, mixed_ref, slope_ref, sums_ref):
    middle = middle.astype(F32)
    total = jnp.zeros(x.shape, F32)
    for k in range(PARTS):
        d_pre = (slope_ref[k] * dot(gradient, weights.down(k), 1, 0)).astype(BF)
        total += dot(d_pre, weights.up(k), 1, 1)
    mid_grad = (gradient.astype(F32) + norm_pull(middle, total)).astype(BF)
    total = jnp.zeros(x.shape, F32)
    for k in range(PARTS):
        d_mixed = dot(mid_grad, weights.proj(k), 1, 0).astype(BF)
        packed = packed_ref[k]
        width = d_mixed.shape[1]
        count = width // HD
        parts = [[], [], []]
        for a in range(count):
            queries, keys, values = head_parts(packed, a)
            d_out = d_mixed[:, a * HD : (a + 1) * HD]
            probs = probs_ref[k * count + a]
            d_probs = dot(d_out, values, 1, 1)
            d_scores = probs * (d_probs - jnp.sum(d_probs * probs, axis=-1, keepdims=True))
            d_scores = (d_scores * HD**-0.5).astype(BF)
            parts[0].append(dot(d_scores, keys, 1, 0))
            parts[1].append(dot(d_scores, queries, 0, 0))
            parts[2].append(dot(probs.astype(BF), d_out, 0, 0))
        d_packed = jnp.concatenate(parts[0] + parts[1] + parts[2], axis=1).astype(BF)
        total += dot(d_packed, weights.qkv(k), 1, 1)
        if k == 0:
            normed = norm_rows(x).astype(BF)
            sums_ref[:, : 3 * width] = (dot(normed, d_packed, 0, 0) * factor).astype(BF)
            sums_ref[:, 3 * width :] = (dot(mid_grad, mixed_ref[...], 0, 0) * factor).astype(BF)
    return (mid_grad.astype(F32) + norm_pull(x, total)).astype(BF)


def first_kernel(pieces, ends, *refs):
    x_ref, refs = refs[0], refs[1:]
    piece_refs, own_refs, refs = refs[:pieces], refs[pieces : pieces + 4], refs[pieces + 4 :]
    out_refs, (w_ref, middle_ref, *saved), sem = refs[:PARTS], refs[PARTS:-1], refs[-1]
    copies = load_weights(0, piece_refs, own_refs, w_ref, sem)
    for copy in copies:
        copy.wait()
    middle, out = forward(x_ref[...].astype(F32), Weights(w_ref, ends), None, *saved)
    middle_ref[...] = middle
    rows = out.shape[0] // PARTS
    for q in range(PARTS):
        out_refs[q][...] = out[q * rows : (q + 1) * rows]


def second_kernel(pieces, ends, factor, *refs):
    x_refs, grad_refs, refs = refs[:PARTS], refs[PARTS : 2 * PARTS], refs[2 * PARTS :]
    column_ref, row_ref, *refs = refs
    piece_refs, own_refs, refs = refs[:pieces], refs[pieces : pieces + 4], refs[pieces + 4 :]
    out_refs, (sums_ref, w_ref, *saved), sem = refs[:PARTS], refs[PARTS:-1], refs[-1]
    copies = load_weights(1, piece_refs, own_refs, w_ref, sem)
    x = jnp.concatenate([ref[...].astype(F32) for ref in x_refs], axis=0)
    allowed = column_ref[...] == row_ref[...]
    for copy in copies:
        copy.wait()
    weights = Weights(w_ref, ends)
    middle, out = forward(x, weights, allowed, *saved)
    rows = out.shape[0] // PARTS
    for q in range(PARTS):
        out_refs[q][0] = out[q * rows : (q + 1) * rows]
    gradient = jnp.concatenate([ref[...].astype(F32) for ref in grad_refs], axis=0).astype(BF)
    result = backward(x, middle, gradient, weights, factor, *saved, sums_ref)
    for q in range(PARTS):
        out_refs[q][1] = result[q * rows : (q + 1) * rows]


def third_kernel(ends, factor, *refs):
    grad_refs, (x_ref, w_ref, middle_ref, *saved), (result_ref, sums_ref) = refs[:PARTS], refs[PARTS:-2], refs[-2:]
    gradient = jnp.concatenate([ref[1].astype(F32) for ref in grad_refs], axis=0).astype(BF)
    weights = Weights(w_ref, ends)
    result_ref[...] = backward(
        x_ref[...].astype(F32), middle_ref[...], gradient, weights, factor, *saved, sums_ref
    )


def vmem_specs(count):
    return [pl.BlockSpec(memory_space=pltpu.VMEM)] * count


def any_specs(count):
    return [pl.BlockSpec(memory_space=pl.ANY)] * count


def hbm_specs(count):
    return [pl.BlockSpec(memory_space=pltpu.HBM)] * count


PARAMS = pltpu.CompilerParams(vmem_limit_bytes=28 * 1024 * 1024)


def cost(flops):
    return pl.CostEstimate(flops=flops, bytes_accessed=8_000_000, transcendentals=600_000)


def scatter(parts, axis):
    size = lax.axis_size(axis)
    parts = parts.reshape(size, -1, parts.shape[-1])
    return jnp.sum(lax.all_to_all(parts, axis, 0, 0).astype(F32), axis=0)


def per_device(inputs, cotangent, qkv_weight, proj_weight, up_weight, down_weight, shift_labels):
    level_count, lat_rows, lon_cols, model_width = inputs.shape
    head_width = qkv_weight.shape[-1]
    tokens = level_count * lat_rows * lon_cols
    quarter = tokens // PARTS
    factor = float(tokens * lax.axis_size("lat") * lax.axis_size("lon")) ** -0.5

    own = (qkv_weight.swapaxes(1, 2), proj_weight, up_weight, down_weight)
    ends = [0, 3 * head_width, 4 * head_width]
    ends = ends + [ends[-1] + up_weight.shape[2], ends[-1] + 2 * up_weight.shape[2]]
    shards = weight_shards(own)
    early = fetch_heads(shards[0])
    ending = send_quads(list(after(quads(cotangent), early[0])), 1)
    edge = ((jnp.arange(lat_rows) < 3) & (lax.axis_index("lat") == 0)).astype(jnp.int32)
    region = jnp.broadcast_to((shift_labels * 2 + edge[:, None])[None, :, :, None], (level_count, 6, 12, 1))
    labels = quads(region)[::-1].reshape(-1)
    column, row = labels[:, None], labels[None, :]
    start = quads(inputs).reshape(tokens, model_width)
    early_block, start, column, row, *ending = lax.optimization_barrier(
        (jnp.stack(early), start, column, row, *ending)
    )
    early_ring = ring_x(early_block, 1)
    early_swaps = [swap_cores(early_block)]
    late = fetch_heads(shards[1], early_swaps[:1])
    late_ring = ring_x(jnp.stack(late), -1, (early_ring[1::2], early_ring[2:3]))
    early_swaps += [swap_cores(piece) for piece in early_ring[1:]]
    early_all = early_ring + early_swaps
    late_swaps = {s: swap_cores(late_ring[s]) for s in (0, len(late_ring) - 1)}
    start = after(start, *late_swaps.values())

    width = head_width // HD * PARTS
    stream = jax.ShapeDtypeStruct((tokens, model_width), BF)
    piece = jax.ShapeDtypeStruct((quarter, model_width), BF)
    pair = jax.ShapeDtypeStruct((2, quarter, model_width), BF)
    sums = jax.ShapeDtypeStruct((model_width, 4 * head_width), BF)
    full_weights = jax.ShapeDtypeStruct((PARTS, model_width, ends[-1]), BF)
    saved = [
        jax.ShapeDtypeStruct((PARTS, tokens, 3 * head_width), BF),
        jax.ShapeDtypeStruct((width, tokens, tokens), F32),
        jax.ShapeDtypeStruct((tokens, head_width), BF),
        jax.ShapeDtypeStruct((PARTS, tokens, up_weight.shape[2]), F32),
    ]
    pieces = len(early_all)
    semaphores = pltpu.SemaphoreType.DMA((pieces + 6,))

    *quarters, early_weights, middle, packed, probs, mixed, slope = pl.pallas_call(
        partial(first_kernel, pieces, ends),
        out_shape=[piece] * PARTS + [full_weights, stream] + saved,
        in_specs=vmem_specs(1) + any_specs(pieces) + hbm_specs(4),
        out_specs=vmem_specs(PARTS + 6),
        scratch_shapes=[semaphores],
        compiler_params=PARAMS,
        cost_estimate=cost(1_800_000_000),
    )(start, *early_all, *own)
    quarters = send_quads(quarters, 1)
    for s, piece in enumerate(late_ring):
        if s not in late_swaps:
            late_swaps[s] = swap_cores(after(piece, *quarters[1:]))
    late_all = late_ring + [late_swaps[s] for s in range(len(late_ring))]
    *pairs, late_sum = pl.pallas_call(
        partial(second_kernel, pieces, ends, factor),
        out_shape=[pair] * PARTS + [sums],
        in_specs=vmem_specs(2 * PARTS + 2) + any_specs(pieces) + hbm_specs(4),
        out_specs=vmem_specs(PARTS + 1),
        scratch_shapes=[pltpu.VMEM(s.shape, s.dtype) for s in [full_weights] + saved] + [semaphores],
        compiler_params=PARAMS,
        cost_estimate=cost(3_800_000_000),
    )(*quarters, *ending, column, row, *late_all, *own)
    pairs = send_quads(pairs, -1)
    late_sum = scatter(late_sum, "lat")
    input_grad, early_sum = pl.pallas_call(
        partial(third_kernel, ends, factor),
        out_shape=[stream, sums],
        in_specs=vmem_specs(PARTS + 7),
        out_specs=vmem_specs(2),
        compiler_params=PARAMS,
        cost_estimate=cost(2_000_000_000),
    )(*pairs, start, early_weights, middle, packed, probs, mixed, slope)

    layer_out = unquads(jnp.stack([p[0] for p in pairs]))
    total = jnp.stack([scatter(early_sum, "lat"), late_sum])
    lons = lax.axis_size("lon")
    total = total.astype(BF).reshape(2, lons, -1, 4 * head_width).swapaxes(0, 1)
    total = scatter(total, "lon").reshape(2, -1, 4 * head_width)
    pack_sum = total[:, :, : 3 * head_width].reshape(2, -1, 3, head_width)
    proj_sum = total[:, :, 3 * head_width :]
    return layer_out, unquads(input_grad.reshape(PARTS, -1, model_width)), pack_sum, proj_sum


def solution(mesh):
    in_specs = (
        P(None, "lat", "lon", None),
        P(None, "lat", "lon", None),
        P(None, None, None, "head"),
        P(None, None, "head"),
        P(None, None, "head"),
        P(None, None, "head"),
        P("lat", "lon"),
    )
    out_specs = (
        P(None, "lat", "lon", None),
        P(None, "lat", "lon", None),
        P(None, ("lat", "lon"), None, "head"),
        P(None, ("lat", "lon"), "head"),
    )
    return jax.shard_map(
        per_device, mesh=mesh, in_specs=in_specs, out_specs=out_specs, check_vma=False
    )
```

time: 1590 us -> 223 us (0.14)
  waiting for transfers between devices: 1480 us -> 43.9 us
  starting transfers between devices: 26.2 us -> 111 us
  Pallas kernels: 0 us -> 26.8 us
  other arithmetic: 26.1 us -> 1.67 us
  matrix products: 23.7 us -> 0 us
  local copies, waits for them, and re-layouts: 14.1 us -> 35.8 us
    unnamed x9 -> x0, waiting for transfers between devices: 1090 us -> none
    psum x7 -> x0, waiting for transfers between devices: 373 us -> none  [head_reduce(): lax.psum(partial_sum.astype(jnp.bfloat16), 'head').astype(jnp.float32)]
    ppermute x8 -> x29, starting transfers between devices: 25.7 us -> 93.3 us  [the longest x9 24.8 us: send_quads(): out.insert(1, lax.ppermute(pieces[q], ('lat', 'lon'), perm))]
    pallas_call x0 -> x4, Pallas kernels: none -> 26.8 us  [the longest x1 12.7 us: per_device(): pl.pallas_call(partial(second_kernel, pieces, ends, factor), out_shape=[p...]
    dot_general x30 -> x0, matrix products: 23.7 us -> none  [the longest x8 13.5 us: contract_last(): lax.dot_general(left, right, (((1,), (1,)), ((), ())), preferred_element_...]
    unnamed x79 -> x94, local copies, waits for them, and re-layouts: 9.01 us -> 30 us
    all_to_all x0 -> x3, starting transfers between devices: none -> 17.8 us  [scatter(): return jnp.sum(lax.all_to_all(parts, axis, 0, 0).astype(F32), axis=0)]
    reduce_sum x24 -> x3, other arithmetic: 16.5 us -> 0.17 us  [scatter(): return jnp.sum(lax.all_to_all(parts, axis, 0, 0).astype(F32), axis=0)]
  transfers between devices with their start and end apart: 16 -> 32, of which waited for: 16 -> 12; matrix products, arithmetic and copies ran while one was open for 1% -> 2% of each run, Pallas kernels for 0% -> 5%
where the time goes in v1:
time: 223 us; the launch traced here: 221 us
  starting transfers between devices  111 us (50%)
  waiting for transfers between devices  43.9 us (20%)
  local copies, waits for them, and re-layouts  35.8 us (16%)
  Pallas kernels  26.8 us (12%)
    unnamed x94, local copies, waits for them, and re-layouts  30 us
    ppermute x9, starting transfers between devices, send_quads(): out.insert(1, lax.ppermute(pieces[q], ('lat', 'lon'), perm))  24.8 us
    ppermute x8, starting transfers between devices, swap_cores(): return lax.ppermute(piece, 'lon', [(i, i ^ 1) for i in range(size)])  22.3 us
    all_to_all x3, starting transfers between devices, scatter(): return jnp.sum(lax.all_to_all(parts, axis, 0, 0).astype(F32), axis=0)  17.8 us
    ppermute x2, starting transfers between devices, fetch_heads(): one = lax.ppermute(shard, ('lat', 'head'), odd(1))  16.3 us
    all_to_all x3, waiting for transfers between devices, scatter(): return jnp.sum(lax.all_to_all(parts, axis, 0, 0).astype(F32), axis=0)  14.4 us
    pallas_call x1, Pallas kernels, per_device(): pl.pallas_call(partial(second_kernel, pieces, ends, factor), out_shape=[p...  12.7 us
    ppermute x4, starting transfers between devices, ring_x(): blocks[sign % ring] = lax.ppermute(sent, 'lat', pairs(sign))  11.6 us
  transfers between devices with their start and end apart: 32, of which 12 were waited for; matrix products, arithmetic and copies ran while one was open for 2% of the time, Pallas kernels for 5%

profile of v1, /device:TPU:1, one launch (start us, length us, event | category | flops | bytes accessed | tf_op | source)
XLA Modules:
  0.0 220.7 jit_solution(11240970370497889577)
XLA Ops:
  2.7 11.5 %collective-permute-start = (bf16[128,768]{1,0:T(8,128)(2,1)}, bf16[128,768]{1,0:T(8,128)(2,1)S(1)}, u32[]{:S(2)}, u32[]{:S(2)}) collective-permute-start(bf16[128,768]{1,0:T(8,128)(2,1)} %get-tuple-element.38), channel_id=1, source_target_pairs={{0,259},{1,256},{2,257},{3,258},{64,323},{65,320},{66,321},{67,322... | collective-permute-start | bytes 589832 | tf_op jit(solution)/shard_map/ppermute | solution.py:108
  16.4 3.7 %collective-permute-start.2 = (bf16[128,768]{1,0:T(8,128)(2,1)}, bf16[128,768]{1,0:T(8,128)(2,1)S(1)}, u32[]{:S(2)}, u32[]{:S(2)}) collective-permute-start(bf16[128,768]{1,0:T(8,128)(2,1)} %get-tuple-element.38), channel_id=1, source_target_pairs={{0,258},{1,259},{2,256},{3,257},{64,322},{65,323},{66,320},{67,321... | collective-permute-start | bytes 589832 | tf_op jit(solution)/shard_map/ppermute | solution.py:106
  23.9 3.1 %collective-permute-start.4 = (bf16[36,512]{1,0:T(8,128)(2,1)S(1)}, bf16[36,512]{1,0:T(8,128)(2,1)S(1)}, u32[]{:S(2)}, u32[]{:S(2)}) collective-permute-start(bf16[36,512]{1,0:T(8,128)(2,1)S(1)} %get-tuple-element.73), channel_id=1, source_target_pairs={{0,64},{4,68},{8,72},{12,76},{16,80},{20,84},{24,88},{28,92},{32,9... | collective-permute-start | bytes 110600 | tf_op jit(solution)/shard_map/ppermute | solution.py:82
  27.1 3.1 %collective-permute-start.5 = (bf16[36,512]{1,0:T(8,128)(2,1)S(1)}, bf16[36,512]{1,0:T(8,128)(2,1)S(1)}, u32[]{:S(2)}, u32[]{:S(2)}) collective-permute-start(bf16[36,512]{1,0:T(8,128)(2,1)S(1)} %get-tuple-element.72), channel_id=1, source_target_pairs={{0,68},{4,72},{8,76},{12,80},{16,84},{20,88},{24,92},{28,96},{32,1... | collective-permute-start | bytes 110600 | tf_op jit(solution)/shard_map/ppermute | solution.py:82
  34.8 2.8 %collective-permute-start.6 = (bf16[3,128,768]{2,1,0:T(8,128)(2,1)S(1)}, bf16[3,128,768]{2,1,0:T(8,128)(2,1)S(1)}, u32[]{:S(2)}, u32[]{:S(2)}) collective-permute-start(bf16[3,128,768]{2,1,0:T(8,128)(2,1)S(1)} %pad_maximum_fusion.refs_1_), channel_id=1, source_target_pairs={{0,4},{4,0},{8,12},{12,8},{16,20},{20,16},{24,28},{28,24},{32,36},... | collective-permute-start | bytes 1769480 | tf_op jit(solution)/shard_map/ppermute | solution.py:114
  39.5 4.6 %collective-permute-start.12 = (bf16[3,128,768]{2,1,0:T(8,128)(2,1)S(1)}, bf16[3,128,768]{2,1,0:T(8,128)(2,1)S(1)}, u32[]{:S(2)}, u32[]{:S(2)}) collective-permute-start(bf16[3,128,768]{2,1,0:T(8,128)(2,1)S(1)} %pad_maximum_fusion.refs_1_), channel_id=1, source_target_pairs={{0,192},{64,0},{128,64},{192,128},{256,448},{320,256},{384,320},{4... | collective-permute-start | bytes 1769480 | tf_op jit(solution)/shard_map/ppermute | solution.py:128
  44.1 4.9 %collective-permute-start.7 = (bf16[128,768]{1,0:T(8,128)(2,1)}, bf16[128,768]{1,0:T(8,128)(2,1)S(1)}, u32[]{:S(2)}, u32[]{:S(2)}) collective-permute-start(bf16[128,768]{1,0:T(8,128)(2,1)} %get-tuple-element.43), channel_id=1, source_target_pairs={{0,259},{1,256},{2,257},{3,258},{64,323},{65,320},{66,321},{67,322... | collective-permute-start | bytes 589832 | tf_op jit(solution)/shard_map/ppermute | solution.py:108
  49.0 3.2 %collective-permute-start.8 = (bf16[128,768]{1,0:T(8,128)(2,1)}, bf16[128,768]{1,0:T(8,128)(2,1)S(1)}, u32[]{:S(2)}, u32[]{:S(2)}) collective-permute-start(bf16[128,768]{1,0:T(8,128)(2,1)} %get-tuple-element.43), channel_id=1, source_target_pairs={{0,3},{1,0},{2,1},{3,2},{64,67},{65,64},{66,65},{67,66},{128,131},... | collective-permute-start | bytes 589832 | tf_op jit(solution)/shard_map/ppermute | solution.py:107
  52.2 2.7 %collective-permute-start.9 = (bf16[128,768]{1,0:T(8,128)(2,1)}, bf16[128,768]{1,0:T(8,128)(2,1)S(1)}, u32[]{:S(2)}, u32[]{:S(2)}) collective-permute-start(bf16[128,768]{1,0:T(8,128)(2,1)} %get-tuple-element.43), channel_id=1, source_target_pairs={{0,258},{1,259},{2,256},{3,257},{64,322},{65,323},{66,320},{67,321... | collective-permute-start | bytes 589832 | tf_op jit(solution)/shard_map/ppermute | solution.py:106
  54.9 2.6 %collective-permute-done.8 = bf16[128,768]{1,0:T(8,128)(2,1)S(1)} collective-permute-done((bf16[128,768]{1,0:T(8,128)(2,1)}, bf16[128,768]{1,0:T(8,128)(2,1)S(1)}, u32[]{:S(2)}, u32[]{:S(2)}) %collective-permute-start.8) | collective-permute-done | bytes 196640 | tf_op jit(solution)/shard_map/ppermute | solution.py:107
  57.5 9.3 %collective-permute-done.9 = bf16[128,768]{1,0:T(8,128)(2,1)S(1)} collective-permute-done((bf16[128,768]{1,0:T(8,128)(2,1)}, bf16[128,768]{1,0:T(8,128)(2,1)S(1)}, u32[]{:S(2)}, u32[]{:S(2)}) %collective-permute-start.9) | collective-permute-done | bytes 196640 | tf_op jit(solution)/shard_map/ppermute | solution.py:106
  66.9 3.2 %collective-permute-start.13 = (bf16[3,128,768]{2,1,0:T(8,128)(2,1)S(1)}, bf16[3,128,768]{2,1,0:T(8,128)(2,1)S(1)}, u32[]{:S(2)}, u32[]{:S(2)}) collective-permute-start(bf16[3,128,768]{2,1,0:T(8,128)(2,1)S(1)} %pad_maximum_fusion.1.refs_10_), channel_id=1, source_target_pairs={{0,192},{64,0},{128,64},{192,128},{256,448},{320,256},{384,320},{4... | collective-permute-start | bytes 1769480 | tf_op jit(solution)/shard_map/ppermute | solution.py:128
  72.2 4.1 %collective-permute-start.10 = (bf16[3,128,768]{2,1,0:T(8,128)(2,1)S(1)}, bf16[3,128,768]{2,1,0:T(8,128)(2,1)S(1)}, u32[]{:S(2)}, u32[]{:S(2)}) collective-permute-start(bf16[3,128,768]{2,1,0:T(8,128)(2,1)S(1)} %pad_maximum_fusion.1.refs_10_), channel_id=1, source_target_pairs={{0,4},{4,0},{8,12},{12,8},{16,20},{20,16},{24,28},{28,24},{32,36},... | collective-permute-start | bytes 1769480 | tf_op jit(solution)/shard_map/ppermute | solution.py:114
  76.4 6.3 %collective-permute-done.13.refs_13_ = bf16[3,128,768]{2,1,0:T(8,128)(2,1)S(1)} collective-permute-done((bf16[3,128,768]{2,1,0:T(8,128)(2,1)S(1)}, bf16[3,128,768]{2,1,0:T(8,128)(2,1)S(1)}, u32[]{:S(2)}, u32[]{:S(2)}) %collective-permute-start.13) | collective-permute-done | bytes 589856 | tf_op jit(solution)/shard_map/ppermute | solution.py:128
  82.7 3.8 %collective-permute-start.14 = (bf16[3,128,768]{2,1,0:T(8,128)(2,1)S(1)}, bf16[3,128,768]{2,1,0:T(8,128)(2,1)S(1)}, u32[]{:S(2)}, u32[]{:S(2)}) collective-permute-start(bf16[3,128,768]{2,1,0:T(8,128)(2,1)S(1)} %collective-permute-done.13.refs_13_), channel_id=1, source_target_pairs={{0,4},{4,0},{8,12},{12,8},{16,20},{20,16},{24,28},{28,24},{32,36},... | collective-permute-start | bytes 1769480 | tf_op jit(solution)/shard_map/ppermute | solution.py:114
  88.4 2.4 %collective-permute-start.18 = (bf16[3,128,768]{2,1,0:T(8,128)(2,1)S(1)}, bf16[3,128,768]{2,1,0:T(8,128)(2,1)S(1)}, u32[]{:S(2)}, u32[]{:S(2)}) collective-permute-start(bf16[3,128,768]{2,1,0:T(8,128)(2,1)S(1)} %collective-permute-done.12.refs_4_), channel_id=1, source_target_pairs={{0,4},{4,0},{8,12},{12,8},{16,20},{20,16},{24,28},{28,24},{32,36},... | collective-permute-start | bytes 1769480 | tf_op jit(solution)/shard_map/ppermute | solution.py:114
  93.6 4.4 %collective-permute-start.23 = (bf16[3,128,768]{2,1,0:T(8,128)(2,1)S(1)}, bf16[3,128,768]{2,1,0:T(8,128)(2,1)}, u32[]{:S(2)}, u32[]{:S(2)}) collective-permute-start(bf16[3,128,768]{2,1,0:T(8,128)(2,1)S(1)} %collective-permute-done.13.refs_13_), channel_id=1, source_target_pairs={{0,192},{64,0},{128,64},{192,128},{256,448},{320,256},{384,320},{4... | collective-permute-start | bytes 1769480 | tf_op jit(solution)/shard_map/ppermute | solution.py:130
  100.9 5.5 %shard_map.103 = (bf16[36,512]{1,0:T(8,128)(2,1)S(1)}, bf16[36,512]{1,0:T(8,128)(2,1)S(1)}, bf16[36,512]{1,0:T(8,128)(2,1)S(1)}, bf16[36,512]{1,0:T(8,128)(2,1)S...) custom-call(bf16[144,512]{1,0:T(8,128)(2,1)S(1)} %reshape_reshape.6., ...), custom_call_target="tpu_custom_call" | custom-call | flops 1800000000 | bytes 8000000 | tf_op jit(solution)/shard_map/pallas_call | solution.py:406
  106.4 2.6 %copy-done = bf16[4,512,1536]{2,1,0:T(8,128)(2,1)} copy-done((bf16[4,512,1536]{2,1,0:T(8,128)(2,1)}, bf16[4,512,1536]{2,1,0:T(8,128)(2,1)S(1)}, u32[]{:S(2)}) %copy-start) | copy-done | bytes 6291480
  116.1 2.8 %collective-permute-start.21 = (bf16[36,512]{1,0:T(8,128)(2,1)S(1)}, bf16[36,512]{1,0:T(8,128)(2,1)S(1)}, u32[]{:S(2)}, u32[]{:S(2)}) collective-permute-start(bf16[36,512]{1,0:T(8,128)(2,1)S(1)} %get-tuple-element.49), channel_id=1, source_target_pairs={{0,68},{4,72},{8,76},{12,80},{16,84},{20,88},{24,92},{28,96},{32,1... | collective-permute-start | bytes 110600 | tf_op jit(solution)/shard_map/ppermute | solution.py:82
  124.4 3.2 %collective-permute-start.25 = (bf16[3,128,768]{2,1,0:T(8,128)(2,1)}, bf16[3,128,768]{2,1,0:T(8,128)(2,1)}, u32[]{:S(2)}, u32[]{:S(2)}) collective-permute-start(bf16[3,128,768]{2,1,0:T(8,128)(2,1)} %collective-permute-done.23.refs_12_), channel_id=1, source_target_pairs={{0,4},{4,0},{8,12},{12,8},{16,20},{20,16},{24,28},{28,24},{32,36},... | collective-permute-start | bytes 1769480 | tf_op jit(solution)/shard_map/ppermute | solution.py:114
  143.2 12.7 %shard_map.104 = (bf16[2,36,512]{2,1,0:T(8,128)(2,1)S(1)}, bf16[2,36,512]{2,1,0:T(8,128)(2,1)S(1)}, bf16[2,36,512]{2,1,0:T(8,128)(2,1)S(1)}, bf16[2,36,512]{2,1,0:T(8,128)(2,1)S(1)}, bf16[512,512]{1,0:T(8,128)(2,1)S(1)}) custom-call(bf16[36,512]{1,0:T(8,128)(2,1)S(1)} %copy-done.35, bf16[36,512]{1,0:T(8,128)(2,1)S(1)} %copy-done.37, ...), custom_call_target="tpu_custom_call" | custom-call | flops 3800000000 | bytes 8000000 | tf_op jit(solution)/shard_map/pallas_call | solution.py:420
  158.7 3.6 %all-to-all-start.1 = ((bf16[8,64,512]{2,1,0:T(8,128)(2,1)}), bf16[8,64,512]{2,1,0:T(8,128)(2,1)S(1)}, u32[]{:S(2)}, u32[]{:S(2)}) async-start(bf16[8,64,512]{2,1,0:T(8,128)(2,1)} %bitcast.49), calls=%async_computation.1 | async-start | bytes 1048576 | tf_op jit(solution)/shard_map/all_to_all | solution.py:358
  162.5 5.7 %collective-permute-start.27 = (bf16[2,36,512]{2,1,0:T(8,128)(2,1)}, bf16[2,36,512]{2,1,0:T(8,128)(2,1)S(1)}, u32[]{:S(2)}, u32[]{:S(2)}) collective-permute-start(bf16[2,36,512]{2,1,0:T(8,128)(2,1)} %copy-done.26), channel_id=1, source_target_pairs={{0,448},{4,452},{8,456},{12,460},{16,464},{20,468},{24,472},{28,47... | collective-permute-start | bytes 221192 | tf_op jit(solution)/shard_map/ppermute | solution.py:82
  168.2 4.1 %collective-permute-start.28 = (bf16[2,36,512]{2,1,0:T(8,128)(2,1)}, bf16[2,36,512]{2,1,0:T(8,128)(2,1)S(1)}, u32[]{:S(2)}, u32[]{:S(2)}) collective-permute-start(bf16[2,36,512]{2,1,0:T(8,128)(2,1)} %copy-done.25), channel_id=1, source_target_pairs={{0,508},{4,448},{8,452},{12,456},{16,460},{20,464},{24,468},{28,47... | collective-permute-start | bytes 221192 | tf_op jit(solution)/shard_map/ppermute | solution.py:82
  172.3 2.9 %collective-permute-done.28.refs_3_ = bf16[2,36,512]{2,1,0:T(8,128)(2,1)S(1)} collective-permute-done((bf16[2,36,512]{2,1,0:T(8,128)(2,1)}, bf16[2,36,512]{2,1,0:T(8,128)(2,1)S(1)}, u32[]{:S(2)}, u32[]{:S(2)}) %collective-permute-start.28) | collective-permute-done | bytes 73760 | tf_op jit(solution)/shard_map/ppermute | solution.py:82
  175.2 2.8 %copy-done.1 = bf16[4,512,1536]{2,1,0:T(8,128)(2,1)S(1)} copy-done((bf16[4,512,1536]{2,1,0:T(8,128)(2,1)S(1)}, bf16[4,512,1536]{2,1,0:T(8,128)(2,1)}, u32[]{:S(2)}) %copy-start.1) | copy-done | bytes 6291480
  181.3 6.7 %shard_map.105 = (bf16[144,512]{1,0:T(8,128)(2,1)S(1)}, bf16[512,512]{1,0:T(8,128)(2,1)}) custom-call(bf16[2,36,512]{2,1,0:T(8,128)(2,1)S(1)} %get-tuple-element.59.refs_0_, bf16[2,36,512]{2,1,0:T(8,128)(2,1)S(1)} %collective-permute-done.26.refs_1_, bf16[2,36,512]{2,1,0:T(8,128)(2,1)S(1)} %collective-permute-done.27.refs_2_, ...), custom_call_target="tpu_custom_call" | custom-call | flops 2000000000 | bytes 8000000 | tf_op jit(solution)/shard_map/pallas_call | solution.py:431
  187.9 4.0 %all-to-all-start = ((bf16[8,64,512]{2,1,0:T(8,128)(2,1)}), bf16[8,64,512]{2,1,0:T(8,128)(2,1)S(1)}, u32[]{:S(2)}, u32[]{:S(2)}) async-start(bf16[8,64,512]{2,1,0:T(8,128)(2,1)} %bitcast.20), calls=%async_computation | async-start | bytes 1048576 | tf_op jit(solution)/shard_map/all_to_all | solution.py:358
  192.0 7.1 %all-to-all-done = bf16[8,64,512]{2,1,0:T(8,128)(2,1)S(1)} async-done(((bf16[8,64,512]{2,1,0:T(8,128)(2,1)}), bf16[8,64,512]{2,1,0:T(8,128)(2,1)S(1)}, u32[]{:S(2)}, u32[]{:S(2)}) %all-to-all-start) | async-done | bytes 524320 | tf_op jit(solution)/shard_map/all_to_all | solution.py:358
  200.1 10.2 %all-to-all-start.2 = ((bf16[16,8,512]{2,1,0:T(8,128)(2,1)}), bf16[16,8,512]{2,1,0:T(8,128)(2,1)S(1)}, u32[]{:S(2)}, u32[]{:S(2)}) async-start(bf16[16,8,512]{2,1,0:T(8,128)(2,1)} %copy.49), calls=%async_computation.2 | async-start | bytes 262144 | tf_op jit(solution)/shard_map/all_to_all | solution.py:358
  212.1 7.3 %all-to-all-done.2 = bf16[16,8,512]{2,1,0:T(8,128)(2,1)S(1)} async-done(((bf16[16,8,512]{2,1,0:T(8,128)(2,1)}), bf16[16,8,512]{2,1,0:T(8,128)(2,1)S(1)}, u32[]{:S(2)}, u32[]{:S(2)}) %all-to-all-start.2) | async-done | bytes 131104 | tf_op jit(solution)/shard_map/all_to_all | solution.py:358
  (169 shorter events, 62.6 us)
Async XLA Ops:
  2.7 18.2 %collective-permute-start = (bf16[128,768]{1,0:T(8,128)(2,1)}, bf16[128,768]{1,0:T(8,128)(2,1)S(1)}, u32[]{:S(2)}, u32[]{:S(2)}) collective-permute-start(bf16[128,768]{1,0:T(8,128)(2,1)} %get-tuple-element.38), channel_id=1, source_target_pairs={{0,259},{1,256},{2,257},{3,258},{64,323},{65,320},{66,321},{67,322... | collective-permute-start | bytes 589832 | tf_op jit(solution)/shard_map/ppermute | solution.py:108
  14.2 16.0 %collective-permute-start.1 = (bf16[128,768]{1,0:T(8,128)(2,1)}, bf16[128,768]{1,0:T(8,128)(2,1)S(1)}, u32[]{:S(2)}, u32[]{:S(2)}) collective-permute-start(bf16[128,768]{1,0:T(8,128)(2,1)} %get-tuple-element.38), channel_id=1, source_target_pairs={{0,3},{1,0},{2,1},{3,2},{64,67},{65,64},{66,65},{67,66},{128,131},... | collective-permute-start | bytes 589832 | tf_op jit(solution)/shard_map/ppermute | solution.py:107
  16.4 13.9 %collective-permute-start.2 = (bf16[128,768]{1,0:T(8,128)(2,1)}, bf16[128,768]{1,0:T(8,128)(2,1)S(1)}, u32[]{:S(2)}, u32[]{:S(2)}) collective-permute-start(bf16[128,768]{1,0:T(8,128)(2,1)} %get-tuple-element.38), channel_id=1, source_target_pairs={{0,258},{1,259},{2,256},{3,257},{64,322},{65,323},{66,320},{67,321... | collective-permute-start | bytes 589832 | tf_op jit(solution)/shard_map/ppermute | solution.py:106
  21.6 10.6 %collective-permute-start.3 = (bf16[36,512]{1,0:T(8,128)(2,1)S(1)}, bf16[36,512]{1,0:T(8,128)(2,1)S(1)}, u32[]{:S(2)}, u32[]{:S(2)}) collective-permute-start(bf16[36,512]{1,0:T(8,128)(2,1)S(1)} %get-tuple-element.74), channel_id=1, source_target_pairs={{0,4},{4,8},{8,12},{12,16},{16,20},{20,24},{24,28},{28,32},{32,36}... | collective-permute-start | bytes 110600 | tf_op jit(solution)/shard_map/ppermute | solution.py:82
  23.9 8.9 %collective-permute-start.4 = (bf16[36,512]{1,0:T(8,128)(2,1)S(1)}, bf16[36,512]{1,0:T(8,128)(2,1)S(1)}, u32[]{:S(2)}, u32[]{:S(2)}) collective-permute-start(bf16[36,512]{1,0:T(8,128)(2,1)S(1)} %get-tuple-element.73), channel_id=1, source_target_pairs={{0,64},{4,68},{8,72},{12,76},{16,80},{20,84},{24,88},{28,92},{32,9... | collective-permute-start | bytes 110600 | tf_op jit(solution)/shard_map/ppermute | solution.py:82
  27.1 7.7 %collective-permute-start.5 = (bf16[36,512]{1,0:T(8,128)(2,1)S(1)}, bf16[36,512]{1,0:T(8,128)(2,1)S(1)}, u32[]{:S(2)}, u32[]{:S(2)}) collective-permute-start(bf16[36,512]{1,0:T(8,128)(2,1)S(1)} %get-tuple-element.72), channel_id=1, source_target_pairs={{0,68},{4,72},{8,76},{12,80},{16,84},{20,88},{24,92},{28,96},{32,1... | collective-permute-start | bytes 110600 | tf_op jit(solution)/shard_map/ppermute | solution.py:82
  34.8 9.3 %collective-permute-start.6 = (bf16[3,128,768]{2,1,0:T(8,128)(2,1)S(1)}, bf16[3,128,768]{2,1,0:T(8,128)(2,1)S(1)}, u32[]{:S(2)}, u32[]{:S(2)}) collective-permute-start(bf16[3,128,768]{2,1,0:T(8,128)(2,1)S(1)} %pad_maximum_fusion.refs_1_), channel_id=1, source_target_pairs={{0,4},{4,0},{8,12},{12,8},{16,20},{20,16},{24,28},{28,24},{32,36},... | collective-permute-start | bytes 1769480 | tf_op jit(solution)/shard_map/ppermute | solution.py:114
  37.6 29.3 %collective-permute-start.11 = (bf16[3,128,768]{2,1,0:T(8,128)(2,1)S(1)}, bf16[3,128,768]{2,1,0:T(8,128)(2,1)S(1)}, u32[]{:S(2)}, u32[]{:S(2)}) collective-permute-start(bf16[3,128,768]{2,1,0:T(8,128)(2,1)S(1)} %pad_maximum_fusion.refs_1_), channel_id=1, source_target_pairs={{0,64},{64,128},{128,192},{192,0},{256,320},{320,384},{384,448},{4... | collective-permute-start | bytes 1769480 | tf_op jit(solution)/shard_map/ppermute | solution.py:128
  39.5 27.4 %collective-permute-start.12 = (bf16[3,128,768]{2,1,0:T(8,128)(2,1)S(1)}, bf16[3,128,768]{2,1,0:T(8,128)(2,1)S(1)}, u32[]{:S(2)}, u32[]{:S(2)}) collective-permute-start(bf16[3,128,768]{2,1,0:T(8,128)(2,1)S(1)} %pad_maximum_fusion.refs_1_), channel_id=1, source_target_pairs={{0,192},{64,0},{128,64},{192,128},{256,448},{320,256},{384,320},{4... | collective-permute-start | bytes 1769480 | tf_op jit(solution)/shard_map/ppermute | solution.py:128
  44.1 10.8 %collective-permute-start.7 = (bf16[128,768]{1,0:T(8,128)(2,1)}, bf16[128,768]{1,0:T(8,128)(2,1)S(1)}, u32[]{:S(2)}, u32[]{:S(2)}) collective-permute-start(bf16[128,768]{1,0:T(8,128)(2,1)} %get-tuple-element.43), channel_id=1, source_target_pairs={{0,259},{1,256},{2,257},{3,258},{64,323},{65,320},{66,321},{67,322... | collective-permute-start | bytes 589832 | tf_op jit(solution)/shard_map/ppermute | solution.py:108
  49.0 8.6 %collective-permute-start.8 = (bf16[128,768]{1,0:T(8,128)(2,1)}, bf16[128,768]{1,0:T(8,128)(2,1)S(1)}, u32[]{:S(2)}, u32[]{:S(2)}) collective-permute-start(bf16[128,768]{1,0:T(8,128)(2,1)} %get-tuple-element.43), channel_id=1, source_target_pairs={{0,3},{1,0},{2,1},{3,2},{64,67},{65,64},{66,65},{67,66},{128,131},... | collective-permute-start | bytes 589832 | tf_op jit(solution)/shard_map/ppermute | solution.py:107
  52.2 14.6 %collective-permute-start.9 = (bf16[128,768]{1,0:T(8,128)(2,1)}, bf16[128,768]{1,0:T(8,128)(2,1)S(1)}, u32[]{:S(2)}, u32[]{:S(2)}) collective-permute-start(bf16[128,768]{1,0:T(8,128)(2,1)} %get-tuple-element.43), channel_id=1, source_target_pairs={{0,258},{1,259},{2,256},{3,257},{64,322},{65,323},{66,320},{67,321... | collective-permute-start | bytes 589832 | tf_op jit(solution)/shard_map/ppermute | solution.py:106
  66.9 15.7 %collective-permute-start.13 = (bf16[3,128,768]{2,1,0:T(8,128)(2,1)S(1)}, bf16[3,128,768]{2,1,0:T(8,128)(2,1)S(1)}, u32[]{:S(2)}, u32[]{:S(2)}) collective-permute-start(bf16[3,128,768]{2,1,0:T(8,128)(2,1)S(1)} %pad_maximum_fusion.1.refs_10_), channel_id=1, source_target_pairs={{0,192},{64,0},{128,64},{192,128},{256,448},{320,256},{384,320},{4... | collective-permute-start | bytes 1769480 | tf_op jit(solution)/shard_map/ppermute | solution.py:128
  70.1 20.7 %collective-permute-start.15 = (bf16[3,128,768]{2,1,0:T(8,128)(2,1)S(1)}, bf16[3,128,768]{2,1,0:T(8,128)(2,1)S(1)}, u32[]{:S(2)}, u32[]{:S(2)}) collective-permute-start(bf16[3,128,768]{2,1,0:T(8,128)(2,1)S(1)} %collective-permute-done.11.refs_2_), channel_id=1, source_target_pairs={{0,64},{64,128},{128,192},{192,0},{256,320},{320,384},{384,448},{4... | collective-permute-start | bytes 1769480 | tf_op jit(solution)/shard_map/ppermute | solution.py:130
  72.2 20.5 %collective-permute-start.10 = (bf16[3,128,768]{2,1,0:T(8,128)(2,1)S(1)}, bf16[3,128,768]{2,1,0:T(8,128)(2,1)S(1)}, u32[]{:S(2)}, u32[]{:S(2)}) collective-permute-start(bf16[3,128,768]{2,1,0:T(8,128)(2,1)S(1)} %pad_maximum_fusion.1.refs_10_), channel_id=1, source_target_pairs={{0,4},{4,0},{8,12},{12,8},{16,20},{20,16},{24,28},{28,24},{32,36},... | collective-permute-start | bytes 1769480 | tf_op jit(solution)/shard_map/ppermute | solution.py:114
  82.7 15.3 %collective-permute-start.14 = (bf16[3,128,768]{2,1,0:T(8,128)(2,1)S(1)}, bf16[3,128,768]{2,1,0:T(8,128)(2,1)S(1)}, u32[]{:S(2)}, u32[]{:S(2)}) collective-permute-start(bf16[3,128,768]{2,1,0:T(8,128)(2,1)S(1)} %collective-permute-done.13.refs_13_), channel_id=1, source_target_pairs={{0,4},{4,0},{8,12},{12,8},{16,20},{20,16},{24,28},{28,24},{32,36},... | collective-permute-start | bytes 1769480 | tf_op jit(solution)/shard_map/ppermute | solution.py:114
  86.5 14.3 %collective-permute-start.16 = (bf16[3,128,768]{2,1,0:T(8,128)(2,1)S(1)}, bf16[3,128,768]{2,1,0:T(8,128)(2,1)S(1)}, u32[]{:S(2)}, u32[]{:S(2)}) collective-permute-start(bf16[3,128,768]{2,1,0:T(8,128)(2,1)S(1)} %collective-permute-done.11.refs_2_), channel_id=1, source_target_pairs={{0,4},{4,0},{8,12},{12,8},{16,20},{20,16},{24,28},{28,24},{32,36},... | collective-permute-start | bytes 1769480 | tf_op jit(solution)/shard_map/ppermute | solution.py:114
  88.4 12.4 %collective-permute-start.18 = (bf16[3,128,768]{2,1,0:T(8,128)(2,1)S(1)}, bf16[3,128,768]{2,1,0:T(8,128)(2,1)S(1)}, u32[]{:S(2)}, u32[]{:S(2)}) collective-permute-start(bf16[3,128,768]{2,1,0:T(8,128)(2,1)S(1)} %collective-permute-done.12.refs_4_), channel_id=1, source_target_pairs={{0,4},{4,0},{8,12},{12,8},{16,20},{20,16},{24,28},{28,24},{32,36},... | collective-permute-start | bytes 1769480 | tf_op jit(solution)/shard_map/ppermute | solution.py:114
  90.8 10.0 %collective-permute-start.17 = (bf16[3,128,768]{2,1,0:T(8,128)(2,1)S(1)}, bf16[3,128,768]{2,1,0:T(8,128)(2,1)S(1)}, u32[]{:S(2)}, u32[]{:S(2)}) collective-permute-start(bf16[3,128,768]{2,1,0:T(8,128)(2,1)S(1)} %collective-permute-done.15.refs_3_), channel_id=1, source_target_pairs={{0,4},{4,0},{8,12},{12,8},{16,20},{20,16},{24,28},{28,24},{32,36},... | collective-permute-start | bytes 1769480 | tf_op jit(solution)/shard_map/ppermute | solution.py:114
  93.6 25.3 %collective-permute-start.23 = (bf16[3,128,768]{2,1,0:T(8,128)(2,1)S(1)}, bf16[3,128,768]{2,1,0:T(8,128)(2,1)}, u32[]{:S(2)}, u32[]{:S(2)}) collective-permute-start(bf16[3,128,768]{2,1,0:T(8,128)(2,1)S(1)} %collective-permute-done.13.refs_13_), channel_id=1, source_target_pairs={{0,192},{64,0},{128,64},{192,128},{256,448},{320,256},{384,320},{4... | collective-permute-start | bytes 1769480 | tf_op jit(solution)/shard_map/ppermute | solution.py:130
  98.9 28.8 %collective-permute-start.22 = (bf16[3,128,768]{2,1,0:T(8,128)(2,1)S(1)}, bf16[3,128,768]{2,1,0:T(8,128)(2,1)}, u32[]{:S(2)}, u32[]{:S(2)}) collective-permute-start(bf16[3,128,768]{2,1,0:T(8,128)(2,1)S(1)} %pad_maximum_fusion.1.refs_10_), channel_id=1, source_target_pairs={{0,64},{64,128},{128,192},{192,0},{256,320},{320,384},{384,448},{4... | collective-permute-start | bytes 1769480 | tf_op jit(solution)/shard_map/ppermute | solution.py:128
  112.6 6.3 %collective-permute-start.19 = (bf16[36,512]{1,0:T(8,128)(2,1)S(1)}, bf16[36,512]{1,0:T(8,128)(2,1)S(1)}, u32[]{:S(2)}, u32[]{:S(2)}) collective-permute-start(bf16[36,512]{1,0:T(8,128)(2,1)S(1)} %get-tuple-element.47), channel_id=1, source_target_pairs={{0,4},{4,8},{8,12},{12,16},{16,20},{20,24},{24,28},{28,32},{32,36}... | collective-permute-start | bytes 110600 | tf_op jit(solution)/shard_map/ppermute | solution.py:82
  114.2 6.9 %collective-permute-start.20 = (bf16[36,512]{1,0:T(8,128)(2,1)S(1)}, bf16[36,512]{1,0:T(8,128)(2,1)S(1)}, u32[]{:S(2)}, u32[]{:S(2)}) collective-permute-start(bf16[36,512]{1,0:T(8,128)(2,1)S(1)} %get-tuple-element.48), channel_id=1, source_target_pairs={{0,64},{4,68},{8,72},{12,76},{16,80},{20,84},{24,88},{28,92},{32,9... | collective-permute-start | bytes 110600 | tf_op jit(solution)/shard_map/ppermute | solution.py:82
  116.1 7.7 %collective-permute-start.21 = (bf16[36,512]{1,0:T(8,128)(2,1)S(1)}, bf16[36,512]{1,0:T(8,128)(2,1)S(1)}, u32[]{:S(2)}, u32[]{:S(2)}) collective-permute-start(bf16[36,512]{1,0:T(8,128)(2,1)S(1)} %get-tuple-element.49), channel_id=1, source_target_pairs={{0,68},{4,72},{8,76},{12,80},{16,84},{20,88},{24,92},{28,96},{32,1... | collective-permute-start | bytes 110600 | tf_op jit(solution)/shard_map/ppermute | solution.py:82
  124.4 6.0 %collective-permute-start.25 = (bf16[3,128,768]{2,1,0:T(8,128)(2,1)}, bf16[3,128,768]{2,1,0:T(8,128)(2,1)}, u32[]{:S(2)}, u32[]{:S(2)}) collective-permute-start(bf16[3,128,768]{2,1,0:T(8,128)(2,1)} %collective-permute-done.23.refs_12_), channel_id=1, source_target_pairs={{0,4},{4,0},{8,12},{12,8},{16,20},{20,16},{24,28},{28,24},{32,36},... | collective-permute-start | bytes 1769480 | tf_op jit(solution)/shard_map/ppermute | solution.py:114
  127.6 4.2 %collective-permute-start.24 = (bf16[3,128,768]{2,1,0:T(8,128)(2,1)}, bf16[3,128,768]{2,1,0:T(8,128)(2,1)}, u32[]{:S(2)}, u32[]{:S(2)}) collective-permute-start(bf16[3,128,768]{2,1,0:T(8,128)(2,1)} %collective-permute-done.22.refs_11_), channel_id=1, source_target_pairs={{0,4},{4,0},{8,12},{12,8},{16,20},{20,16},{24,28},{28,24},{32,36},... | collective-permute-start | bytes 1769480 | tf_op jit(solution)/shard_map/ppermute | solution.py:114
  158.7 29.3 %all-to-all-start.1 = ((bf16[8,64,512]{2,1,0:T(8,128)(2,1)}), bf16[8,64,512]{2,1,0:T(8,128)(2,1)S(1)}, u32[]{:S(2)}, u32[]{:S(2)}) async-start(bf16[8,64,512]{2,1,0:T(8,128)(2,1)} %bitcast.49), calls=%async_computation.1 | async-start | bytes 1048576 | tf_op jit(solution)/shard_map/all_to_all | solution.py:358
  162.3 10.0 %collective-permute-start.26 = (bf16[2,36,512]{2,1,0:T(8,128)(2,1)}, bf16[2,36,512]{2,1,0:T(8,128)(2,1)S(1)}, u32[]{:S(2)}, u32[]{:S(2)}) collective-permute-start(bf16[2,36,512]{2,1,0:T(8,128)(2,1)} %copy-done.27), channel_id=1, source_target_pairs={{0,60},{4,0},{8,4},{12,8},{16,12},{20,16},{24,20},{28,24},{32,28},... | collective-permute-start | bytes 221192 | tf_op jit(solution)/shard_map/ppermute | solution.py:82
  162.5 9.8 %collective-permute-start.27 = (bf16[2,36,512]{2,1,0:T(8,128)(2,1)}, bf16[2,36,512]{2,1,0:T(8,128)(2,1)S(1)}, u32[]{:S(2)}, u32[]{:S(2)}) collective-permute-start(bf16[2,36,512]{2,1,0:T(8,128)(2,1)} %copy-done.26), channel_id=1, source_target_pairs={{0,448},{4,452},{8,456},{12,460},{16,464},{20,468},{24,472},{28,47... | collective-permute-start | bytes 221192 | tf_op jit(solution)/shard_map/ppermute | solution.py:82
  168.2 7.0 %collective-permute-start.28 = (bf16[2,36,512]{2,1,0:T(8,128)(2,1)}, bf16[2,36,512]{2,1,0:T(8,128)(2,1)S(1)}, u32[]{:S(2)}, u32[]{:S(2)}) collective-permute-start(bf16[2,36,512]{2,1,0:T(8,128)(2,1)} %copy-done.25), channel_id=1, source_target_pairs={{0,508},{4,448},{8,452},{12,456},{16,460},{20,464},{24,468},{28,47... | collective-permute-start | bytes 221192 | tf_op jit(solution)/shard_map/ppermute | solution.py:82
  187.9 11.2 %all-to-all-start = ((bf16[8,64,512]{2,1,0:T(8,128)(2,1)}), bf16[8,64,512]{2,1,0:T(8,128)(2,1)S(1)}, u32[]{:S(2)}, u32[]{:S(2)}) async-start(bf16[8,64,512]{2,1,0:T(8,128)(2,1)} %bitcast.20), calls=%async_computation | async-start | bytes 1048576 | tf_op jit(solution)/shard_map/all_to_all | solution.py:358
  200.1 19.4 %all-to-all-start.2 = ((bf16[16,8,512]{2,1,0:T(8,128)(2,1)}), bf16[16,8,512]{2,1,0:T(8,128)(2,1)S(1)}, u32[]{:S(2)}, u32[]{:S(2)}) async-start(bf16[16,8,512]{2,1,0:T(8,128)(2,1)} %copy.49), calls=%async_computation.2 | async-start | bytes 262144 | tf_op jit(solution)/shard_map/all_to_all | solution.py:358
  (47 other events, 710.1 us)

commit v2 on v1

--- a/solution.py
+++ b/solution.py
@@ -132,8 +132,8 @@
 
 
 def shard_kernel(ring, qkv_ref, proj_ref, up_ref, down_ref, *refs):
-    out_refs, sem = refs[:-1], refs[-1]
-    rows, half = out_refs[0].shape
+    out_ref, sem = refs
+    rows, half = out_ref.shape[1:]
     side = lax.axis_index("lon") % 2
     start = pl.multiple_of(lax.axis_index("lat") % ring * rows, rows)
     width, hidden = proj_ref.shape[2], up_ref.shape[2]
@@ -141,10 +141,10 @@
 
     def run(views):
         copies = []
-        for layer, out_ref in enumerate(out_refs):
+        for layer in range(2):
             at = 0
             for view in views(layer):
-                target = out_ref.at[:, pl.ds(at, view.shape[1])]
+                target = out_ref.at[layer, :, pl.ds(at, view.shape[1])]
                 copies.append(pltpu.make_async_copy(view, target, sem.at[len(copies)]))
                 at += view.shape[1]
         for copy in copies:
@@ -172,15 +172,39 @@
 def weight_shards(own):
     ring = lat_parts()[1]
     columns = 4 * own[1].shape[2] + 2 * own[2].shape[2]
-    shard = jax.ShapeDtypeStruct((own[1].shape[1] // ring, columns // 2), BF)
+    shard = jax.ShapeDtypeStruct((2, own[1].shape[1] // ring, columns // 2), BF)
     return pl.pallas_call(
         partial(shard_kernel, ring),
-        out_shape=[shard] * 2,
+        out_shape=shard,
         in_specs=hbm_specs(4),
-        out_specs=vmem_specs(2),
+        out_specs=pl.BlockSpec(memory_space=pltpu.VMEM),
         scratch_shapes=[pltpu.SemaphoreType.DMA((10,))],
         compiler_params=pltpu.CompilerParams(vmem_limit_bytes=58 * 1024 * 1024),
     )(*own)
+
+
+def pack_kernel(*refs):
+    in_refs, out_refs, sem = refs[:-3], refs[-3:-1], refs[-1]
+    copies = []
+    for k, ref in enumerate(in_refs):
+        for layer, out_ref in enumerate(out_refs):
+            copies.append(pltpu.make_async_copy(ref.at[layer], out_ref.at[k], sem.at[len(copies)]))
+    for copy in copies:
+        copy.start()
+    for copy in copies:
+        copy.wait()
+
+
+def pack_shards(fetched):
+    block = jax.ShapeDtypeStruct((len(fetched),) + fetched[0].shape[1:], BF)
+    return pl.pallas_call(
+        pack_kernel,
+        out_shape=[block] * 2,
+        in_specs=any_specs(len(fetched)),
+        out_specs=any_specs(2),
+        scratch_shapes=[pltpu.SemaphoreType.DMA((2 * len(fetched),))],
+        compiler_params=pltpu.CompilerParams(vmem_limit_bytes=4 * 1024 * 1024),
+    )(*fetched)
 
 
 def load_weights(layer, piece_refs, own_refs, w_ref, sem):
@@ -240,7 +264,7 @@
                 scores = jnp.where(allowed, scores, -1e30)
             exps = jnp.exp(scores - jnp.max(scores, axis=-1, keepdims=True))
             probs = exps / jnp.sum(exps, axis=-1, keepdims=True)
-            probs_ref[k * count + a] = probs
+            probs_ref[k * count + a] = probs.astype(probs_ref.dtype)
             outs.append(dot(probs.astype(BF), values, 1, 0))
         mixed = jnp.concatenate(outs, axis=1).astype(BF)
         if k == 0:
@@ -251,7 +275,7 @@
     total = jnp.zeros(x.shape, F32)
     for k in range(PARTS):
         active, slope = gelu_and_slope(dot(second, weights.up(k), 1, 0))
-        slope_ref[k] = slope
+        slope_ref[k] = slope.astype(slope_ref.dtype)
         total += dot(active.astype(BF), weights.down(k), 1, 1)
     return middle, (middle.astype(F32) + total).astype(BF)
 
@@ -260,7 +284,7 @@
     middle = middle.astype(F32)
     total = jnp.zeros(x.shape, F32)
     for k in range(PARTS):
-        d_pre = (slope_ref[k] * dot(gradient, weights.down(k), 1, 0)).astype(BF)
+        d_pre = (slope_ref[k].astype(F32) * dot(gradient, weights.down(k), 1, 0)).astype(BF)
         total += dot(d_pre, weights.up(k), 1, 1)
     mid_grad = (gradient.astype(F32) + norm_pull(middle, total)).astype(BF)
     total = jnp.zeros(x.shape, F32)
@@ -273,7 +297,7 @@
         for a in range(count):
             queries, keys, values = head_parts(packed, a)
             d_out = d_mixed[:, a * HD : (a + 1) * HD]
-            probs = probs_ref[k * count + a]
+            probs = probs_ref[k * count + a].astype(F32)
             d_probs = dot(d_out, values, 1, 1)
             d_scores = probs * (d_probs - jnp.sum(d_probs * probs, axis=-1, keepdims=True))
             d_scores = (d_scores * HD**-0.5).astype(BF)
@@ -284,15 +308,22 @@
         total += dot(d_packed, weights.qkv(k), 1, 1)
         if k == 0:
             normed = norm_rows(x).astype(BF)
-            sums_ref[:, : 3 * width] = (dot(normed, d_packed, 0, 0) * factor).astype(BF)
-            sums_ref[:, 3 * width :] = (dot(mid_grad, mixed_ref[...], 0, 0) * factor).astype(BF)
+            first = (dot(normed, d_packed, 0, 0) * factor).astype(BF)
+            second = (dot(mid_grad, mixed_ref[...], 0, 0) * factor).astype(BF)
+            if len(sums_ref.shape) == 2:
+                sums_ref[:, : 3 * width] = first
+                sums_ref[:, 3 * width :] = second
+            else:
+                lats, _, rows, _ = sums_ref.shape
+                sums_ref[:, 0, :, : 3 * width] = first.reshape(lats, rows, 3 * width)
+                sums_ref[:, 0, :, 3 * width :] = second.reshape(lats, rows, width)
     return (mid_grad.astype(F32) + norm_pull(x, total)).astype(BF)
 
 
 def first_kernel(pieces, ends, *refs):
     x_ref, refs = refs[0], refs[1:]
     piece_refs, own_refs, refs = refs[:pieces], refs[pieces : pieces + 4], refs[pieces + 4 :]
-    out_refs, (w_ref, middle_ref, *saved), sem = refs[:PARTS], refs[PARTS:-1], refs[-1]
+    out_refs, (middle_ref, *saved), (w_ref, sem) = refs[:PARTS], refs[PARTS:-2], refs[-2:]
     copies = load_weights(0, piece_refs, own_refs, w_ref, sem)
     for copy in copies:
         copy.wait()
@@ -305,12 +336,12 @@
 
 def second_kernel(pieces, ends, factor, *refs):
     x_refs, grad_refs, refs = refs[:PARTS], refs[PARTS : 2 * PARTS], refs[2 * PARTS :]
-    column_ref, row_ref, *refs = refs
+    mask_ref, *refs = refs
     piece_refs, own_refs, refs = refs[:pieces], refs[pieces : pieces + 4], refs[pieces + 4 :]
     out_refs, (sums_ref, w_ref, *saved), sem = refs[:PARTS], refs[PARTS:-1], refs[-1]
     copies = load_weights(1, piece_refs, own_refs, w_ref, sem)
     x = jnp.concatenate([ref[...].astype(F32) for ref in x_refs], axis=0)
-    allowed = column_ref[...] == row_ref[...]
+    allowed = mask_ref[...] > 0
     for copy in copies:
         copy.wait()
     weights = Weights(w_ref, ends)
@@ -324,9 +355,17 @@
         out_refs[q][1] = result[q * rows : (q + 1) * rows]
 
 
-def third_kernel(ends, factor, *refs):
-    grad_refs, (x_ref, w_ref, middle_ref, *saved), (result_ref, sums_ref) = refs[:PARTS], refs[PARTS:-2], refs[-2:]
+def third_kernel(pieces, ends, factor, *refs):
+    grad_refs, (late_ref, x_ref), refs = refs[:PARTS], refs[PARTS : PARTS + 2], refs[PARTS + 2 :]
+    (middle_ref, *saved), refs = refs[:5], refs[5:]
+    piece_refs, own_refs, refs = refs[:pieces], refs[pieces : pieces + 4], refs[pieces + 4 :]
+    result_ref, sums_ref, w_ref, sem = refs
+    copies = load_weights(0, piece_refs, own_refs, w_ref, sem)
     gradient = jnp.concatenate([ref[1].astype(F32) for ref in grad_refs], axis=0).astype(BF)
+    lats, _, rows, columns = sums_ref.shape
+    sums_ref[:, 1] = late_ref[...].reshape(lats, rows, columns)
+    for copy in copies:
+        copy.wait()
     weights = Weights(w_ref, ends)
     result_ref[...] = backward(
         x_ref[...].astype(F32), middle_ref[...], gradient, weights, factor, *saved, sums_ref
@@ -345,7 +384,7 @@
     return [pl.BlockSpec(memory_space=pltpu.HBM)] * count
 
 
-PARAMS = pltpu.CompilerParams(vmem_limit_bytes=28 * 1024 * 1024)
+PARAMS = pltpu.CompilerParams(vmem_limit_bytes=36 * 1024 * 1024)
 
 
 def cost(flops):
@@ -368,23 +407,19 @@
     own = (qkv_weight.swapaxes(1, 2), proj_weight, up_weight, down_weight)
     ends = [0, 3 * head_width, 4 * head_width]
     ends = ends + [ends[-1] + up_weight.shape[2], ends[-1] + 2 * up_weight.shape[2]]
-    shards = weight_shards(own)
-    early = fetch_heads(shards[0])
-    ending = send_quads(list(after(quads(cotangent), early[0])), 1)
+    fetched = fetch_heads(weight_shards(own))
+    ending = send_quads(list(after(quads(cotangent), fetched[0])), 1)
     edge = ((jnp.arange(lat_rows) < 3) & (lax.axis_index("lat") == 0)).astype(jnp.int32)
     region = jnp.broadcast_to((shift_labels * 2 + edge[:, None])[None, :, :, None], (level_count, 6, 12, 1))
     labels = quads(region)[::-1].reshape(-1)
-    column, row = labels[:, None], labels[None, :]
+    mask = (labels[:, None] == labels[None, :]).astype(F32)
     start = quads(inputs).reshape(tokens, model_width)
-    early_block, start, column, row, *ending = lax.optimization_barrier(
-        (jnp.stack(early), start, column, row, *ending)
-    )
+    *fetched, start, mask, e0, e1, e2, e3 = lax.optimization_barrier((*fetched, start, mask, *ending))
+    ending = (e0, e1, e2, e3)
+    early_block, late_block = pack_shards(fetched)
     early_ring = ring_x(early_block, 1)
-    early_swaps = [swap_cores(early_block)]
-    late = fetch_heads(shards[1], early_swaps[:1])
-    late_ring = ring_x(jnp.stack(late), -1, (early_ring[1::2], early_ring[2:3]))
-    early_swaps += [swap_cores(piece) for piece in early_ring[1:]]
-    early_all = early_ring + early_swaps
+    late_ring = ring_x(late_block, -1, (early_ring[1::2], early_ring[2:3]))
+    early_all = early_ring + [swap_cores(piece) for piece in early_ring]
     late_swaps = {s: swap_cores(late_ring[s]) for s in (0, len(late_ring) - 1)}
     start = after(start, *late_swaps.values())
 
@@ -393,22 +428,23 @@
     piece = jax.ShapeDtypeStruct((quarter, model_width), BF)
     pair = jax.ShapeDtypeStruct((2, quarter, model_width), BF)
     sums = jax.ShapeDtypeStruct((model_width, 4 * head_width), BF)
-    full_weights = jax.ShapeDtypeStruct((PARTS, model_width, ends[-1]), BF)
+    weight_space = pltpu.VMEM((PARTS, model_width, ends[-1]), BF)
     saved = [
         jax.ShapeDtypeStruct((PARTS, tokens, 3 * head_width), BF),
         jax.ShapeDtypeStruct((width, tokens, tokens), F32),
         jax.ShapeDtypeStruct((tokens, head_width), BF),
         jax.ShapeDtypeStruct((PARTS, tokens, up_weight.shape[2]), F32),
     ]
+    held = [jax.ShapeDtypeStruct(s.shape, BF) for s in saved]
     pieces = len(early_all)
     semaphores = pltpu.SemaphoreType.DMA((pieces + 6,))
 
-    *quarters, early_weights, middle, packed, probs, mixed, slope = pl.pallas_call(
+    *quarters, middle, packed, probs, mixed, slope = pl.pallas_call(
         partial(first_kernel, pieces, ends),
-        out_shape=[piece] * PARTS + [full_weights, stream] + saved,
+        out_shape=[piece] * PARTS + [stream] + held,
         in_specs=vmem_specs(1) + any_specs(pieces) + hbm_specs(4),
-        out_specs=vmem_specs(PARTS + 6),
-        scratch_shapes=[semaphores],
+        out_specs=vmem_specs(PARTS + 5),
+        scratch_shapes=[weight_space, semaphores],
         compiler_params=PARAMS,
         cost_estimate=cost(1_800_000_000),
     )(start, *early_all, *own)
@@ -420,27 +456,27 @@
     *pairs, late_sum = pl.pallas_call(
         partial(second_kernel, pieces, ends, factor),
         out_shape=[pair] * PARTS + [sums],
-        in_specs=vmem_specs(2 * PARTS + 2) + any_specs(pieces) + hbm_specs(4),
+        in_specs=vmem_specs(2 * PARTS + 1) + any_specs(pieces) + hbm_specs(4),
         out_specs=vmem_specs(PARTS + 1),
-        scratch_shapes=[pltpu.VMEM(s.shape, s.dtype) for s in [full_weights] + saved] + [semaphores],
+        scratch_shapes=[weight_space] + [pltpu.VMEM(s.shape, s.dtype) for s in saved] + [semaphores],
         compiler_params=PARAMS,
         cost_estimate=cost(3_800_000_000),
-    )(*quarters, *ending, column, row, *late_all, *own)
+    )(*quarters, *ending, mask, *late_all, *own)
     pairs = send_quads(pairs, -1)
-    late_sum = scatter(late_sum, "lat")
-    input_grad, early_sum = pl.pallas_call(
-        partial(third_kernel, ends, factor),
-        out_shape=[stream, sums],
-        in_specs=vmem_specs(PARTS + 7),
+    lats, lons = lax.axis_size("lat"), lax.axis_size("lon")
+    both = jax.ShapeDtypeStruct((lats, 2, model_width // lats, 4 * head_width), BF)
+    input_grad, total = pl.pallas_call(
+        partial(third_kernel, pieces, ends, factor),
+        out_shape=[stream, both],
+        in_specs=vmem_specs(PARTS + 7) + any_specs(pieces) + hbm_specs(4),
         out_specs=vmem_specs(2),
+        scratch_shapes=[weight_space, semaphores],
         compiler_params=PARAMS,
         cost_estimate=cost(2_000_000_000),
-    )(*pairs, start, early_weights, middle, packed, probs, mixed, slope)
+    )(*pairs, late_sum, start, middle, packed, probs, mixed, slope, *early_all, *own)
 
     layer_out = unquads(jnp.stack([p[0] for p in pairs]))
-    total = jnp.stack([scatter(early_sum, "lat"), late_sum])
-    lons = lax.axis_size("lon")
-    total = total.astype(BF).reshape(2, lons, -1, 4 * head_width).swapaxes(0, 1)
+    total = scatter(total, "lat").astype(BF).reshape(2, lons, -1, 4 * head_width).swapaxes(0, 1)
     total = scatter(total, "lon").reshape(2, -1, 4 * head_width)
     pack_sum = total[:, :, : 3 * head_width].reshape(2, -1, 3, head_width)
     proj_sum = total[:, :, 3 * head_width :]

time: 223 us -> 209 us (0.937)
  local copies, waits for them, and re-layouts: 35.8 us -> 10.7 us
  starting transfers between devices: 111 us -> 87.9 us
  blocking collectives: 0 us -> 17.9 us
  waiting for transfers between devices: 43.9 us -> 61.4 us
    ppermute x2 -> x1, waiting for transfers between devices: 0.01 us -> 27.3 us  [fetch_heads(): one = lax.ppermute(shard, ('lat', 'head'), odd(1))]
    unnamed x94 -> x38, local copies, waits for them, and re-layouts: 30 us -> 3.31 us
    all_to_all x0 -> x1, blocking collectives: none -> 17.9 us  [scatter(): return jnp.sum(lax.all_to_all(parts, axis, 0, 0).astype(F32), axis=0)]
    ppermute x2 -> x1, starting transfers between devices: 16.3 us -> 4.55 us  [fetch_heads(): one = lax.ppermute(shard, ('lat', 'head'), odd(1))]
    ppermute x2 -> x1, waiting for transfers between devices: 9.35 us -> 0.01 us  [fetch_heads(): three = lax.ppermute(shard, ('lat', 'head'), odd(2))]
    all_to_all x3 -> x1, starting transfers between devices: 17.8 us -> 8.74 us  [scatter(): return jnp.sum(lax.all_to_all(parts, axis, 0, 0).astype(F32), axis=0)]
    ppermute x4, waiting for transfers between devices: 6.3 us -> 14.5 us  [ring_x(): blocks[sign % ring] = lax.ppermute(sent, 'lat', pairs(sign))]
    all_to_all x3 -> x1, waiting for transfers between devices: 14.4 us -> 6.39 us  [scatter(): return jnp.sum(lax.all_to_all(parts, axis, 0, 0).astype(F32), axis=0)]
  transfers between devices with their start and end apart: 32 -> 27, of which waited for: 12 -> 11; matrix products, arithmetic and copies ran while one was open for 2% -> 2% of each run, Pallas kernels for 5% -> 3%
where the time goes in v2:
time: 209 us; the launch traced here: 208 us
  starting transfers between devices  87.9 us (42%)
  waiting for transfers between devices  61.4 us (29%)
  Pallas kernels  28.2 us (13%)
  blocking collectives  17.9 us (9%)
  local copies, waits for them, and re-layouts  10.7 us (5%)
    ppermute x1, waiting for transfers between devices, fetch_heads(): one = lax.ppermute(shard, ('lat', 'head'), odd(1))  27.3 us
    ppermute x8, starting transfers between devices, swap_cores(): return lax.ppermute(piece, 'lon', [(i, i ^ 1) for i in range(size)])  23.8 us
    ppermute x9, starting transfers between devices, send_quads(): out.insert(1, lax.ppermute(pieces[q], ('lat', 'lon'), perm))  20.9 us
    all_to_all x1, blocking collectives, scatter(): return jnp.sum(lax.all_to_all(parts, axis, 0, 0).astype(F32), axis=0)  17.9 us
    ppermute x4, waiting for transfers between devices, ring_x(): blocks[sign % ring] = lax.ppermute(sent, 'lat', pairs(sign))  14.5 us
    pallas_call x1, Pallas kernels, per_device(): pl.pallas_call(partial(second_kernel, pieces, ends, factor), out_shape=[p...  12.2 us
    ppermute x1, starting transfers between devices, fetch_heads(): three = lax.ppermute(shard, ('lat', 'head'), odd(2))  11.5 us
    ppermute x4, starting transfers between devices, ring_x(): blocks[sign % ring] = lax.ppermute(sent, 'lat', pairs(sign))  11 us
  transfers between devices with their start and end apart: 27, of which 11 were waited for; matrix products, arithmetic and copies ran while one was open for 2% of the time, Pallas kernels for 3%

profile of v2, /device:TPU:1, one launch (start us, length us, event | category | flops | bytes accessed | tf_op | source)
XLA Modules:
  0.0 207.8 jit_solution(8626574372009214200)
XLA Ops:
  2.6 11.5 %collective-permute-start.2 = (bf16[2,128,768]{2,1,0:T(8,128)(2,1)}, bf16[2,128,768]{2,1,0:T(8,128)(2,1)}, u32[]{:S(2)}, u32[]{:S(2)}) collective-permute-start(bf16[2,128,768]{2,1,0:T(8,128)(2,1)} %shard_map.102), channel_id=1, source_target_pairs={{0,258},{1,259},{2,256},{3,257},{64,322},{65,323},{66,320},{67,321... | collective-permute-start | bytes 1179656 | tf_op jit(solution)/shard_map/ppermute | solution.py:106
  16.1 4.6 %collective-permute-start = (bf16[2,128,768]{2,1,0:T(8,128)(2,1)}, bf16[2,128,768]{2,1,0:T(8,128)(2,1)S(1)}, u32[]{:S(2)}, u32[]{:S(2)}) collective-permute-start(bf16[2,128,768]{2,1,0:T(8,128)(2,1)} %shard_map.102), channel_id=1, source_target_pairs={{0,259},{1,256},{2,257},{3,258},{64,323},{65,320},{66,321},{67,322... | collective-permute-start | bytes 1179656 | tf_op jit(solution)/shard_map/ppermute | solution.py:108
  21.9 27.3 %collective-permute-done.refs_0_ = bf16[2,128,768]{2,1,0:T(8,128)(2,1)S(1)} collective-permute-done((bf16[2,128,768]{2,1,0:T(8,128)(2,1)}, bf16[2,128,768]{2,1,0:T(8,128)(2,1)S(1)}, u32[]{:S(2)}, u32[]{:S(2)}) %collective-permute-start) | collective-permute-done | bytes 393248 | tf_op jit(solution)/shard_map/ppermute | solution.py:108
  50.7 4.6 %collective-permute-start.5 = (bf16[36,512]{1,0:T(8,128)(2,1)}, bf16[36,512]{1,0:T(8,128)(2,1)S(1)}, u32[]{:S(2)}, u32[]{:S(2)}) collective-permute-start(bf16[36,512]{1,0:T(8,128)(2,1)} %get-tuple-element.70), channel_id=1, source_target_pairs={{0,68},{4,72},{8,76},{12,80},{16,84},{20,88},{24,92},{28,96},{32,1... | collective-permute-start | bytes 110600 | tf_op jit(solution)/shard_map/ppermute | solution.py:82
  55.3 3.1 %collective-permute-start.4 = (bf16[36,512]{1,0:T(8,128)(2,1)}, bf16[36,512]{1,0:T(8,128)(2,1)S(1)}, u32[]{:S(2)}, u32[]{:S(2)}) collective-permute-start(bf16[36,512]{1,0:T(8,128)(2,1)} %get-tuple-element.71), channel_id=1, source_target_pairs={{0,64},{4,68},{8,72},{12,76},{16,80},{20,84},{24,88},{28,92},{32,9... | collective-permute-start | bytes 110600 | tf_op jit(solution)/shard_map/ppermute | solution.py:82
  67.1 3.4 %collective-permute-start.7 = (bf16[3,128,768]{2,1,0:T(8,128)(2,1)S(1)}, bf16[3,128,768]{2,1,0:T(8,128)(2,1)S(1)}, u32[]{:S(2)}, u32[]{:S(2)}) collective-permute-start(bf16[3,128,768]{2,1,0:T(8,128)(2,1)S(1)} %get-tuple-element.43.refs_1_.refs_11_), channel_id=1, source_target_pairs={{0,64},{64,128},{128,192},{192,0},{256,320},{320,384},{384,448},{4... | collective-permute-start | bytes 1769480 | tf_op jit(solution)/shard_map/ppermute | solution.py:128
  70.5 11.2 %collective-permute-done.8.refs_4_.refs_14_ = bf16[3,128,768]{2,1,0:T(8,128)(2,1)S(1)} collective-permute-done((bf16[3,128,768]{2,1,0:T(8,128)(2,1)S(1)}, bf16[3,128,768]{2,1,0:T(8,128)(2,1)S(1)}, u32[]{:S(2)}, u32[]{:S(2)}) %collective-permute-start.8) | collective-permute-done | bytes 589856 | tf_op jit(solution)/shard_map/ppermute | solution.py:128
  83.3 2.4 %collective-permute-start.9 = (bf16[3,128,768]{2,1,0:T(8,128)(2,1)S(1)}, bf16[3,128,768]{2,1,0:T(8,128)(2,1)S(1)}, u32[]{:S(2)}, u32[]{:S(2)}) collective-permute-start(bf16[3,128,768]{2,1,0:T(8,128)(2,1)S(1)} %get-tuple-element.55.refs_9_), channel_id=1, source_target_pairs={{0,192},{64,0},{128,64},{192,128},{256,448},{320,256},{384,320},{4... | collective-permute-start | bytes 1769480 | tf_op jit(solution)/shard_map/ppermute | solution.py:128
  85.7 4.3 %collective-permute-start.6 = (bf16[3,128,768]{2,1,0:T(8,128)(2,1)S(1)}, bf16[3,128,768]{2,1,0:T(8,128)(2,1)S(1)}, u32[]{:S(2)}, u32[]{:S(2)}) collective-permute-start(bf16[3,128,768]{2,1,0:T(8,128)(2,1)S(1)} %get-tuple-element.55.refs_9_), channel_id=1, source_target_pairs={{0,4},{4,0},{8,12},{12,8},{16,20},{20,16},{24,28},{28,24},{32,36},... | collective-permute-start | bytes 1769480 | tf_op jit(solution)/shard_map/ppermute | solution.py:114
  90.0 3.6 %collective-permute-start.11 = (bf16[3,128,768]{2,1,0:T(8,128)(2,1)S(1)}, bf16[3,128,768]{2,1,0:T(8,128)(2,1)S(1)}, u32[]{:S(2)}, u32[]{:S(2)}) collective-permute-start(bf16[3,128,768]{2,1,0:T(8,128)(2,1)S(1)} %collective-permute-done.7.refs_2_.refs_12_), channel_id=1, source_target_pairs={{0,64},{64,128},{128,192},{192,0},{256,320},{320,384},{384,448},{4... | collective-permute-start | bytes 1769480 | tf_op jit(solution)/shard_map/ppermute | solution.py:130
  93.6 2.2 %collective-permute-start.12 = (bf16[3,128,768]{2,1,0:T(8,128)(2,1)S(1)}, bf16[3,128,768]{2,1,0:T(8,128)(2,1)S(1)}, u32[]{:S(2)}, u32[]{:S(2)}) collective-permute-start(bf16[3,128,768]{2,1,0:T(8,128)(2,1)S(1)} %get-tuple-element.43.refs_1_.refs_11_), channel_id=1, source_target_pairs={{0,4},{4,0},{8,12},{12,8},{16,20},{20,16},{24,28},{28,24},{32,36},... | collective-permute-start | bytes 1769480 | tf_op jit(solution)/shard_map/ppermute | solution.py:114
  97.5 5.5 %collective-permute-start.10 = (bf16[3,128,768]{2,1,0:T(8,128)(2,1)S(1)}, bf16[3,128,768]{2,1,0:T(8,128)(2,1)S(1)}, u32[]{:S(2)}, u32[]{:S(2)}) collective-permute-start(bf16[3,128,768]{2,1,0:T(8,128)(2,1)S(1)} %collective-permute-done.9.refs_12_), channel_id=1, source_target_pairs={{0,4},{4,0},{8,12},{12,8},{16,20},{20,16},{24,28},{28,24},{32,36},... | collective-permute-start | bytes 1769480 | tf_op jit(solution)/shard_map/ppermute | solution.py:114
  104.9 2.4 %collective-permute-start.13 = (bf16[3,128,768]{2,1,0:T(8,128)(2,1)S(1)}, bf16[3,128,768]{2,1,0:T(8,128)(2,1)S(1)}, u32[]{:S(2)}, u32[]{:S(2)}) collective-permute-start(bf16[3,128,768]{2,1,0:T(8,128)(2,1)S(1)} %collective-permute-done.7.refs_2_.refs_12_), channel_id=1, source_target_pairs={{0,4},{4,0},{8,12},{12,8},{16,20},{20,16},{24,28},{28,24},{32,36},... | collective-permute-start | bytes 1769480 | tf_op jit(solution)/shard_map/ppermute | solution.py:114
  108.0 2.7 %collective-permute-start.14 = (bf16[3,128,768]{2,1,0:T(8,128)(2,1)S(1)}, bf16[3,128,768]{2,1,0:T(8,128)(2,1)S(1)}, u32[]{:S(2)}, u32[]{:S(2)}) collective-permute-start(bf16[3,128,768]{2,1,0:T(8,128)(2,1)S(1)} %collective-permute-done.11.refs_3_.refs_13_), channel_id=1, source_target_pairs={{0,4},{4,0},{8,12},{12,8},{16,20},{20,16},{24,28},{28,24},{32,36},... | collective-permute-start | bytes 1769480 | tf_op jit(solution)/shard_map/ppermute | solution.py:114
  110.7 2.0 collective-permute-start.20
  112.8 3.3 %collective-permute-start.19 = (bf16[3,128,768]{2,1,0:T(8,128)(2,1)S(1)}, bf16[3,128,768]{2,1,0:T(8,128)(2,1)S(1)}, u32[]{:S(2)}, u32[]{:S(2)}) collective-permute-start(bf16[3,128,768]{2,1,0:T(8,128)(2,1)S(1)} %get-tuple-element.55.refs_9_), channel_id=1, source_target_pairs={{0,64},{64,128},{128,192},{192,0},{256,320},{320,384},{384,448},{4... | collective-permute-start | bytes 1769480 | tf_op jit(solution)/shard_map/ppermute | solution.py:128
  116.1 5.5 %shard_map.104 = (bf16[36,512]{1,0:T(8,128)(2,1)S(1)}, bf16[36,512]{1,0:T(8,128)(2,1)S(1)}, bf16[36,512]{1,0:T(8,128)(2,1)S(1)}, bf16[36,512]{1,0:T(8,128)(2,1)S...) custom-call(bf16[144,512]{1,0:T(8,128)(2,1)S(1)} %reshape_reshape.6., ...), custom_call_target="tpu_custom_call" | custom-call | flops 1800000000 | bytes 8000000 | tf_op jit(solution)/shard_map/pallas_call | solution.py:442
  121.6 2.0 collective-permute-start.16
  123.6 2.2 %collective-permute-start.17 = (bf16[36,512]{1,0:T(8,128)(2,1)S(1)}, bf16[36,512]{1,0:T(8,128)(2,1)S(1)}, u32[]{:S(2)}, u32[]{:S(2)}) collective-permute-start(bf16[36,512]{1,0:T(8,128)(2,1)S(1)} %get-tuple-element.48), channel_id=1, source_target_pairs={{0,64},{4,68},{8,72},{12,76},{16,80},{20,84},{24,88},{28,92},{32,9... | collective-permute-start | bytes 110600 | tf_op jit(solution)/shard_map/ppermute | solution.py:82
  125.9 2.2 %collective-permute-start.18 = (bf16[36,512]{1,0:T(8,128)(2,1)S(1)}, bf16[36,512]{1,0:T(8,128)(2,1)S(1)}, u32[]{:S(2)}, u32[]{:S(2)}) collective-permute-start(bf16[36,512]{1,0:T(8,128)(2,1)S(1)} %get-tuple-element.49), channel_id=1, source_target_pairs={{0,68},{4,72},{8,76},{12,80},{16,84},{20,88},{24,92},{28,96},{32,1... | collective-permute-start | bytes 110600 | tf_op jit(solution)/shard_map/ppermute | solution.py:82
  128.1 2.5 %collective-permute-done.17.refs_2_ = bf16[36,512]{1,0:T(8,128)(2,1)S(1)} collective-permute-done((bf16[36,512]{1,0:T(8,128)(2,1)S(1)}, bf16[36,512]{1,0:T(8,128)(2,1)S(1)}, u32[]{:S(2)}, u32[]{:S(2)}) %collective-permute-start.17) | collective-permute-done | bytes 36896 | tf_op jit(solution)/shard_map/ppermute | solution.py:82
  130.5 3.1 %collective-permute-done.18.refs_3_ = bf16[36,512]{1,0:T(8,128)(2,1)S(1)} collective-permute-done((bf16[36,512]{1,0:T(8,128)(2,1)S(1)}, bf16[36,512]{1,0:T(8,128)(2,1)S(1)}, u32[]{:S(2)}, u32[]{:S(2)}) %collective-permute-start.18) | collective-permute-done | bytes 36896 | tf_op jit(solution)/shard_map/ppermute | solution.py:82
  133.6 2.7 %collective-permute-start.21 = (bf16[3,128,768]{2,1,0:T(8,128)(2,1)S(1)}, bf16[3,128,768]{2,1,0:T(8,128)(2,1)S(1)}, u32[]{:S(2)}, u32[]{:S(2)}) collective-permute-start(bf16[3,128,768]{2,1,0:T(8,128)(2,1)S(1)} %collective-permute-done.19.refs_10_), channel_id=1, source_target_pairs={{0,4},{4,0},{8,12},{12,8},{16,20},{20,16},{24,28},{28,24},{32,36},... | collective-permute-start | bytes 1769480 | tf_op jit(solution)/shard_map/ppermute | solution.py:114
  136.3 2.1 %collective-permute-start.22 = (bf16[3,128,768]{2,1,0:T(8,128)(2,1)S(1)}, bf16[3,128,768]{2,1,0:T(8,128)(2,1)S(1)}, u32[]{:S(2)}, u32[]{:S(2)}) collective-permute-start(bf16[3,128,768]{2,1,0:T(8,128)(2,1)S(1)} %collective-permute-done.20.refs_11_), channel_id=1, source_target_pairs={{0,4},{4,0},{8,12},{12,8},{16,20},{20,16},{24,28},{28,24},{32,36},... | collective-permute-start | bytes 1769480 | tf_op jit(solution)/shard_map/ppermute | solution.py:114
  140.2 12.2 %shard_map.105 = (bf16[2,36,512]{2,1,0:T(8,128)(2,1)S(1)}, bf16[2,36,512]{2,1,0:T(8,128)(2,1)S(1)}, bf16[2,36,512]{2,1,0:T(8,128)(2,1)S(1)}, bf16[2,36,512]{2,1,0:T(8,128)(2,1)S(1)}, bf16[512,512]{1,0:T(8,128)(2,1)S(1)}) custom-call(bf16[36,512]{1,0:T(8,128)(2,1)S(1)} %get-tuple-element.46.refs_0_, bf16[36,512]{1,0:T(8,128)(2,1)S(1)} %collective-permute-done.16.refs_1_, ...), custom_call_target="tpu_custom_call" | custom-call | flops 3800000000 | bytes 8000000 | tf_op jit(solution)/shard_map/pallas_call | solution.py:456
  152.6 3.0 %collective-permute-start.24 = (bf16[2,36,512]{2,1,0:T(8,128)(2,1)S(1)}, bf16[2,36,512]{2,1,0:T(8,128)(2,1)S(1)}, u32[]{:S(2)}, u32[]{:S(2)}) collective-permute-start(bf16[2,36,512]{2,1,0:T(8,128)(2,1)S(1)} %get-tuple-element.60), channel_id=1, source_target_pairs={{0,448},{4,452},{8,456},{12,460},{16,464},{20,468},{24,472},{28,47... | collective-permute-start | bytes 221192 | tf_op jit(solution)/shard_map/ppermute | solution.py:82
  155.6 3.1 %collective-permute-start.25 = (bf16[2,36,512]{2,1,0:T(8,128)(2,1)S(1)}, bf16[2,36,512]{2,1,0:T(8,128)(2,1)S(1)}, u32[]{:S(2)}, u32[]{:S(2)}) collective-permute-start(bf16[2,36,512]{2,1,0:T(8,128)(2,1)S(1)} %get-tuple-element.61), channel_id=1, source_target_pairs={{0,508},{4,448},{8,452},{12,456},{16,460},{20,464},{24,468},{28,47... | collective-permute-start | bytes 221192 | tf_op jit(solution)/shard_map/ppermute | solution.py:82
  158.7 3.5 %collective-permute-done.25.refs_3_ = bf16[2,36,512]{2,1,0:T(8,128)(2,1)S(1)} collective-permute-done((bf16[2,36,512]{2,1,0:T(8,128)(2,1)S(1)}, bf16[2,36,512]{2,1,0:T(8,128)(2,1)S(1)}, u32[]{:S(2)}, u32[]{:S(2)}) %collective-permute-start.25) | collective-permute-done | bytes 73760 | tf_op jit(solution)/shard_map/ppermute | solution.py:82
  162.2 6.8 %shard_map.106 = (bf16[144,512]{1,0:T(8,128)(2,1)S(1)}, bf16[8,2,64,512]{3,2,1,0:T(8,128)(2,1)S(1)}) custom-call(bf16[2,36,512]{2,1,0:T(8,128)(2,1)S(1)} %get-tuple-element.58.refs_0_, bf16[2,36,512]{2,1,0:T(8,128)(2,1)S(1)} %collective-permute-done.23.refs_1_, bf16[2,36,512]{2,1,0:T(8,128)(2,1)S(1)} %collective-permute-done.24.refs_2_, ...), custom_call_target="tpu_custom_call" | custom-call | flops 2000000000 | bytes 8000000 | tf_op jit(solution)/shard_map/pallas_call | solution.py:468
  169.7 17.9 %all_to_all.10 = bf16[8,128,512]{2,1,0:T(8,128)(2,1)S(1)} all-to-all(bf16[8,128,512]{2,1,0:T(8,128)(2,1)S(1)} %bitcast.40), channel_id=1, replica_groups=mesh['lat'=8,'lon'=16,'head'=4] {'lat'}, dimensions={0} | all-to-all | bytes 2097152 | tf_op jit(solution)/shard_map/all_to_all | solution.py:397
  188.6 8.7 %all-to-all-start.1 = ((bf16[16,8,512]{2,1,0:T(8,128)(2,1)}), bf16[16,8,512]{2,1,0:T(8,128)(2,1)S(1)}, u32[]{:S(2)}, u32[]{:S(2)}) async-start(bf16[16,8,512]{2,1,0:T(8,128)(2,1)} %copy.45), calls=%async_computation.1 | async-start | bytes 262144 | tf_op jit(solution)/shard_map/all_to_all | solution.py:397
  200.2 6.4 %all-to-all-done.1 = bf16[16,8,512]{2,1,0:T(8,128)(2,1)S(1)} async-done(((bf16[16,8,512]{2,1,0:T(8,128)(2,1)}), bf16[16,8,512]{2,1,0:T(8,128)(2,1)S(1)}, u32[]{:S(2)}, u32[]{:S(2)}) %all-to-all-start.1) | async-done | bytes 131104 | tf_op jit(solution)/shard_map/all_to_all | solution.py:397
  (102 shorter events, 28.7 us)
Async XLA Ops:
  0.6 58.4 %copy-start.17 = (bf16[2,6,12,512]{3,0,2,1:T(2,128)(2,1)S(1)}, bf16[2,6,12,512]{3,0,2,1:T(2,128)(2,1)}, u32[]{:S(2)}) copy-start(bf16[2,6,12,512]{3,0,2,1:T(2,128)(2,1)} %param.7) | copy-start | bytes 442372
  2.6 58.1 %collective-permute-start.2 = (bf16[2,128,768]{2,1,0:T(8,128)(2,1)}, bf16[2,128,768]{2,1,0:T(8,128)(2,1)}, u32[]{:S(2)}, u32[]{:S(2)}) collective-permute-start(bf16[2,128,768]{2,1,0:T(8,128)(2,1)} %shard_map.102), channel_id=1, source_target_pairs={{0,258},{1,259},{2,256},{3,257},{64,322},{65,323},{66,320},{67,321... | collective-permute-start | bytes 1179656 | tf_op jit(solution)/shard_map/ppermute | solution.py:106
  14.1 46.6 %collective-permute-start.1 = (bf16[2,128,768]{2,1,0:T(8,128)(2,1)}, bf16[2,128,768]{2,1,0:T(8,128)(2,1)}, u32[]{:S(2)}, u32[]{:S(2)}) collective-permute-start(bf16[2,128,768]{2,1,0:T(8,128)(2,1)} %shard_map.102), channel_id=1, source_target_pairs={{0,3},{1,0},{2,1},{3,2},{64,67},{65,64},{66,65},{67,66},{128,131},... | collective-permute-start | bytes 1179656 | tf_op jit(solution)/shard_map/ppermute | solution.py:107
  16.1 33.1 %collective-permute-start = (bf16[2,128,768]{2,1,0:T(8,128)(2,1)}, bf16[2,128,768]{2,1,0:T(8,128)(2,1)S(1)}, u32[]{:S(2)}, u32[]{:S(2)}) collective-permute-start(bf16[2,128,768]{2,1,0:T(8,128)(2,1)} %shard_map.102), channel_id=1, source_target_pairs={{0,259},{1,256},{2,257},{3,258},{64,323},{65,320},{66,321},{67,322... | collective-permute-start | bytes 1179656 | tf_op jit(solution)/shard_map/ppermute | solution.py:108
  21.7 94.4 %copy-start.3 = (bf16[2,512,128]{2,1,0:T(8,128)(2,1)S(1)}, bf16[2,512,128]{2,1,0:T(8,128)(2,1)}, u32[]{:S(2)}) copy-start(bf16[2,512,128]{2,1,0:T(8,128)(2,1)} %refs_20_.3) | copy-start | bytes 786436
  21.8 94.3 %copy-start.2 = (bf16[2,512,3,128]{3,1,2,0:T(8,128)(2,1)S(1)}, bf16[2,512,3,128]{3,1,2,0:T(8,128)(2,1)}, u32[]{:S(2)}) copy-start(bf16[2,512,3,128]{3,1,2,0:T(8,128)(2,1)} %param.9) | copy-start | bytes 2359300
  50.0 66.1 %copy-start.1 = (bf16[2,512,512]{2,1,0:T(8,128)(2,1)S(1)}, bf16[2,512,512]{2,1,0:T(8,128)(2,1)}, u32[]{:S(2)}) copy-start(bf16[2,512,512]{2,1,0:T(8,128)(2,1)} %refs_22_.1) | copy-start | bytes 3145732
  50.7 65.4 %copy-start = (bf16[2,512,512]{2,1,0:T(8,128)(2,1)S(1)}, bf16[2,512,512]{2,1,0:T(8,128)(2,1)}, u32[]{:S(2)}) copy-start(bf16[2,512,512]{2,1,0:T(8,128)(2,1)} %refs_21_.1) | copy-start | bytes 3145732
  50.7 10.1 %collective-permute-start.5 = (bf16[36,512]{1,0:T(8,128)(2,1)}, bf16[36,512]{1,0:T(8,128)(2,1)S(1)}, u32[]{:S(2)}, u32[]{:S(2)}) collective-permute-start(bf16[36,512]{1,0:T(8,128)(2,1)} %get-tuple-element.70), channel_id=1, source_target_pairs={{0,68},{4,72},{8,76},{12,80},{16,84},{20,88},{24,92},{28,96},{32,1... | collective-permute-start | bytes 110600 | tf_op jit(solution)/shard_map/ppermute | solution.py:82
  55.3 7.1 %collective-permute-start.4 = (bf16[36,512]{1,0:T(8,128)(2,1)}, bf16[36,512]{1,0:T(8,128)(2,1)S(1)}, u32[]{:S(2)}, u32[]{:S(2)}) collective-permute-start(bf16[36,512]{1,0:T(8,128)(2,1)} %get-tuple-element.71), channel_id=1, source_target_pairs={{0,64},{4,68},{8,72},{12,76},{16,80},{20,84},{24,88},{28,92},{32,9... | collective-permute-start | bytes 110600 | tf_op jit(solution)/shard_map/ppermute | solution.py:82
  58.4 3.9 %collective-permute-start.3 = (bf16[36,512]{1,0:T(8,128)(2,1)}, bf16[36,512]{1,0:T(8,128)(2,1)}, u32[]{:S(2)}, u32[]{:S(2)}) collective-permute-start(bf16[36,512]{1,0:T(8,128)(2,1)} %get-tuple-element.72), channel_id=1, source_target_pairs={{0,4},{4,8},{8,12},{12,16},{16,20},{20,24},{24,28},{28,32},{32,36}... | collective-permute-start | bytes 110600 | tf_op jit(solution)/shard_map/ppermute | solution.py:82
  65.2 16.5 %collective-permute-start.8 = (bf16[3,128,768]{2,1,0:T(8,128)(2,1)S(1)}, bf16[3,128,768]{2,1,0:T(8,128)(2,1)S(1)}, u32[]{:S(2)}, u32[]{:S(2)}) collective-permute-start(bf16[3,128,768]{2,1,0:T(8,128)(2,1)S(1)} %get-tuple-element.43.refs_1_.refs_11_), channel_id=1, source_target_pairs={{0,192},{64,0},{128,64},{192,128},{256,448},{320,256},{384,320},{4... | collective-permute-start | bytes 1769480 | tf_op jit(solution)/shard_map/ppermute | solution.py:128
  67.1 16.2 %collective-permute-start.7 = (bf16[3,128,768]{2,1,0:T(8,128)(2,1)S(1)}, bf16[3,128,768]{2,1,0:T(8,128)(2,1)S(1)}, u32[]{:S(2)}, u32[]{:S(2)}) collective-permute-start(bf16[3,128,768]{2,1,0:T(8,128)(2,1)S(1)} %get-tuple-element.43.refs_1_.refs_11_), channel_id=1, source_target_pairs={{0,64},{64,128},{128,192},{192,0},{256,320},{320,384},{384,448},{4... | collective-permute-start | bytes 1769480 | tf_op jit(solution)/shard_map/ppermute | solution.py:128
  83.3 14.2 %collective-permute-start.9 = (bf16[3,128,768]{2,1,0:T(8,128)(2,1)S(1)}, bf16[3,128,768]{2,1,0:T(8,128)(2,1)S(1)}, u32[]{:S(2)}, u32[]{:S(2)}) collective-permute-start(bf16[3,128,768]{2,1,0:T(8,128)(2,1)S(1)} %get-tuple-element.55.refs_9_), channel_id=1, source_target_pairs={{0,192},{64,0},{128,64},{192,128},{256,448},{320,256},{384,320},{4... | collective-permute-start | bytes 1769480 | tf_op jit(solution)/shard_map/ppermute | solution.py:128
  85.7 19.2 %collective-permute-start.6 = (bf16[3,128,768]{2,1,0:T(8,128)(2,1)S(1)}, bf16[3,128,768]{2,1,0:T(8,128)(2,1)S(1)}, u32[]{:S(2)}, u32[]{:S(2)}) collective-permute-start(bf16[3,128,768]{2,1,0:T(8,128)(2,1)S(1)} %get-tuple-element.55.refs_9_), channel_id=1, source_target_pairs={{0,4},{4,0},{8,12},{12,8},{16,20},{20,16},{24,28},{28,24},{32,36},... | collective-permute-start | bytes 1769480 | tf_op jit(solution)/shard_map/ppermute | solution.py:114
  90.0 18.1 %collective-permute-start.11 = (bf16[3,128,768]{2,1,0:T(8,128)(2,1)S(1)}, bf16[3,128,768]{2,1,0:T(8,128)(2,1)S(1)}, u32[]{:S(2)}, u32[]{:S(2)}) collective-permute-start(bf16[3,128,768]{2,1,0:T(8,128)(2,1)S(1)} %collective-permute-done.7.refs_2_.refs_12_), channel_id=1, source_target_pairs={{0,64},{64,128},{128,192},{192,0},{256,320},{320,384},{384,448},{4... | collective-permute-start | bytes 1769480 | tf_op jit(solution)/shard_map/ppermute | solution.py:130
  93.6 17.2 %collective-permute-start.12 = (bf16[3,128,768]{2,1,0:T(8,128)(2,1)S(1)}, bf16[3,128,768]{2,1,0:T(8,128)(2,1)S(1)}, u32[]{:S(2)}, u32[]{:S(2)}) collective-permute-start(bf16[3,128,768]{2,1,0:T(8,128)(2,1)S(1)} %get-tuple-element.43.refs_1_.refs_11_), channel_id=1, source_target_pairs={{0,4},{4,0},{8,12},{12,8},{16,20},{20,16},{24,28},{28,24},{32,36},... | collective-permute-start | bytes 1769480 | tf_op jit(solution)/shard_map/ppermute | solution.py:114
  97.5 15.3 %collective-permute-start.10 = (bf16[3,128,768]{2,1,0:T(8,128)(2,1)S(1)}, bf16[3,128,768]{2,1,0:T(8,128)(2,1)S(1)}, u32[]{:S(2)}, u32[]{:S(2)}) collective-permute-start(bf16[3,128,768]{2,1,0:T(8,128)(2,1)S(1)} %collective-permute-done.9.refs_12_), channel_id=1, source_target_pairs={{0,4},{4,0},{8,12},{12,8},{16,20},{20,16},{24,28},{28,24},{32,36},... | collective-permute-start | bytes 1769480 | tf_op jit(solution)/shard_map/ppermute | solution.py:114
  103.0 13.1 %collective-permute-start.15 = (bf16[3,128,768]{2,1,0:T(8,128)(2,1)S(1)}, bf16[3,128,768]{2,1,0:T(8,128)(2,1)S(1)}, u32[]{:S(2)}, u32[]{:S(2)}) collective-permute-start(bf16[3,128,768]{2,1,0:T(8,128)(2,1)S(1)} %collective-permute-done.8.refs_4_.refs_14_), channel_id=1, source_target_pairs={{0,4},{4,0},{8,12},{12,8},{16,20},{20,16},{24,28},{28,24},{32,36},... | collective-permute-start | bytes 1769480 | tf_op jit(solution)/shard_map/ppermute | solution.py:114
  104.9 11.2 %collective-permute-start.13 = (bf16[3,128,768]{2,1,0:T(8,128)(2,1)S(1)}, bf16[3,128,768]{2,1,0:T(8,128)(2,1)S(1)}, u32[]{:S(2)}, u32[]{:S(2)}) collective-permute-start(bf16[3,128,768]{2,1,0:T(8,128)(2,1)S(1)} %collective-permute-done.7.refs_2_.refs_12_), channel_id=1, source_target_pairs={{0,4},{4,0},{8,12},{12,8},{16,20},{20,16},{24,28},{28,24},{32,36},... | collective-permute-start | bytes 1769480 | tf_op jit(solution)/shard_map/ppermute | solution.py:114
  108.0 8.0 %collective-permute-start.14 = (bf16[3,128,768]{2,1,0:T(8,128)(2,1)S(1)}, bf16[3,128,768]{2,1,0:T(8,128)(2,1)S(1)}, u32[]{:S(2)}, u32[]{:S(2)}) collective-permute-start(bf16[3,128,768]{2,1,0:T(8,128)(2,1)S(1)} %collective-permute-done.11.refs_3_.refs_13_), channel_id=1, source_target_pairs={{0,4},{4,0},{8,12},{12,8},{16,20},{20,16},{24,28},{28,24},{32,36},... | collective-permute-start | bytes 1769480 | tf_op jit(solution)/shard_map/ppermute | solution.py:114
  110.7 17.3 %collective-permute-start.20 = (bf16[3,128,768]{2,1,0:T(8,128)(2,1)S(1)}, bf16[3,128,768]{2,1,0:T(8,128)(2,1)S(1)}, u32[]{:S(2)}, u32[]{:S(2)}) collective-permute-start(bf16[3,128,768]{2,1,0:T(8,128)(2,1)S(1)} %collective-permute-done.9.refs_12_), channel_id=1, source_target_pairs={{0,192},{64,0},{128,64},{192,128},{256,448},{320,256},{384,320},{4... | collective-permute-start | bytes 1769480 | tf_op jit(solution)/shard_map/ppermute | solution.py:130
  112.8 20.9 %collective-permute-start.19 = (bf16[3,128,768]{2,1,0:T(8,128)(2,1)S(1)}, bf16[3,128,768]{2,1,0:T(8,128)(2,1)S(1)}, u32[]{:S(2)}, u32[]{:S(2)}) collective-permute-start(bf16[3,128,768]{2,1,0:T(8,128)(2,1)S(1)} %get-tuple-element.55.refs_9_), channel_id=1, source_target_pairs={{0,64},{64,128},{128,192},{192,0},{256,320},{320,384},{384,448},{4... | collective-permute-start | bytes 1769480 | tf_op jit(solution)/shard_map/ppermute | solution.py:128
  121.6 6.4 %collective-permute-start.16 = (bf16[36,512]{1,0:T(8,128)(2,1)S(1)}, bf16[36,512]{1,0:T(8,128)(2,1)S(1)}, u32[]{:S(2)}, u32[]{:S(2)}) collective-permute-start(bf16[36,512]{1,0:T(8,128)(2,1)S(1)} %get-tuple-element.47), channel_id=1, source_target_pairs={{0,4},{4,8},{8,12},{12,16},{16,20},{20,24},{24,28},{28,32},{32,36}... | collective-permute-start | bytes 110600 | tf_op jit(solution)/shard_map/ppermute | solution.py:82
  123.6 6.9 %collective-permute-start.17 = (bf16[36,512]{1,0:T(8,128)(2,1)S(1)}, bf16[36,512]{1,0:T(8,128)(2,1)S(1)}, u32[]{:S(2)}, u32[]{:S(2)}) collective-permute-start(bf16[36,512]{1,0:T(8,128)(2,1)S(1)} %get-tuple-element.48), channel_id=1, source_target_pairs={{0,64},{4,68},{8,72},{12,76},{16,80},{20,84},{24,88},{28,92},{32,9... | collective-permute-start | bytes 110600 | tf_op jit(solution)/shard_map/ppermute | solution.py:82
  125.9 7.7 %collective-permute-start.18 = (bf16[36,512]{1,0:T(8,128)(2,1)S(1)}, bf16[36,512]{1,0:T(8,128)(2,1)S(1)}, u32[]{:S(2)}, u32[]{:S(2)}) collective-permute-start(bf16[36,512]{1,0:T(8,128)(2,1)S(1)} %get-tuple-element.49), channel_id=1, source_target_pairs={{0,68},{4,72},{8,76},{12,80},{16,84},{20,88},{24,92},{28,96},{32,1... | collective-permute-start | bytes 110600 | tf_op jit(solution)/shard_map/ppermute | solution.py:82
  133.6 4.8 %collective-permute-start.21 = (bf16[3,128,768]{2,1,0:T(8,128)(2,1)S(1)}, bf16[3,128,768]{2,1,0:T(8,128)(2,1)S(1)}, u32[]{:S(2)}, u32[]{:S(2)}) collective-permute-start(bf16[3,128,768]{2,1,0:T(8,128)(2,1)S(1)} %collective-permute-done.19.refs_10_), channel_id=1, source_target_pairs={{0,4},{4,0},{8,12},{12,8},{16,20},{20,16},{24,28},{28,24},{32,36},... | collective-permute-start | bytes 1769480 | tf_op jit(solution)/shard_map/ppermute | solution.py:114
  136.3 3.9 %collective-permute-start.22 = (bf16[3,128,768]{2,1,0:T(8,128)(2,1)S(1)}, bf16[3,128,768]{2,1,0:T(8,128)(2,1)S(1)}, u32[]{:S(2)}, u32[]{:S(2)}) collective-permute-start(bf16[3,128,768]{2,1,0:T(8,128)(2,1)S(1)} %collective-permute-done.20.refs_11_), channel_id=1, source_target_pairs={{0,4},{4,0},{8,12},{12,8},{16,20},{20,16},{24,28},{28,24},{32,36},... | collective-permute-start | bytes 1769480 | tf_op jit(solution)/shard_map/ppermute | solution.py:114
  152.4 6.3 %collective-permute-start.23 = (bf16[2,36,512]{2,1,0:T(8,128)(2,1)S(1)}, bf16[2,36,512]{2,1,0:T(8,128)(2,1)S(1)}, u32[]{:S(2)}, u32[]{:S(2)}) collective-permute-start(bf16[2,36,512]{2,1,0:T(8,128)(2,1)S(1)} %get-tuple-element.59), channel_id=1, source_target_pairs={{0,60},{4,0},{8,4},{12,8},{16,12},{20,16},{24,20},{28,24},{32,28},... | collective-permute-start | bytes 221192 | tf_op jit(solution)/shard_map/ppermute | solution.py:82
  152.6 6.1 %collective-permute-start.24 = (bf16[2,36,512]{2,1,0:T(8,128)(2,1)S(1)}, bf16[2,36,512]{2,1,0:T(8,128)(2,1)S(1)}, u32[]{:S(2)}, u32[]{:S(2)}) collective-permute-start(bf16[2,36,512]{2,1,0:T(8,128)(2,1)S(1)} %get-tuple-element.60), channel_id=1, source_target_pairs={{0,448},{4,452},{8,456},{12,460},{16,464},{20,468},{24,472},{28,47... | collective-permute-start | bytes 221192 | tf_op jit(solution)/shard_map/ppermute | solution.py:82
  155.6 6.7 %collective-permute-start.25 = (bf16[2,36,512]{2,1,0:T(8,128)(2,1)S(1)}, bf16[2,36,512]{2,1,0:T(8,128)(2,1)S(1)}, u32[]{:S(2)}, u32[]{:S(2)}) collective-permute-start(bf16[2,36,512]{2,1,0:T(8,128)(2,1)S(1)} %get-tuple-element.61), channel_id=1, source_target_pairs={{0,508},{4,448},{8,452},{12,456},{16,460},{20,464},{24,468},{28,47... | collective-permute-start | bytes 221192 | tf_op jit(solution)/shard_map/ppermute | solution.py:82
  188.6 17.9 %all-to-all-start.1 = ((bf16[16,8,512]{2,1,0:T(8,128)(2,1)}), bf16[16,8,512]{2,1,0:T(8,128)(2,1)S(1)}, u32[]{:S(2)}, u32[]{:S(2)}) async-start(bf16[16,8,512]{2,1,0:T(8,128)(2,1)} %copy.45), calls=%async_computation.1 | async-start | bytes 262144 | tf_op jit(solution)/shard_map/all_to_all | solution.py:397
  (17 other events, 289.7 us)

commit v3 on v2

--- a/solution.py
+++ b/solution.py
@@ -114,26 +114,29 @@
     return lax.ppermute(piece, "lon", [(i, i ^ 1) for i in range(size)])
 
 
-def ring_x(own, long_way, gates=((), ())):
-    low, ring = lat_parts()
-    size = lax.axis_size("lat")
-
-    def pairs(by):
-        return [(i, i // ring * ring + (i + by) % ring) for i in range(size)]
-
-    blocks = {0: own}
-    for sign, gate in zip((long_way, -long_way), gates):
-        if ring > 2 or sign == long_way:
-            sent = after(own, *gate)
-            blocks[sign % ring] = lax.ppermute(sent, "lat", pairs(sign))
+def along_x(block, by):
+    ring, size = lat_parts()[1], lax.axis_size("lat")
+    return lax.ppermute(block, "lat", [(i, i // ring * ring + (i + by) % ring) for i in range(size)])
+
+
+def ring_near(own):
+    ring = lat_parts()[1]
+    blocks = {0: own, 1 % ring: along_x(own, 1)}
     if ring > 2:
-        blocks[2] = lax.ppermute(blocks[long_way % ring], "lat", pairs(long_way))
+        blocks[ring - 1] = along_x(own, -1)
+    return blocks
+
+
+def ring_far(blocks, by, *gate):
+    ring = lat_parts()[1]
+    if ring > 2:
+        blocks[2] = along_x(after(blocks[by % ring], *gate), by)
     return [blocks[s] for s in range(ring)]
 
 
 def shard_kernel(ring, qkv_ref, proj_ref, up_ref, down_ref, *refs):
-    out_ref, sem = refs
-    rows, half = out_ref.shape[1:]
+    out_refs, sem = refs[:-1], refs[-1]
+    rows, half = out_refs[0].shape
     side = lax.axis_index("lon") % 2
     start = pl.multiple_of(lax.axis_index("lat") % ring * rows, rows)
     width, hidden = proj_ref.shape[2], up_ref.shape[2]
@@ -141,10 +144,10 @@
 
     def run(views):
         copies = []
-        for layer in range(2):
+        for layer, out_ref in enumerate(out_refs):
             at = 0
             for view in views(layer):
-                target = out_ref.at[layer, :, pl.ds(at, view.shape[1])]
+                target = out_ref.at[:, pl.ds(at, view.shape[1])]
                 copies.append(pltpu.make_async_copy(view, target, sem.at[len(copies)]))
                 at += view.shape[1]
         for copy in copies:
@@ -172,23 +175,20 @@
 def weight_shards(own):
     ring = lat_parts()[1]
     columns = 4 * own[1].shape[2] + 2 * own[2].shape[2]
-    shard = jax.ShapeDtypeStruct((2, own[1].shape[1] // ring, columns // 2), BF)
+    shard = jax.ShapeDtypeStruct((own[1].shape[1] // ring, columns // 2), BF)
     return pl.pallas_call(
         partial(shard_kernel, ring),
-        out_shape=shard,
+        out_shape=[shard] * 2,
         in_specs=hbm_specs(4),
-        out_specs=pl.BlockSpec(memory_space=pltpu.VMEM),
+        out_specs=vmem_specs(2),
         scratch_shapes=[pltpu.SemaphoreType.DMA((10,))],
         compiler_params=pltpu.CompilerParams(vmem_limit_bytes=58 * 1024 * 1024),
     )(*own)
 
 
 def pack_kernel(*refs):
-    in_refs, out_refs, sem = refs[:-3], refs[-3:-1], refs[-1]
-    copies = []
-    for k, ref in enumerate(in_refs):
-        for layer, out_ref in enumerate(out_refs):
-            copies.append(pltpu.make_async_copy(ref.at[layer], out_ref.at[k], sem.at[len(copies)]))
+    in_refs, out_ref, sem = refs[:-2], refs[-2], refs[-1]
+    copies = [pltpu.make_async_copy(ref, out_ref.at[k], sem.at[k]) for k, ref in enumerate(in_refs)]
     for copy in copies:
         copy.start()
     for copy in copies:
@@ -196,13 +196,12 @@
 
 
 def pack_shards(fetched):
-    block = jax.ShapeDtypeStruct((len(fetched),) + fetched[0].shape[1:], BF)
     return pl.pallas_call(
         pack_kernel,
-        out_shape=[block] * 2,
+        out_shape=jax.ShapeDtypeStruct((len(fetched),) + fetched[0].shape, BF),
         in_specs=any_specs(len(fetched)),
-        out_specs=any_specs(2),
-        scratch_shapes=[pltpu.SemaphoreType.DMA((2 * len(fetched),))],
+        out_specs=pl.BlockSpec(memory_space=pl.ANY),
+        scratch_shapes=[pltpu.SemaphoreType.DMA((len(fetched),))],
         compiler_params=pltpu.CompilerParams(vmem_limit_bytes=4 * 1024 * 1024),
     )(*fetched)
 
@@ -407,21 +406,23 @@
     own = (qkv_weight.swapaxes(1, 2), proj_weight, up_weight, down_weight)
     ends = [0, 3 * head_width, 4 * head_width]
     ends = ends + [ends[-1] + up_weight.shape[2], ends[-1] + 2 * up_weight.shape[2]]
-    fetched = fetch_heads(weight_shards(own))
-    ending = send_quads(list(after(quads(cotangent), fetched[0])), 1)
+    shards = weight_shards(own)
+    early = fetch_heads(shards[0])
+    ending = send_quads(list(after(quads(cotangent), shards[0])), 1)
     edge = ((jnp.arange(lat_rows) < 3) & (lax.axis_index("lat") == 0)).astype(jnp.int32)
     region = jnp.broadcast_to((shift_labels * 2 + edge[:, None])[None, :, :, None], (level_count, 6, 12, 1))
     labels = quads(region)[::-1].reshape(-1)
     mask = (labels[:, None] == labels[None, :]).astype(F32)
     start = quads(inputs).reshape(tokens, model_width)
-    *fetched, start, mask, e0, e1, e2, e3 = lax.optimization_barrier((*fetched, start, mask, *ending))
+    *early, start, mask, e0, e1, e2, e3 = lax.optimization_barrier((*early, start, mask, *ending))
     ending = (e0, e1, e2, e3)
-    early_block, late_block = pack_shards(fetched)
-    early_ring = ring_x(early_block, 1)
-    late_ring = ring_x(late_block, -1, (early_ring[1::2], early_ring[2:3]))
-    early_all = early_ring + [swap_cores(piece) for piece in early_ring]
-    late_swaps = {s: swap_cores(late_ring[s]) for s in (0, len(late_ring) - 1)}
-    start = after(start, *late_swaps.values())
+    early_block = pack_shards(early)
+    early_ring = ring_far(ring_near(early_block), 1)
+    early_swaps = [swap_cores(early_block)]
+    late = fetch_heads(shards[1], early_swaps)
+    late = lax.optimization_barrier((*late, *early_ring[1:]))[:3]
+    late_near = ring_near(pack_shards(late))
+    early_all = early_ring + early_swaps + [swap_cores(piece) for piece in early_ring[1:]]
 
     width = head_width // HD * PARTS
     stream = jax.ShapeDtypeStruct((tokens, model_width), BF)
@@ -448,11 +449,10 @@
         compiler_params=PARAMS,
         cost_estimate=cost(1_800_000_000),
     )(start, *early_all, *own)
+    late_ring = ring_far(late_near, -1, quarters[0])
     quarters = send_quads(quarters, 1)
-    for s, piece in enumerate(late_ring):
-        if s not in late_swaps:
-            late_swaps[s] = swap_cores(after(piece, *quarters[1:]))
-    late_all = late_ring + [late_swaps[s] for s in range(len(late_ring))]
+    late_swaps = [swap_cores(piece if s == 2 else after(piece, *quarters[1:])) for s, piece in enumerate(late_ring)]
+    late_all = late_ring + late_swaps
     *pairs, late_sum = pl.pallas_call(
         partial(second_kernel, pieces, ends, factor),
         out_shape=[pair] * PARTS + [sums],

time: 209 us -> 189 us (0.904)
  waiting for transfers between devices: 61.4 us -> 24 us
  starting transfers between devices: 87.9 us -> 114 us
  local copies, waits for them, and re-layouts: 10.7 us -> 5.18 us
    ppermute x1 -> x2, waiting for transfers between devices: 27.3 us -> 0.01 us  [fetch_heads(): one = lax.ppermute(shard, ('lat', 'head'), odd(1))]
    ppermute x6, waiting for transfers between devices: 15.2 us -> 6.54 us  [along_x(): lax.ppermute(block, 'lat', [(i, i // ring * ring + (i + by) % ring) for i...]
    ppermute x9, starting transfers between devices: 20.9 us -> 27 us  [send_quads(): out.insert(1, lax.ppermute(pieces[q], ('lat', 'lon'), perm))]
    ppermute x1 -> x2, starting transfers between devices: 11.5 us -> 16.4 us  [fetch_heads(): three = lax.ppermute(shard, ('lat', 'head'), odd(2))]
    ppermute x1 -> x2, starting transfers between devices: 4.55 us -> 9.37 us  [fetch_heads(): one = lax.ppermute(shard, ('lat', 'head'), odd(1))]
    ppermute x1 -> x2, starting transfers between devices: 1.93 us -> 6.43 us  [fetch_heads(): two = lax.ppermute(shard, ('lat', 'head'), joint(sizes, even))]
    ppermute x6, starting transfers between devices: 16.5 us -> 20.7 us  [along_x(): lax.ppermute(block, 'lat', [(i, i // ring * ring + (i + by) % ring) for i...]
    unnamed x38 -> x20, local copies, waits for them, and re-layouts: 3.31 us -> 0.06 us
  transfers between devices with their start and end apart: 27 -> 30, of which waited for: 11 -> 8; matrix products, arithmetic and copies ran while one was open for 2% -> 1% of each run, Pallas kernels for 3% -> 3%
where the time goes in v3:
time: 189 us; the launch traced here: 188 us
  starting transfers between devices  114 us (60%)
  Pallas kernels  27.2 us (14%)
  waiting for transfers between devices  24 us (13%)
  blocking collectives  16.4 us (9%)
  local copies, waits for them, and re-layouts  5.18 us (3%)
    ppermute x9, starting transfers between devices, send_quads(): out.insert(1, lax.ppermute(pieces[q], ('lat', 'lon'), perm))  27 us
    ppermute x8, starting transfers between devices, swap_cores(): return lax.ppermute(piece, 'lon', [(i, i ^ 1) for i in range(size)])  23.4 us
    ppermute x6, starting transfers between devices, along_x(): lax.ppermute(block, 'lat', [(i, i // ring * ring + (i + by) % ring) for i...  20.7 us
    ppermute x2, starting transfers between devices, fetch_heads(): three = lax.ppermute(shard, ('lat', 'head'), odd(2))  16.4 us
    all_to_all x1, blocking collectives, scatter(): return jnp.sum(lax.all_to_all(parts, axis, 0, 0).astype(F32), axis=0)  16.4 us
    pallas_call x1, Pallas kernels, per_device(): pl.pallas_call(partial(second_kernel, pieces, ends, factor), out_shape=[p...  11.4 us
    all_to_all x1, starting transfers between devices, scatter(): return jnp.sum(lax.all_to_all(parts, axis, 0, 0).astype(F32), axis=0)  10.4 us
    ppermute x9, waiting for transfers between devices, send_quads(): out.insert(1, lax.ppermute(pieces[q], ('lat', 'lon'), perm))  9.45 us
  transfers between devices with their start and end apart: 30, of which 8 were waited for; matrix products, arithmetic and copies ran while one was open for 1% of the time, Pallas kernels for 3%

profile of v3, /device:TPU:1, one launch (start us, length us, event | category | flops | bytes accessed | tf_op | source)
XLA Modules:
  0.0 188.2 jit_solution(368209771991384781)
XLA Ops:
  0.6 1.9 %shard_map.102 = (bf16[128,768]{1,0:T(8,128)(2,1)}, bf16[128,768]{1,0:T(8,128)(2,1)}) custom-call(bf16[2,3,512,128]{3,2,1,0:T(8,128)(2,1)} %bitcast.36, bf16[2,512,128]{2,1,0:T(8,128)(2,1)} %refs_20_.3, bf16[2,512,512]{2,1,0:T(8,128)(2,1)} %refs_21_.1, bf16[2,512,512]{2,1,0:T(8,128)(2,1)} %refs_22_.1), custom_call_target="tpu_custom_call" | custom-call | tf_op jit(solution)/shard_map/pallas_call | solution.py:179
  2.6 11.5 %collective-permute-start.2 = (bf16[128,768]{1,0:T(8,128)(2,1)}, bf16[128,768]{1,0:T(8,128)(2,1)S(1)}, u32[]{:S(2)}, u32[]{:S(2)}) collective-permute-start(bf16[128,768]{1,0:T(8,128)(2,1)} %get-tuple-element.40), channel_id=1, source_target_pairs={{0,258},{1,259},{2,256},{3,257},{64,322},{65,323},{66,320},{67,321... | collective-permute-start | bytes 589832 | tf_op jit(solution)/shard_map/ppermute | solution.py:106
  16.0 4.6 %collective-permute-start = (bf16[128,768]{1,0:T(8,128)(2,1)}, bf16[128,768]{1,0:T(8,128)(2,1)S(1)}, u32[]{:S(2)}, u32[]{:S(2)}) collective-permute-start(bf16[128,768]{1,0:T(8,128)(2,1)} %get-tuple-element.40), channel_id=1, source_target_pairs={{0,259},{1,256},{2,257},{3,258},{64,323},{65,320},{66,321},{67,322... | collective-permute-start | bytes 589832 | tf_op jit(solution)/shard_map/ppermute | solution.py:108
  20.9 5.6 %collective-permute-start.5 = (bf16[36,512]{1,0:T(8,128)(2,1)S(1)}, bf16[36,512]{1,0:T(8,128)(2,1)S(1)}, u32[]{:S(2)}, u32[]{:S(2)}) collective-permute-start(bf16[36,512]{1,0:T(8,128)(2,1)S(1)} %get-tuple-element.76), channel_id=1, source_target_pairs={{0,68},{4,72},{8,76},{12,80},{16,84},{20,88},{24,92},{28,96},{32,1... | collective-permute-start | bytes 110600 | tf_op jit(solution)/shard_map/ppermute | solution.py:82
  26.5 3.1 %collective-permute-start.4 = (bf16[36,512]{1,0:T(8,128)(2,1)S(1)}, bf16[36,512]{1,0:T(8,128)(2,1)S(1)}, u32[]{:S(2)}, u32[]{:S(2)}) collective-permute-start(bf16[36,512]{1,0:T(8,128)(2,1)S(1)} %get-tuple-element.77), channel_id=1, source_target_pairs={{0,64},{4,68},{8,72},{12,76},{16,80},{20,84},{24,88},{28,92},{32,9... | collective-permute-start | bytes 110600 | tf_op jit(solution)/shard_map/ppermute | solution.py:82
  30.0 2.2 %collective-permute-start.3 = (bf16[36,512]{1,0:T(8,128)(2,1)S(1)}, bf16[36,512]{1,0:T(8,128)(2,1)S(1)}, u32[]{:S(2)}, u32[]{:S(2)}) collective-permute-start(bf16[36,512]{1,0:T(8,128)(2,1)S(1)} %get-tuple-element.78), channel_id=1, source_target_pairs={{0,4},{4,8},{8,12},{12,16},{16,20},{20,24},{24,28},{28,32},{32,36}... | collective-permute-start | bytes 110600 | tf_op jit(solution)/shard_map/ppermute | solution.py:82
  34.2 2.0 %collective-permute-start.6 = (bf16[3,128,768]{2,1,0:T(8,128)(2,1)S(1)}, bf16[3,128,768]{2,1,0:T(8,128)(2,1)S(1)}, u32[]{:S(2)}, u32[]{:S(2)}) collective-permute-start(bf16[3,128,768]{2,1,0:T(8,128)(2,1)S(1)} %shard_map.103.refs_1_.refs_11_), channel_id=1, source_target_pairs={{0,64},{64,128},{128,192},{192,0},{256,320},{320,384},{384,448},{4... | collective-permute-start | bytes 1769480 | tf_op jit(solution)/shard_map/ppermute | solution.py:119
  36.2 5.3 %collective-permute-start.9 = (bf16[3,128,768]{2,1,0:T(8,128)(2,1)S(1)}, bf16[3,128,768]{2,1,0:T(8,128)(2,1)S(1)}, u32[]{:S(2)}, u32[]{:S(2)}) collective-permute-start(bf16[3,128,768]{2,1,0:T(8,128)(2,1)S(1)} %shard_map.103.refs_1_.refs_11_), channel_id=1, source_target_pairs={{0,4},{4,0},{8,12},{12,8},{16,20},{20,16},{24,28},{28,24},{32,36},... | collective-permute-start | bytes 1769480 | tf_op jit(solution)/shard_map/ppermute | solution.py:114
  41.5 4.9 %collective-permute-start.8 = (bf16[3,128,768]{2,1,0:T(8,128)(2,1)S(1)}, bf16[3,128,768]{2,1,0:T(8,128)(2,1)S(1)}, u32[]{:S(2)}, u32[]{:S(2)}) collective-permute-start(bf16[3,128,768]{2,1,0:T(8,128)(2,1)S(1)} %shard_map.103.refs_1_.refs_11_), channel_id=1, source_target_pairs={{0,192},{64,0},{128,64},{192,128},{256,448},{320,256},{384,320},{4... | collective-permute-start | bytes 1769480 | tf_op jit(solution)/shard_map/ppermute | solution.py:119
  46.4 2.2 %collective-permute-done.6.refs_2_.refs_12_ = bf16[3,128,768]{2,1,0:T(8,128)(2,1)S(1)} collective-permute-done((bf16[3,128,768]{2,1,0:T(8,128)(2,1)S(1)}, bf16[3,128,768]{2,1,0:T(8,128)(2,1)S(1)}, u32[]{:S(2)}, u32[]{:S(2)}) %collective-permute-start.6) | collective-permute-done | bytes 589856 | tf_op jit(solution)/shard_map/ppermute | solution.py:119
  50.6 4.9 %collective-permute-start.18 = (bf16[128,768]{1,0:T(8,128)(2,1)S(1)}, bf16[128,768]{1,0:T(8,128)(2,1)S(1)}, u32[]{:S(2)}, u32[]{:S(2)}) collective-permute-start(bf16[128,768]{1,0:T(8,128)(2,1)S(1)} %copy-done.9), channel_id=1, source_target_pairs={{0,258},{1,259},{2,256},{3,257},{64,322},{65,323},{66,320},{67,321... | collective-permute-start | bytes 589832 | tf_op jit(solution)/shard_map/ppermute | solution.py:106
  55.5 4.5 %collective-permute-start.17 = (bf16[128,768]{1,0:T(8,128)(2,1)S(1)}, bf16[128,768]{1,0:T(8,128)(2,1)S(1)}, u32[]{:S(2)}, u32[]{:S(2)}) collective-permute-start(bf16[128,768]{1,0:T(8,128)(2,1)S(1)} %copy-done.9), channel_id=1, source_target_pairs={{0,3},{1,0},{2,1},{3,2},{64,67},{65,64},{66,65},{67,66},{128,131},... | collective-permute-start | bytes 589832 | tf_op jit(solution)/shard_map/ppermute | solution.py:107
  60.0 4.8 %collective-permute-start.16 = (bf16[128,768]{1,0:T(8,128)(2,1)S(1)}, bf16[128,768]{1,0:T(8,128)(2,1)S(1)}, u32[]{:S(2)}, u32[]{:S(2)}) collective-permute-start(bf16[128,768]{1,0:T(8,128)(2,1)S(1)} %copy-done.9), channel_id=1, source_target_pairs={{0,259},{1,256},{2,257},{3,258},{64,323},{65,320},{66,321},{67,322... | collective-permute-start | bytes 589832 | tf_op jit(solution)/shard_map/ppermute | solution.py:108
  64.8 4.9 %collective-permute-start.10 = (bf16[3,128,768]{2,1,0:T(8,128)(2,1)S(1)}, bf16[3,128,768]{2,1,0:T(8,128)(2,1)S(1)}, u32[]{:S(2)}, u32[]{:S(2)}) collective-permute-start(bf16[3,128,768]{2,1,0:T(8,128)(2,1)S(1)} %collective-permute-done.6.refs_2_.refs_12_), channel_id=1, source_target_pairs={{0,4},{4,0},{8,12},{12,8},{16,20},{20,16},{24,28},{28,24},{32,36},... | collective-permute-start | bytes 1769480 | tf_op jit(solution)/shard_map/ppermute | solution.py:114
  71.7 2.4 %collective-permute-start.11 = (bf16[3,128,768]{2,1,0:T(8,128)(2,1)S(1)}, bf16[3,128,768]{2,1,0:T(8,128)(2,1)S(1)}, u32[]{:S(2)}, u32[]{:S(2)}) collective-permute-start(bf16[3,128,768]{2,1,0:T(8,128)(2,1)S(1)} %collective-permute-done.7.refs_3_.refs_13_), channel_id=1, source_target_pairs={{0,4},{4,0},{8,12},{12,8},{16,20},{20,16},{24,28},{28,24},{32,36},... | collective-permute-start | bytes 1769480 | tf_op jit(solution)/shard_map/ppermute | solution.py:114
  74.9 4.8 %collective-permute-start.20 = (bf16[3,128,768]{2,1,0:T(8,128)(2,1)S(1)}, bf16[3,128,768]{2,1,0:T(8,128)(2,1)S(1)}, u32[]{:S(2)}, u32[]{:S(2)}) collective-permute-start(bf16[3,128,768]{2,1,0:T(8,128)(2,1)S(1)} %shard_map.105.refs_9_), channel_id=1, source_target_pairs={{0,192},{64,0},{128,64},{192,128},{256,448},{320,256},{384,320},{4... | collective-permute-start | bytes 1769480 | tf_op jit(solution)/shard_map/ppermute | solution.py:119
  81.7 5.5 %shard_map.104 = (bf16[36,512]{1,0:T(8,128)(2,1)S(1)}, bf16[36,512]{1,0:T(8,128)(2,1)S(1)}, bf16[36,512]{1,0:T(8,128)(2,1)S(1)}, bf16[36,512]{1,0:T(8,128)(2,1)S...) custom-call(bf16[144,512]{1,0:T(8,128)(2,1)S(1)} %reshape_reshape.6., ...), custom_call_target="tpu_custom_call" | custom-call | flops 1800000000 | bytes 8000000 | tf_op jit(solution)/shard_map/pallas_call | solution.py:443
  87.2 4.3 %collective-permute-done.20.refs_12_ = bf16[3,128,768]{2,1,0:T(8,128)(2,1)S(1)} collective-permute-done((bf16[3,128,768]{2,1,0:T(8,128)(2,1)S(1)}, bf16[3,128,768]{2,1,0:T(8,128)(2,1)S(1)}, u32[]{:S(2)}, u32[]{:S(2)}) %collective-permute-start.20) | collective-permute-done | bytes 589856 | tf_op jit(solution)/shard_map/ppermute | solution.py:119
  91.5 5.3 %collective-permute-start.21 = (bf16[3,128,768]{2,1,0:T(8,128)(2,1)S(1)}, bf16[3,128,768]{2,1,0:T(8,128)(2,1)S(1)}, u32[]{:S(2)}, u32[]{:S(2)}) collective-permute-start(bf16[3,128,768]{2,1,0:T(8,128)(2,1)S(1)} %collective-permute-done.20.refs_12_), channel_id=1, source_target_pairs={{0,192},{64,0},{128,64},{192,128},{256,448},{320,256},{384,320},{4... | collective-permute-start | bytes 1769480 | tf_op jit(solution)/shard_map/ppermute | solution.py:119
  96.8 4.6 %collective-permute-start.13 = (bf16[36,512]{1,0:T(8,128)(2,1)S(1)}, bf16[36,512]{1,0:T(8,128)(2,1)S(1)}, u32[]{:S(2)}, u32[]{:S(2)}) collective-permute-start(bf16[36,512]{1,0:T(8,128)(2,1)S(1)} %get-tuple-element.47), channel_id=1, source_target_pairs={{0,4},{4,8},{8,12},{12,16},{16,20},{20,24},{24,28},{28,32},{32,36}... | collective-permute-start | bytes 110600 | tf_op jit(solution)/shard_map/ppermute | solution.py:82
  105.2 3.0 %collective-permute-done.14.refs_2_ = bf16[36,512]{1,0:T(8,128)(2,1)S(1)} collective-permute-done((bf16[36,512]{1,0:T(8,128)(2,1)S(1)}, bf16[36,512]{1,0:T(8,128)(2,1)S(1)}, u32[]{:S(2)}, u32[]{:S(2)}) %collective-permute-start.14) | collective-permute-done | bytes 36896 | tf_op jit(solution)/shard_map/ppermute | solution.py:82
  108.2 2.5 %collective-permute-done.15.refs_3_ = bf16[36,512]{1,0:T(8,128)(2,1)S(1)} collective-permute-done((bf16[36,512]{1,0:T(8,128)(2,1)S(1)}, bf16[36,512]{1,0:T(8,128)(2,1)S(1)}, u32[]{:S(2)}, u32[]{:S(2)}) %collective-permute-start.15) | collective-permute-done | bytes 36896 | tf_op jit(solution)/shard_map/ppermute | solution.py:82
  112.7 2.4 %collective-permute-start.23 = (bf16[3,128,768]{2,1,0:T(8,128)(2,1)S(1)}, bf16[3,128,768]{2,1,0:T(8,128)(2,1)S(1)}, u32[]{:S(2)}, u32[]{:S(2)}) collective-permute-start(bf16[3,128,768]{2,1,0:T(8,128)(2,1)S(1)} %collective-permute-done.19.refs_10_), channel_id=1, source_target_pairs={{0,4},{4,0},{8,12},{12,8},{16,20},{20,16},{24,28},{28,24},{32,36},... | collective-permute-start | bytes 1769480 | tf_op jit(solution)/shard_map/ppermute | solution.py:114
  117.0 2.6 %collective-permute-start.24 = (bf16[3,128,768]{2,1,0:T(8,128)(2,1)S(1)}, bf16[3,128,768]{2,1,0:T(8,128)(2,1)S(1)}, u32[]{:S(2)}, u32[]{:S(2)}) collective-permute-start(bf16[3,128,768]{2,1,0:T(8,128)(2,1)S(1)} %collective-permute-done.21.refs_11_), channel_id=1, source_target_pairs={{0,4},{4,0},{8,12},{12,8},{16,20},{20,16},{24,28},{28,24},{32,36},... | collective-permute-start | bytes 1769480 | tf_op jit(solution)/shard_map/ppermute | solution.py:114
  121.0 11.4 %shard_map.106 = (bf16[2,36,512]{2,1,0:T(8,128)(2,1)S(1)}, bf16[2,36,512]{2,1,0:T(8,128)(2,1)S(1)}, bf16[2,36,512]{2,1,0:T(8,128)(2,1)S(1)}, bf16[2,36,512]{2,1,0:T(8,128)(2,1)S(1)}, bf16[512,512]{1,0:T(8,128)(2,1)S(1)}) custom-call(bf16[36,512]{1,0:T(8,128)(2,1)S(1)} %get-tuple-element.46.refs_0_, bf16[36,512]{1,0:T(8,128)(2,1)S(1)} %collective-permute-done.13.refs_1_, ...), custom_call_target="tpu_custom_call" | custom-call | flops 3800000000 | bytes 8000000 | tf_op jit(solution)/shard_map/pallas_call | solution.py:456
  132.8 3.6 %collective-permute-start.27 = (bf16[2,36,512]{2,1,0:T(8,128)(2,1)S(1)}, bf16[2,36,512]{2,1,0:T(8,128)(2,1)S(1)}, u32[]{:S(2)}, u32[]{:S(2)}) collective-permute-start(bf16[2,36,512]{2,1,0:T(8,128)(2,1)S(1)} %get-tuple-element.66), channel_id=1, source_target_pairs={{0,448},{4,452},{8,456},{12,460},{16,464},{20,468},{24,472},{28,47... | collective-permute-start | bytes 221192 | tf_op jit(solution)/shard_map/ppermute | solution.py:82
  136.5 3.6 %collective-permute-start.28 = (bf16[2,36,512]{2,1,0:T(8,128)(2,1)S(1)}, bf16[2,36,512]{2,1,0:T(8,128)(2,1)S(1)}, u32[]{:S(2)}, u32[]{:S(2)}) collective-permute-start(bf16[2,36,512]{2,1,0:T(8,128)(2,1)S(1)} %get-tuple-element.67), channel_id=1, source_target_pairs={{0,508},{4,448},{8,452},{12,456},{16,460},{20,464},{24,468},{28,47... | collective-permute-start | bytes 221192 | tf_op jit(solution)/shard_map/ppermute | solution.py:82
  140.2 3.0 %collective-permute-done.28.refs_3_ = bf16[2,36,512]{2,1,0:T(8,128)(2,1)S(1)} collective-permute-done((bf16[2,36,512]{2,1,0:T(8,128)(2,1)S(1)}, bf16[2,36,512]{2,1,0:T(8,128)(2,1)S(1)}, u32[]{:S(2)}, u32[]{:S(2)}) %collective-permute-start.28) | collective-permute-done | bytes 73760 | tf_op jit(solution)/shard_map/ppermute | solution.py:82
  143.2 6.8 %shard_map.107 = (bf16[144,512]{1,0:T(8,128)(2,1)S(1)}, bf16[8,2,64,512]{3,2,1,0:T(8,128)(2,1)S(1)}) custom-call(bf16[2,36,512]{2,1,0:T(8,128)(2,1)S(1)} %get-tuple-element.64.refs_0_, bf16[2,36,512]{2,1,0:T(8,128)(2,1)S(1)} %collective-permute-done.26.refs_1_, bf16[2,36,512]{2,1,0:T(8,128)(2,1)S(1)} %collective-permute-done.27.refs_2_, ...), custom_call_target="tpu_custom_call" | custom-call | flops 2000000000 | bytes 8000000 | tf_op jit(solution)/shard_map/pallas_call | solution.py:468
  150.0 16.4 %all_to_all.10 = bf16[8,128,512]{2,1,0:T(8,128)(2,1)S(1)} all-to-all(bf16[8,128,512]{2,1,0:T(8,128)(2,1)S(1)} %bitcast.40), channel_id=1, replica_groups=mesh['lat'=8,'lon'=16,'head'=4] {'lat'}, dimensions={0} | all-to-all | bytes 2097152 | tf_op jit(solution)/shard_map/all_to_all | solution.py:396
  167.4 10.4 %all-to-all-start.1 = ((bf16[16,8,512]{2,1,0:T(8,128)(2,1)}), bf16[16,8,512]{2,1,0:T(8,128)(2,1)S(1)}, u32[]{:S(2)}, u32[]{:S(2)}) async-start(bf16[16,8,512]{2,1,0:T(8,128)(2,1)} %copy.45), calls=%async_computation.1 | async-start | bytes 262144 | tf_op jit(solution)/shard_map/all_to_all | solution.py:396
  180.4 6.5 %all-to-all-done.1 = bf16[16,8,512]{2,1,0:T(8,128)(2,1)S(1)} async-done(((bf16[16,8,512]{2,1,0:T(8,128)(2,1)}), bf16[16,8,512]{2,1,0:T(8,128)(2,1)S(1)}, u32[]{:S(2)}, u32[]{:S(2)}) %all-to-all-start.1) | async-done | bytes 131104 | tf_op jit(solution)/shard_map/all_to_all | solution.py:396
  (90 shorter events, 25.2 us)
Async XLA Ops:
  2.6 30.8 %collective-permute-start.2 = (bf16[128,768]{1,0:T(8,128)(2,1)}, bf16[128,768]{1,0:T(8,128)(2,1)S(1)}, u32[]{:S(2)}, u32[]{:S(2)}) collective-permute-start(bf16[128,768]{1,0:T(8,128)(2,1)} %get-tuple-element.40), channel_id=1, source_target_pairs={{0,258},{1,259},{2,256},{3,257},{64,322},{65,323},{66,320},{67,321... | collective-permute-start | bytes 589832 | tf_op jit(solution)/shard_map/ppermute | solution.py:106
  14.1 19.3 %collective-permute-start.1 = (bf16[128,768]{1,0:T(8,128)(2,1)}, bf16[128,768]{1,0:T(8,128)(2,1)S(1)}, u32[]{:S(2)}, u32[]{:S(2)}) collective-permute-start(bf16[128,768]{1,0:T(8,128)(2,1)} %get-tuple-element.40), channel_id=1, source_target_pairs={{0,3},{1,0},{2,1},{3,2},{64,67},{65,64},{66,65},{67,66},{128,131},... | collective-permute-start | bytes 589832 | tf_op jit(solution)/shard_map/ppermute | solution.py:107
  16.0 17.4 %collective-permute-start = (bf16[128,768]{1,0:T(8,128)(2,1)}, bf16[128,768]{1,0:T(8,128)(2,1)S(1)}, u32[]{:S(2)}, u32[]{:S(2)}) collective-permute-start(bf16[128,768]{1,0:T(8,128)(2,1)} %get-tuple-element.40), channel_id=1, source_target_pairs={{0,259},{1,256},{2,257},{3,258},{64,323},{65,320},{66,321},{67,322... | collective-permute-start | bytes 589832 | tf_op jit(solution)/shard_map/ppermute | solution.py:108
  20.9 9.2 %collective-permute-start.5 = (bf16[36,512]{1,0:T(8,128)(2,1)S(1)}, bf16[36,512]{1,0:T(8,128)(2,1)S(1)}, u32[]{:S(2)}, u32[]{:S(2)}) collective-permute-start(bf16[36,512]{1,0:T(8,128)(2,1)S(1)} %get-tuple-element.76), channel_id=1, source_target_pairs={{0,68},{4,72},{8,76},{12,80},{16,84},{20,88},{24,92},{28,96},{32,1... | collective-permute-start | bytes 110600 | tf_op jit(solution)/shard_map/ppermute | solution.py:82
  26.5 6.9 %collective-permute-start.4 = (bf16[36,512]{1,0:T(8,128)(2,1)S(1)}, bf16[36,512]{1,0:T(8,128)(2,1)S(1)}, u32[]{:S(2)}, u32[]{:S(2)}) collective-permute-start(bf16[36,512]{1,0:T(8,128)(2,1)S(1)} %get-tuple-element.77), channel_id=1, source_target_pairs={{0,64},{4,68},{8,72},{12,76},{16,80},{20,84},{24,88},{28,92},{32,9... | collective-permute-start | bytes 110600 | tf_op jit(solution)/shard_map/ppermute | solution.py:82
  30.0 3.3 %collective-permute-start.3 = (bf16[36,512]{1,0:T(8,128)(2,1)S(1)}, bf16[36,512]{1,0:T(8,128)(2,1)S(1)}, u32[]{:S(2)}, u32[]{:S(2)}) collective-permute-start(bf16[36,512]{1,0:T(8,128)(2,1)S(1)} %get-tuple-element.78), channel_id=1, source_target_pairs={{0,4},{4,8},{8,12},{12,16},{16,20},{20,24},{24,28},{28,32},{32,36}... | collective-permute-start | bytes 110600 | tf_op jit(solution)/shard_map/ppermute | solution.py:82
  32.2 49.5 %copy-start.3 = (bf16[2,512,128]{2,1,0:T(8,128)(2,1)S(1)}, bf16[2,512,128]{2,1,0:T(8,128)(2,1)}, u32[]{:S(2)}) copy-start(bf16[2,512,128]{2,1,0:T(8,128)(2,1)} %refs_20_.3) | copy-start | bytes 786436
  32.3 49.4 %copy-start.2 = (bf16[2,512,3,128]{3,1,2,0:T(8,128)(2,1)S(1)}, bf16[2,512,3,128]{3,1,2,0:T(8,128)(2,1)}, u32[]{:S(2)}) copy-start(bf16[2,512,3,128]{3,1,2,0:T(8,128)(2,1)} %param.9) | copy-start | bytes 2359300
  34.2 14.4 %collective-permute-start.6 = (bf16[3,128,768]{2,1,0:T(8,128)(2,1)S(1)}, bf16[3,128,768]{2,1,0:T(8,128)(2,1)S(1)}, u32[]{:S(2)}, u32[]{:S(2)}) collective-permute-start(bf16[3,128,768]{2,1,0:T(8,128)(2,1)S(1)} %shard_map.103.refs_1_.refs_11_), channel_id=1, source_target_pairs={{0,64},{64,128},{128,192},{192,0},{256,320},{320,384},{384,448},{4... | collective-permute-start | bytes 1769480 | tf_op jit(solution)/shard_map/ppermute | solution.py:119
  36.2 14.3 %collective-permute-start.9 = (bf16[3,128,768]{2,1,0:T(8,128)(2,1)S(1)}, bf16[3,128,768]{2,1,0:T(8,128)(2,1)S(1)}, u32[]{:S(2)}, u32[]{:S(2)}) collective-permute-start(bf16[3,128,768]{2,1,0:T(8,128)(2,1)S(1)} %shard_map.103.refs_1_.refs_11_), channel_id=1, source_target_pairs={{0,4},{4,0},{8,12},{12,8},{16,20},{20,16},{24,28},{28,24},{32,36},... | collective-permute-start | bytes 1769480 | tf_op jit(solution)/shard_map/ppermute | solution.py:114
  41.5 23.3 %collective-permute-start.8 = (bf16[3,128,768]{2,1,0:T(8,128)(2,1)S(1)}, bf16[3,128,768]{2,1,0:T(8,128)(2,1)S(1)}, u32[]{:S(2)}, u32[]{:S(2)}) collective-permute-start(bf16[3,128,768]{2,1,0:T(8,128)(2,1)S(1)} %shard_map.103.refs_1_.refs_11_), channel_id=1, source_target_pairs={{0,192},{64,0},{128,64},{192,128},{256,448},{320,256},{384,320},{4... | collective-permute-start | bytes 1769480 | tf_op jit(solution)/shard_map/ppermute | solution.py:119
  48.6 23.1 %collective-permute-start.7 = (bf16[3,128,768]{2,1,0:T(8,128)(2,1)S(1)}, bf16[3,128,768]{2,1,0:T(8,128)(2,1)S(1)}, u32[]{:S(2)}, u32[]{:S(2)}) collective-permute-start(bf16[3,128,768]{2,1,0:T(8,128)(2,1)S(1)} %collective-permute-done.6.refs_2_.refs_12_), channel_id=1, source_target_pairs={{0,64},{64,128},{128,192},{192,0},{256,320},{320,384},{384,448},{4... | collective-permute-start | bytes 1769480 | tf_op jit(solution)/shard_map/ppermute | solution.py:119
  50.6 19.2 %collective-permute-start.18 = (bf16[128,768]{1,0:T(8,128)(2,1)S(1)}, bf16[128,768]{1,0:T(8,128)(2,1)S(1)}, u32[]{:S(2)}, u32[]{:S(2)}) collective-permute-start(bf16[128,768]{1,0:T(8,128)(2,1)S(1)} %copy-done.9), channel_id=1, source_target_pairs={{0,258},{1,259},{2,256},{3,257},{64,322},{65,323},{66,320},{67,321... | collective-permute-start | bytes 589832 | tf_op jit(solution)/shard_map/ppermute | solution.py:106
  55.5 18.6 %collective-permute-start.17 = (bf16[128,768]{1,0:T(8,128)(2,1)S(1)}, bf16[128,768]{1,0:T(8,128)(2,1)S(1)}, u32[]{:S(2)}, u32[]{:S(2)}) collective-permute-start(bf16[128,768]{1,0:T(8,128)(2,1)S(1)} %copy-done.9), channel_id=1, source_target_pairs={{0,3},{1,0},{2,1},{3,2},{64,67},{65,64},{66,65},{67,66},{128,131},... | collective-permute-start | bytes 589832 | tf_op jit(solution)/shard_map/ppermute | solution.py:107
  60.0 14.1 %collective-permute-start.16 = (bf16[128,768]{1,0:T(8,128)(2,1)S(1)}, bf16[128,768]{1,0:T(8,128)(2,1)S(1)}, u32[]{:S(2)}, u32[]{:S(2)}) collective-permute-start(bf16[128,768]{1,0:T(8,128)(2,1)S(1)} %copy-done.9), channel_id=1, source_target_pairs={{0,259},{1,256},{2,257},{3,258},{64,323},{65,320},{66,321},{67,322... | collective-permute-start | bytes 589832 | tf_op jit(solution)/shard_map/ppermute | solution.py:108
  64.8 16.8 %collective-permute-start.10 = (bf16[3,128,768]{2,1,0:T(8,128)(2,1)S(1)}, bf16[3,128,768]{2,1,0:T(8,128)(2,1)S(1)}, u32[]{:S(2)}, u32[]{:S(2)}) collective-permute-start(bf16[3,128,768]{2,1,0:T(8,128)(2,1)S(1)} %collective-permute-done.6.refs_2_.refs_12_), channel_id=1, source_target_pairs={{0,4},{4,0},{8,12},{12,8},{16,20},{20,16},{24,28},{28,24},{32,36},... | collective-permute-start | bytes 1769480 | tf_op jit(solution)/shard_map/ppermute | solution.py:114
  69.8 11.9 %collective-permute-start.12 = (bf16[3,128,768]{2,1,0:T(8,128)(2,1)S(1)}, bf16[3,128,768]{2,1,0:T(8,128)(2,1)S(1)}, u32[]{:S(2)}, u32[]{:S(2)}) collective-permute-start(bf16[3,128,768]{2,1,0:T(8,128)(2,1)S(1)} %collective-permute-done.8.refs_4_.refs_14_), channel_id=1, source_target_pairs={{0,4},{4,0},{8,12},{12,8},{16,20},{20,16},{24,28},{28,24},{32,36},... | collective-permute-start | bytes 1769480 | tf_op jit(solution)/shard_map/ppermute | solution.py:114
  71.7 9.9 %collective-permute-start.11 = (bf16[3,128,768]{2,1,0:T(8,128)(2,1)S(1)}, bf16[3,128,768]{2,1,0:T(8,128)(2,1)S(1)}, u32[]{:S(2)}, u32[]{:S(2)}) collective-permute-start(bf16[3,128,768]{2,1,0:T(8,128)(2,1)S(1)} %collective-permute-done.7.refs_3_.refs_13_), channel_id=1, source_target_pairs={{0,4},{4,0},{8,12},{12,8},{16,20},{20,16},{24,28},{28,24},{32,36},... | collective-permute-start | bytes 1769480 | tf_op jit(solution)/shard_map/ppermute | solution.py:114
  74.9 16.6 %collective-permute-start.20 = (bf16[3,128,768]{2,1,0:T(8,128)(2,1)S(1)}, bf16[3,128,768]{2,1,0:T(8,128)(2,1)S(1)}, u32[]{:S(2)}, u32[]{:S(2)}) collective-permute-start(bf16[3,128,768]{2,1,0:T(8,128)(2,1)S(1)} %shard_map.105.refs_9_), channel_id=1, source_target_pairs={{0,192},{64,0},{128,64},{192,128},{256,448},{320,256},{384,320},{4... | collective-permute-start | bytes 1769480 | tf_op jit(solution)/shard_map/ppermute | solution.py:119
  79.7 31.0 %collective-permute-start.19 = (bf16[3,128,768]{2,1,0:T(8,128)(2,1)S(1)}, bf16[3,128,768]{2,1,0:T(8,128)(2,1)S(1)}, u32[]{:S(2)}, u32[]{:S(2)}) collective-permute-start(bf16[3,128,768]{2,1,0:T(8,128)(2,1)S(1)} %shard_map.105.refs_9_), channel_id=1, source_target_pairs={{0,64},{64,128},{128,192},{192,0},{256,320},{320,384},{384,448},{4... | collective-permute-start | bytes 1769480 | tf_op jit(solution)/shard_map/ppermute | solution.py:119
  91.5 25.5 %collective-permute-start.21 = (bf16[3,128,768]{2,1,0:T(8,128)(2,1)S(1)}, bf16[3,128,768]{2,1,0:T(8,128)(2,1)S(1)}, u32[]{:S(2)}, u32[]{:S(2)}) collective-permute-start(bf16[3,128,768]{2,1,0:T(8,128)(2,1)S(1)} %collective-permute-done.20.refs_12_), channel_id=1, source_target_pairs={{0,192},{64,0},{128,64},{192,128},{256,448},{320,256},{384,320},{4... | collective-permute-start | bytes 1769480 | tf_op jit(solution)/shard_map/ppermute | solution.py:119
  96.8 8.4 %collective-permute-start.13 = (bf16[36,512]{1,0:T(8,128)(2,1)S(1)}, bf16[36,512]{1,0:T(8,128)(2,1)S(1)}, u32[]{:S(2)}, u32[]{:S(2)}) collective-permute-start(bf16[36,512]{1,0:T(8,128)(2,1)S(1)} %get-tuple-element.47), channel_id=1, source_target_pairs={{0,4},{4,8},{8,12},{12,16},{16,20},{20,24},{24,28},{28,32},{32,36}... | collective-permute-start | bytes 110600 | tf_op jit(solution)/shard_map/ppermute | solution.py:82
  101.4 6.8 %collective-permute-start.14 = (bf16[36,512]{1,0:T(8,128)(2,1)S(1)}, bf16[36,512]{1,0:T(8,128)(2,1)S(1)}, u32[]{:S(2)}, u32[]{:S(2)}) collective-permute-start(bf16[36,512]{1,0:T(8,128)(2,1)S(1)} %get-tuple-element.48), channel_id=1, source_target_pairs={{0,64},{4,68},{8,72},{12,76},{16,80},{20,84},{24,88},{28,92},{32,9... | collective-permute-start | bytes 110600 | tf_op jit(solution)/shard_map/ppermute | solution.py:82
  103.3 7.4 %collective-permute-start.15 = (bf16[36,512]{1,0:T(8,128)(2,1)S(1)}, bf16[36,512]{1,0:T(8,128)(2,1)S(1)}, u32[]{:S(2)}, u32[]{:S(2)}) collective-permute-start(bf16[36,512]{1,0:T(8,128)(2,1)S(1)} %get-tuple-element.49), channel_id=1, source_target_pairs={{0,68},{4,72},{8,76},{12,80},{16,84},{20,88},{24,92},{28,96},{32,1... | collective-permute-start | bytes 110600 | tf_op jit(solution)/shard_map/ppermute | solution.py:82
  110.7 8.9 %collective-permute-start.22 = (bf16[3,128,768]{2,1,0:T(8,128)(2,1)S(1)}, bf16[3,128,768]{2,1,0:T(8,128)(2,1)S(1)}, u32[]{:S(2)}, u32[]{:S(2)}) collective-permute-start(bf16[3,128,768]{2,1,0:T(8,128)(2,1)S(1)} %shard_map.105.refs_9_), channel_id=1, source_target_pairs={{0,4},{4,0},{8,12},{12,8},{16,20},{20,16},{24,28},{28,24},{32,36},... | collective-permute-start | bytes 1769480 | tf_op jit(solution)/shard_map/ppermute | solution.py:114
  112.7 7.0 %collective-permute-start.23 = (bf16[3,128,768]{2,1,0:T(8,128)(2,1)S(1)}, bf16[3,128,768]{2,1,0:T(8,128)(2,1)S(1)}, u32[]{:S(2)}, u32[]{:S(2)}) collective-permute-start(bf16[3,128,768]{2,1,0:T(8,128)(2,1)S(1)} %collective-permute-done.19.refs_10_), channel_id=1, source_target_pairs={{0,4},{4,0},{8,12},{12,8},{16,20},{20,16},{24,28},{28,24},{32,36},... | collective-permute-start | bytes 1769480 | tf_op jit(solution)/shard_map/ppermute | solution.py:114
  115.1 4.6 %collective-permute-start.25 = (bf16[3,128,768]{2,1,0:T(8,128)(2,1)S(1)}, bf16[3,128,768]{2,1,0:T(8,128)(2,1)S(1)}, u32[]{:S(2)}, u32[]{:S(2)}) collective-permute-start(bf16[3,128,768]{2,1,0:T(8,128)(2,1)S(1)} %collective-permute-done.20.refs_12_), channel_id=1, source_target_pairs={{0,4},{4,0},{8,12},{12,8},{16,20},{20,16},{24,28},{28,24},{32,36},... | collective-permute-start | bytes 1769480 | tf_op jit(solution)/shard_map/ppermute | solution.py:114
  117.0 4.0 %collective-permute-start.24 = (bf16[3,128,768]{2,1,0:T(8,128)(2,1)S(1)}, bf16[3,128,768]{2,1,0:T(8,128)(2,1)S(1)}, u32[]{:S(2)}, u32[]{:S(2)}) collective-permute-start(bf16[3,128,768]{2,1,0:T(8,128)(2,1)S(1)} %collective-permute-done.21.refs_11_), channel_id=1, source_target_pairs={{0,4},{4,0},{8,12},{12,8},{16,20},{20,16},{24,28},{28,24},{32,36},... | collective-permute-start | bytes 1769480 | tf_op jit(solution)/shard_map/ppermute | solution.py:114
  132.4 7.7 %collective-permute-start.26 = (bf16[2,36,512]{2,1,0:T(8,128)(2,1)S(1)}, bf16[2,36,512]{2,1,0:T(8,128)(2,1)S(1)}, u32[]{:S(2)}, u32[]{:S(2)}) collective-permute-start(bf16[2,36,512]{2,1,0:T(8,128)(2,1)S(1)} %get-tuple-element.65), channel_id=1, source_target_pairs={{0,60},{4,0},{8,4},{12,8},{16,12},{20,16},{24,20},{28,24},{32,28},... | collective-permute-start | bytes 221192 | tf_op jit(solution)/shard_map/ppermute | solution.py:82
  132.8 7.3 %collective-permute-start.27 = (bf16[2,36,512]{2,1,0:T(8,128)(2,1)S(1)}, bf16[2,36,512]{2,1,0:T(8,128)(2,1)S(1)}, u32[]{:S(2)}, u32[]{:S(2)}) collective-permute-start(bf16[2,36,512]{2,1,0:T(8,128)(2,1)S(1)} %get-tuple-element.66), channel_id=1, source_target_pairs={{0,448},{4,452},{8,456},{12,460},{16,464},{20,468},{24,472},{28,47... | collective-permute-start | bytes 221192 | tf_op jit(solution)/shard_map/ppermute | solution.py:82
  136.5 6.7 %collective-permute-start.28 = (bf16[2,36,512]{2,1,0:T(8,128)(2,1)S(1)}, bf16[2,36,512]{2,1,0:T(8,128)(2,1)S(1)}, u32[]{:S(2)}, u32[]{:S(2)}) collective-permute-start(bf16[2,36,512]{2,1,0:T(8,128)(2,1)S(1)} %get-tuple-element.67), channel_id=1, source_target_pairs={{0,508},{4,448},{8,452},{12,456},{16,460},{20,464},{24,468},{28,47... | collective-permute-start | bytes 221192 | tf_op jit(solution)/shard_map/ppermute | solution.py:82
  167.4 19.6 %all-to-all-start.1 = ((bf16[16,8,512]{2,1,0:T(8,128)(2,1)}), bf16[16,8,512]{2,1,0:T(8,128)(2,1)S(1)}, u32[]{:S(2)}, u32[]{:S(2)}) async-start(bf16[16,8,512]{2,1,0:T(8,128)(2,1)} %copy.45), calls=%async_computation.1 | async-start | bytes 262144 | tf_op jit(solution)/shard_map/all_to_all | solution.py:396
  (10 other events, 243.5 us)

commit v4 on v3

--- a/solution.py
+++ b/solution.py
@@ -103,9 +103,9 @@
     def even(a, h):
         return (a, h + (1 if a // ring else -1))
 
+    one = lax.ppermute(shard, ("lat", "head"), odd(1))
+    two = lax.ppermute(shard, ("lat", "head"), joint(sizes, even))
     three = lax.ppermute(shard, ("lat", "head"), odd(2))
-    two = lax.ppermute(shard, ("lat", "head"), joint(sizes, even))
-    one = lax.ppermute(shard, ("lat", "head"), odd(1))
     return one, two, three
 
 
@@ -119,11 +119,11 @@
     return lax.ppermute(block, "lat", [(i, i // ring * ring + (i + by) % ring) for i in range(size)])
 
 
-def ring_near(own):
+def ring_near(own, ahead=(), behind=()):
     ring = lat_parts()[1]
-    blocks = {0: own, 1 % ring: along_x(own, 1)}
+    blocks = {0: own, 1 % ring: along_x(after(own, *ahead), 1)}
     if ring > 2:
-        blocks[ring - 1] = along_x(own, -1)
+        blocks[ring - 1] = along_x(after(own, *behind), -1)
     return blocks
 
 
@@ -203,6 +203,7 @@
         out_specs=pl.BlockSpec(memory_space=pl.ANY),
         scratch_shapes=[pltpu.SemaphoreType.DMA((len(fetched),))],
         compiler_params=pltpu.CompilerParams(vmem_limit_bytes=4 * 1024 * 1024),
+        cost_estimate=pl.CostEstimate(flops=1_000_000, bytes_accessed=1_200_000, transcendentals=0),
     )(*fetched)
 
 
@@ -279,7 +280,18 @@
     return middle, (middle.astype(F32) + total).astype(BF)
 
 
-def backward(x, middle, gradient, weights, factor, packed_ref, probs_ref, mixed_ref, slope_ref, sums_ref):
+def core_halves(sums):
+    rows, columns = sums.shape
+    tiles = sums.reshape(rows // 16, 2, 8, columns)
+    even, odd = (
+        jnp.concatenate([tiles[:, 0, i : i + 4], tiles[:, 1, i : i + 4]], axis=1).reshape(rows // 2, columns)
+        for i in (0, 4)
+    )
+    here = lax.axis_index("lon") % 2 == 0
+    return jnp.where(here, even, odd).astype(BF), jnp.where(here, odd, even).astype(BF)
+
+
+def backward(x, middle, gradient, weights, factor, packed_ref, probs_ref, mixed_ref, slope_ref, put_sums):
     middle = middle.astype(F32)
     total = jnp.zeros(x.shape, F32)
     for k in range(PARTS):
@@ -307,15 +319,9 @@
         total += dot(d_packed, weights.qkv(k), 1, 1)
         if k == 0:
             normed = norm_rows(x).astype(BF)
-            first = (dot(normed, d_packed, 0, 0) * factor).astype(BF)
-            second = (dot(mid_grad, mixed_ref[...], 0, 0) * factor).astype(BF)
-            if len(sums_ref.shape) == 2:
-                sums_ref[:, : 3 * width] = first
-                sums_ref[:, 3 * width :] = second
-            else:
-                lats, _, rows, _ = sums_ref.shape
-                sums_ref[:, 0, :, : 3 * width] = first.reshape(lats, rows, 3 * width)
-                sums_ref[:, 0, :, 3 * width :] = second.reshape(lats, rows, width)
+            first = dot(normed, d_packed, 0, 0) * factor
+            second = dot(mid_grad, mixed_ref[...], 0, 0) * factor
+            put_sums(jnp.concatenate([first, second], axis=1))
     return (mid_grad.astype(F32) + norm_pull(x, total)).astype(BF)
 
 
@@ -337,7 +343,7 @@
     x_refs, grad_refs, refs = refs[:PARTS], refs[PARTS : 2 * PARTS], refs[2 * PARTS :]
     mask_ref, *refs = refs
     piece_refs, own_refs, refs = refs[:pieces], refs[pieces : pieces + 4], refs[pieces + 4 :]
-    out_refs, (sums_ref, w_ref, *saved), sem = refs[:PARTS], refs[PARTS:-1], refs[-1]
+    out_refs, (keep_ref, send_ref, w_ref, *saved), sem = refs[:PARTS], refs[PARTS:-1], refs[-1]
     copies = load_weights(1, piece_refs, own_refs, w_ref, sem)
     x = jnp.concatenate([ref[...].astype(F32) for ref in x_refs], axis=0)
     allowed = mask_ref[...] > 0
@@ -349,25 +355,35 @@
     for q in range(PARTS):
         out_refs[q][0] = out[q * rows : (q + 1) * rows]
     gradient = jnp.concatenate([ref[...].astype(F32) for ref in grad_refs], axis=0).astype(BF)
-    result = backward(x, middle, gradient, weights, factor, *saved, sums_ref)
+
+    def put_sums(value):
+        keep_ref[...], send_ref[...] = core_halves(value)
+
+    result = backward(x, middle, gradient, weights, factor, *saved, put_sums)
     for q in range(PARTS):
         out_refs[q][1] = result[q * rows : (q + 1) * rows]
 
 
 def third_kernel(pieces, ends, factor, *refs):
-    grad_refs, (late_ref, x_ref), refs = refs[:PARTS], refs[PARTS : PARTS + 2], refs[PARTS + 2 :]
+    grad_refs, (late_keep, late_send, x_ref), refs = refs[:PARTS], refs[PARTS : PARTS + 3], refs[PARTS + 3 :]
     (middle_ref, *saved), refs = refs[:5], refs[5:]
     piece_refs, own_refs, refs = refs[:pieces], refs[pieces : pieces + 4], refs[pieces + 4 :]
-    result_ref, sums_ref, w_ref, sem = refs
+    result_ref, keep_ref, send_ref, w_ref, sem = refs
     copies = load_weights(0, piece_refs, own_refs, w_ref, sem)
     gradient = jnp.concatenate([ref[1].astype(F32) for ref in grad_refs], axis=0).astype(BF)
-    lats, _, rows, columns = sums_ref.shape
-    sums_ref[:, 1] = late_ref[...].reshape(lats, rows, columns)
+    lats, _, rows, columns = keep_ref.shape
+    for late_ref, out_ref in ((late_keep, keep_ref), (late_send, send_ref)):
+        out_ref[:, 1] = late_ref[...].reshape(lats, rows, columns)
+
+    def put_sums(value):
+        for half, out_ref in zip(core_halves(value), (keep_ref, send_ref)):
+            out_ref[:, 0] = half.reshape(lats, rows, columns)
+
     for copy in copies:
         copy.wait()
     weights = Weights(w_ref, ends)
     result_ref[...] = backward(
-        x_ref[...].astype(F32), middle_ref[...], gradient, weights, factor, *saved, sums_ref
+        x_ref[...].astype(F32), middle_ref[...], gradient, weights, factor, *saved, put_sums
     )
 
 
@@ -390,10 +406,11 @@
     return pl.CostEstimate(flops=flops, bytes_accessed=8_000_000, transcendentals=600_000)
 
 
-def scatter(parts, axis):
-    size = lax.axis_size(axis)
+def scatter(parts, axis, groups=None):
+    size = lax.axis_size(axis) if groups is None else len(groups[0])
     parts = parts.reshape(size, -1, parts.shape[-1])
-    return jnp.sum(lax.all_to_all(parts, axis, 0, 0).astype(F32), axis=0)
+    parts = lax.all_to_all(parts, axis, 0, 0, axis_index_groups=groups)
+    return jnp.sum(parts.astype(F32), axis=0)
 
 
 def per_device(inputs, cotangent, qkv_weight, proj_weight, up_weight, down_weight, shift_labels):
@@ -417,18 +434,19 @@
     *early, start, mask, e0, e1, e2, e3 = lax.optimization_barrier((*early, start, mask, *ending))
     ending = (e0, e1, e2, e3)
     early_block = pack_shards(early)
-    early_ring = ring_far(ring_near(early_block), 1)
+    early_near = ring_near(early_block)
+    late = fetch_heads(shards[1], (early_block,))
+    early_ring = ring_far(early_near, 1, late[0])
     early_swaps = [swap_cores(early_block)]
-    late = fetch_heads(shards[1], early_swaps)
-    late = lax.optimization_barrier((*late, *early_ring[1:]))[:3]
-    late_near = ring_near(pack_shards(late))
+    late_block = pack_shards(late)
+    late_near = ring_near(late_block, early_ring[2:3], early_ring[1::2])
     early_all = early_ring + early_swaps + [swap_cores(piece) for piece in early_ring[1:]]
 
     width = head_width // HD * PARTS
     stream = jax.ShapeDtypeStruct((tokens, model_width), BF)
     piece = jax.ShapeDtypeStruct((quarter, model_width), BF)
     pair = jax.ShapeDtypeStruct((2, quarter, model_width), BF)
-    sums = jax.ShapeDtypeStruct((model_width, 4 * head_width), BF)
+    sums = jax.ShapeDtypeStruct((model_width // 2, 4 * head_width), BF)
     weight_space = pltpu.VMEM((PARTS, model_width, ends[-1]), BF)
     saved = [
         jax.ShapeDtypeStruct((PARTS, tokens, 3 * head_width), BF),
@@ -453,31 +471,33 @@
     quarters = send_quads(quarters, 1)
     late_swaps = [swap_cores(piece if s == 2 else after(piece, *quarters[1:])) for s, piece in enumerate(late_ring)]
     late_all = late_ring + late_swaps
-    *pairs, late_sum = pl.pallas_call(
+    *pairs, late_keep, late_send = pl.pallas_call(
         partial(second_kernel, pieces, ends, factor),
-        out_shape=[pair] * PARTS + [sums],
+        out_shape=[pair] * PARTS + [sums] * 2,
         in_specs=vmem_specs(2 * PARTS + 1) + any_specs(pieces) + hbm_specs(4),
-        out_specs=vmem_specs(PARTS + 1),
+        out_specs=vmem_specs(PARTS + 2),
         scratch_shapes=[weight_space] + [pltpu.VMEM(s.shape, s.dtype) for s in saved] + [semaphores],
         compiler_params=PARAMS,
         cost_estimate=cost(3_800_000_000),
     )(*quarters, *ending, mask, *late_all, *own)
     pairs = send_quads(pairs, -1)
     lats, lons = lax.axis_size("lat"), lax.axis_size("lon")
-    both = jax.ShapeDtypeStruct((lats, 2, model_width // lats, 4 * head_width), BF)
-    input_grad, total = pl.pallas_call(
+    both = jax.ShapeDtypeStruct((lats, 2, model_width // lats // 2, 4 * head_width), BF)
+    input_grad, keep, send = pl.pallas_call(
         partial(third_kernel, pieces, ends, factor),
-        out_shape=[stream, both],
-        in_specs=vmem_specs(PARTS + 7) + any_specs(pieces) + hbm_specs(4),
-        out_specs=vmem_specs(2),
+        out_shape=[stream, both, both],
+        in_specs=vmem_specs(PARTS + 8) + any_specs(pieces) + hbm_specs(4),
+        out_specs=vmem_specs(3),
         scratch_shapes=[weight_space, semaphores],
         compiler_params=PARAMS,
         cost_estimate=cost(2_000_000_000),
-    )(*pairs, late_sum, start, middle, packed, probs, mixed, slope, *early_all, *own)
+    )(*pairs, late_keep, late_send, start, middle, packed, probs, mixed, slope, *early_all, *own)
 
     layer_out = unquads(jnp.stack([p[0] for p in pairs]))
-    total = scatter(total, "lat").astype(BF).reshape(2, lons, -1, 4 * head_width).swapaxes(0, 1)
-    total = scatter(total, "lon").reshape(2, -1, 4 * head_width)
+    total = (keep.astype(F32) + swap_cores(send).astype(F32)).astype(BF)
+    total = scatter(total, "lat").astype(BF).reshape(2, lons // 2, -1, 4 * head_width).swapaxes(0, 1)
+    sides = [list(range(side, lons, 2)) for side in range(2)]
+    total = scatter(total, "lon", sides).reshape(2, -1, 4 * head_width)
     pack_sum = total[:, :, : 3 * head_width].reshape(2, -1, 3, head_width)
     proj_sum = total[:, :, 3 * head_width :]
     return layer_out, unquads(input_grad.reshape(PARTS, -1, model_width)), pack_sum, proj_sum

time: 189 us -> 188 us (level)
  blocking collectives: 16.4 us -> 0 us
  waiting for transfers between devices: 24 us -> 37.8 us
    all_to_all x1 -> x0, blocking collectives: 16.4 us -> none  [scatter(): return jnp.sum(lax.all_to_all(parts, axis, 0, 0).astype(F32), axis=0)]
    all_to_all x1 -> x2, waiting for transfers between devices: 6.55 us -> 13.8 us  [scatter(): parts = lax.all_to_all(parts, axis, 0, 0, axis_index_groups=groups)]
    ppermute x6, waiting for transfers between devices: 6.54 us -> 10 us  [along_x(): lax.ppermute(block, 'lat', [(i, i // ring * ring + (i + by) % ring) for i...]
    ppermute x8 -> x9, starting transfers between devices: 23.4 us -> 26.1 us  [swap_cores(): return lax.ppermute(piece, 'lon', [(i, i ^ 1) for i in range(size)])]
    all_to_all x1 -> x2, starting transfers between devices: 10.4 us -> 9.99 us  [scatter(): parts = lax.all_to_all(parts, axis, 0, 0, axis_index_groups=groups)]
  transfers between devices with their start and end apart: 30 -> 32, of which waited for: 8 -> 11; matrix products, arithmetic and copies ran while one was open for 1% -> 1% of each run, Pallas kernels for 3% -> 3%
where the time goes in v4:
time: 188 us; the launch traced here: 185 us
  starting transfers between devices  114 us (61%)
  waiting for transfers between devices  37.8 us (20%)
  Pallas kernels  27.2 us (14%)
  local copies, waits for them, and re-layouts  4.31 us (2%)
    ppermute x9, starting transfers between devices, send_quads(): out.insert(1, lax.ppermute(pieces[q], ('lat', 'lon'), perm))  27.3 us
    ppermute x9, starting transfers between devices, swap_cores(): return lax.ppermute(piece, 'lon', [(i, i ^ 1) for i in range(size)])  26.1 us
    ppermute x6, starting transfers between devices, along_x(): lax.ppermute(block, 'lat', [(i, i // ring * ring + (i + by) % ring) for i...  19.2 us
    ppermute x2, starting transfers between devices, fetch_heads(): three = lax.ppermute(shard, ('lat', 'head'), odd(2))  16.4 us
    all_to_all x2, waiting for transfers between devices, scatter(): parts = lax.all_to_all(parts, axis, 0, 0, axis_index_groups=groups)  13.8 us
    pallas_call x1, Pallas kernels, per_device(): pl.pallas_call(partial(second_kernel, pieces, ends, factor), out_shape=[p...  11.4 us
    ppermute x9, waiting for transfers between devices, send_quads(): out.insert(1, lax.ppermute(pieces[q], ('lat', 'lon'), perm))  10.1 us
    ppermute x6, waiting for transfers between devices, along_x(): lax.ppermute(block, 'lat', [(i, i // ring * ring + (i + by) % ring) for i...  10 us
  transfers between devices with their start and end apart: 32, of which 11 were waited for; matrix products, arithmetic and copies ran while one was open for 1% of the time, Pallas kernels for 3%

profile of v4, /device:TPU:1, one launch (start us, length us, event | category | flops | bytes accessed | tf_op | source)
XLA Modules:
  0.0 185.5 jit_solution(3909149331124385709)
XLA Ops:
  2.6 11.5 %collective-permute-start.2 = (bf16[128,768]{1,0:T(8,128)(2,1)}, bf16[128,768]{1,0:T(8,128)(2,1)S(1)}, u32[]{:S(2)}, u32[]{:S(2)}) collective-permute-start(bf16[128,768]{1,0:T(8,128)(2,1)} %get-tuple-element.42), channel_id=1, source_target_pairs={{0,258},{1,259},{2,256},{3,257},{64,322},{65,323},{66,320},{67,321... | collective-permute-start | bytes 589832 | tf_op jit(solution)/shard_map/ppermute | solution.py:108
  16.0 4.6 %collective-permute-start = (bf16[128,768]{1,0:T(8,128)(2,1)}, bf16[128,768]{1,0:T(8,128)(2,1)S(1)}, u32[]{:S(2)}, u32[]{:S(2)}) collective-permute-start(bf16[128,768]{1,0:T(8,128)(2,1)} %get-tuple-element.42), channel_id=1, source_target_pairs={{0,259},{1,256},{2,257},{3,258},{64,323},{65,320},{66,321},{67,322... | collective-permute-start | bytes 589832 | tf_op jit(solution)/shard_map/ppermute | solution.py:106
  20.9 5.6 %collective-permute-start.5 = (bf16[36,512]{1,0:T(8,128)(2,1)S(1)}, bf16[36,512]{1,0:T(8,128)(2,1)S(1)}, u32[]{:S(2)}, u32[]{:S(2)}) collective-permute-start(bf16[36,512]{1,0:T(8,128)(2,1)S(1)} %get-tuple-element.80), channel_id=1, source_target_pairs={{0,68},{4,72},{8,76},{12,80},{16,84},{20,88},{24,92},{28,96},{32,1... | collective-permute-start | bytes 110600 | tf_op jit(solution)/shard_map/ppermute | solution.py:82
  26.5 3.1 %collective-permute-start.4 = (bf16[36,512]{1,0:T(8,128)(2,1)S(1)}, bf16[36,512]{1,0:T(8,128)(2,1)S(1)}, u32[]{:S(2)}, u32[]{:S(2)}) collective-permute-start(bf16[36,512]{1,0:T(8,128)(2,1)S(1)} %get-tuple-element.81), channel_id=1, source_target_pairs={{0,64},{4,68},{8,72},{12,76},{16,80},{20,84},{24,88},{28,92},{32,9... | collective-permute-start | bytes 110600 | tf_op jit(solution)/shard_map/ppermute | solution.py:82
  30.0 2.2 %collective-permute-start.3 = (bf16[36,512]{1,0:T(8,128)(2,1)S(1)}, bf16[36,512]{1,0:T(8,128)(2,1)S(1)}, u32[]{:S(2)}, u32[]{:S(2)}) collective-permute-start(bf16[36,512]{1,0:T(8,128)(2,1)S(1)} %get-tuple-element.82), channel_id=1, source_target_pairs={{0,4},{4,8},{8,12},{12,16},{16,20},{20,24},{24,28},{28,32},{32,36}... | collective-permute-start | bytes 110600 | tf_op jit(solution)/shard_map/ppermute | solution.py:82
  36.2 3.5 %collective-permute-start.7 = (bf16[128,768]{1,0:T(8,128)(2,1)S(1)}, bf16[128,768]{1,0:T(8,128)(2,1)S(1)}, u32[]{:S(2)}, u32[]{:S(2)}) collective-permute-start(bf16[128,768]{1,0:T(8,128)(2,1)S(1)} %copy-done.10), channel_id=1, source_target_pairs={{0,259},{1,256},{2,257},{3,258},{64,323},{65,320},{66,321},{67,322... | collective-permute-start | bytes 589832 | tf_op jit(solution)/shard_map/ppermute | solution.py:106
  39.8 3.4 %collective-permute-start.9 = (bf16[3,128,768]{2,1,0:T(8,128)(2,1)S(1)}, bf16[3,128,768]{2,1,0:T(8,128)(2,1)S(1)}, u32[]{:S(2)}, u32[]{:S(2)}) collective-permute-start(bf16[3,128,768]{2,1,0:T(8,128)(2,1)S(1)} %shard_map.103.refs_1_.refs_12_), channel_id=1, source_target_pairs={{0,192},{64,0},{128,64},{192,128},{256,448},{320,256},{384,320},{4... | collective-permute-start | bytes 1769480 | tf_op jit(solution)/shard_map/ppermute | solution.py:119
  44.1 4.5 %collective-permute-done.6.refs_2_.refs_13_ = bf16[3,128,768]{2,1,0:T(8,128)(2,1)S(1)} collective-permute-done((bf16[3,128,768]{2,1,0:T(8,128)(2,1)S(1)}, bf16[3,128,768]{2,1,0:T(8,128)(2,1)S(1)}, u32[]{:S(2)}, u32[]{:S(2)}) %collective-permute-start.6) | collective-permute-done | bytes 589856 | tf_op jit(solution)/shard_map/ppermute | solution.py:119
  50.5 4.9 %collective-permute-start.18 = (bf16[128,768]{1,0:T(8,128)(2,1)S(1)}, bf16[128,768]{1,0:T(8,128)(2,1)S(1)}, u32[]{:S(2)}, u32[]{:S(2)}) collective-permute-start(bf16[128,768]{1,0:T(8,128)(2,1)S(1)} %copy-done.10), channel_id=1, source_target_pairs={{0,258},{1,259},{2,256},{3,257},{64,322},{65,323},{66,320},{67,321... | collective-permute-start | bytes 589832 | tf_op jit(solution)/shard_map/ppermute | solution.py:108
  55.5 4.5 %collective-permute-start.17 = (bf16[128,768]{1,0:T(8,128)(2,1)S(1)}, bf16[128,768]{1,0:T(8,128)(2,1)S(1)}, u32[]{:S(2)}, u32[]{:S(2)}) collective-permute-start(bf16[128,768]{1,0:T(8,128)(2,1)S(1)} %copy-done.10), channel_id=1, source_target_pairs={{0,3},{1,0},{2,1},{3,2},{64,67},{65,64},{66,65},{67,66},{128,131},... | collective-permute-start | bytes 589832 | tf_op jit(solution)/shard_map/ppermute | solution.py:107
  60.0 6.7 %collective-permute-start.10 = (bf16[3,128,768]{2,1,0:T(8,128)(2,1)S(1)}, bf16[3,128,768]{2,1,0:T(8,128)(2,1)S(1)}, u32[]{:S(2)}, u32[]{:S(2)}) collective-permute-start(bf16[3,128,768]{2,1,0:T(8,128)(2,1)S(1)} %shard_map.103.refs_1_.refs_12_), channel_id=1, source_target_pairs={{0,4},{4,0},{8,12},{12,8},{16,20},{20,16},{24,28},{28,24},{32,36},... | collective-permute-start | bytes 1769480 | tf_op jit(solution)/shard_map/ppermute | solution.py:114
  66.7 3.0 %collective-permute-start.11 = (bf16[3,128,768]{2,1,0:T(8,128)(2,1)S(1)}, bf16[3,128,768]{2,1,0:T(8,128)(2,1)S(1)}, u32[]{:S(2)}, u32[]{:S(2)}) collective-permute-start(bf16[3,128,768]{2,1,0:T(8,128)(2,1)S(1)} %collective-permute-done.6.refs_2_.refs_13_), channel_id=1, source_target_pairs={{0,4},{4,0},{8,12},{12,8},{16,20},{20,16},{24,28},{28,24},{32,36},... | collective-permute-start | bytes 1769480 | tf_op jit(solution)/shard_map/ppermute | solution.py:114
  71.6 2.4 %collective-permute-start.12 = (bf16[3,128,768]{2,1,0:T(8,128)(2,1)S(1)}, bf16[3,128,768]{2,1,0:T(8,128)(2,1)S(1)}, u32[]{:S(2)}, u32[]{:S(2)}) collective-permute-start(bf16[3,128,768]{2,1,0:T(8,128)(2,1)S(1)} %collective-permute-done.8.refs_3_.refs_14_), channel_id=1, source_target_pairs={{0,4},{4,0},{8,12},{12,8},{16,20},{20,16},{24,28},{28,24},{32,36},... | collective-permute-start | bytes 1769480 | tf_op jit(solution)/shard_map/ppermute | solution.py:114
  74.8 5.0 %collective-permute-start.20 = (bf16[3,128,768]{2,1,0:T(8,128)(2,1)S(1)}, bf16[3,128,768]{2,1,0:T(8,128)(2,1)S(1)}, u32[]{:S(2)}, u32[]{:S(2)}) collective-permute-start(bf16[3,128,768]{2,1,0:T(8,128)(2,1)S(1)} %shard_map.105.refs_9_), channel_id=1, source_target_pairs={{0,192},{64,0},{128,64},{192,128},{256,448},{320,256},{384,320},{4... | collective-permute-start | bytes 1769480 | tf_op jit(solution)/shard_map/ppermute | solution.py:119
  81.8 5.5 %shard_map.104 = (bf16[36,512]{1,0:T(8,128)(2,1)S(1)}, bf16[36,512]{1,0:T(8,128)(2,1)S(1)}, bf16[36,512]{1,0:T(8,128)(2,1)S(1)}, bf16[36,512]{1,0:T(8,128)(2,1)S...) custom-call(bf16[144,512]{1,0:T(8,128)(2,1)S(1)} %reshape_reshape.6., ...), custom_call_target="tpu_custom_call" | custom-call | flops 1800000000 | bytes 8000000 | tf_op jit(solution)/shard_map/pallas_call | solution.py:461
  87.3 5.5 %collective-permute-done.20.refs_12_ = bf16[3,128,768]{2,1,0:T(8,128)(2,1)S(1)} collective-permute-done((bf16[3,128,768]{2,1,0:T(8,128)(2,1)S(1)}, bf16[3,128,768]{2,1,0:T(8,128)(2,1)S(1)}, u32[]{:S(2)}, u32[]{:S(2)}) %collective-permute-start.20) | collective-permute-done | bytes 589856 | tf_op jit(solution)/shard_map/ppermute | solution.py:119
  92.8 5.0 %collective-permute-start.21 = (bf16[3,128,768]{2,1,0:T(8,128)(2,1)S(1)}, bf16[3,128,768]{2,1,0:T(8,128)(2,1)S(1)}, u32[]{:S(2)}, u32[]{:S(2)}) collective-permute-start(bf16[3,128,768]{2,1,0:T(8,128)(2,1)S(1)} %collective-permute-done.20.refs_12_), channel_id=1, source_target_pairs={{0,192},{64,0},{128,64},{192,128},{256,448},{320,256},{384,320},{4... | collective-permute-start | bytes 1769480 | tf_op jit(solution)/shard_map/ppermute | solution.py:119
  97.8 5.4 %collective-permute-start.14 = (bf16[36,512]{1,0:T(8,128)(2,1)S(1)}, bf16[36,512]{1,0:T(8,128)(2,1)S(1)}, u32[]{:S(2)}, u32[]{:S(2)}) collective-permute-start(bf16[36,512]{1,0:T(8,128)(2,1)S(1)} %get-tuple-element.52), channel_id=1, source_target_pairs={{0,4},{4,8},{8,12},{12,16},{16,20},{20,24},{24,28},{28,32},{32,36}... | collective-permute-start | bytes 110600 | tf_op jit(solution)/shard_map/ppermute | solution.py:82
  107.1 3.0 %collective-permute-done.15.refs_2_ = bf16[36,512]{1,0:T(8,128)(2,1)S(1)} collective-permute-done((bf16[36,512]{1,0:T(8,128)(2,1)S(1)}, bf16[36,512]{1,0:T(8,128)(2,1)S(1)}, u32[]{:S(2)}, u32[]{:S(2)}) %collective-permute-start.15) | collective-permute-done | bytes 36896 | tf_op jit(solution)/shard_map/ppermute | solution.py:82
  110.1 2.5 %collective-permute-done.16.refs_3_ = bf16[36,512]{1,0:T(8,128)(2,1)S(1)} collective-permute-done((bf16[36,512]{1,0:T(8,128)(2,1)S(1)}, bf16[36,512]{1,0:T(8,128)(2,1)S(1)}, u32[]{:S(2)}, u32[]{:S(2)}) %collective-permute-start.16) | collective-permute-done | bytes 36896 | tf_op jit(solution)/shard_map/ppermute | solution.py:82
  114.5 2.4 %collective-permute-start.23 = (bf16[3,128,768]{2,1,0:T(8,128)(2,1)S(1)}, bf16[3,128,768]{2,1,0:T(8,128)(2,1)S(1)}, u32[]{:S(2)}, u32[]{:S(2)}) collective-permute-start(bf16[3,128,768]{2,1,0:T(8,128)(2,1)S(1)} %collective-permute-done.19.refs_10_), channel_id=1, source_target_pairs={{0,4},{4,0},{8,12},{12,8},{16,20},{20,16},{24,28},{28,24},{32,36},... | collective-permute-start | bytes 1769480 | tf_op jit(solution)/shard_map/ppermute | solution.py:114
  118.9 2.6 %collective-permute-start.24 = (bf16[3,128,768]{2,1,0:T(8,128)(2,1)S(1)}, bf16[3,128,768]{2,1,0:T(8,128)(2,1)S(1)}, u32[]{:S(2)}, u32[]{:S(2)}) collective-permute-start(bf16[3,128,768]{2,1,0:T(8,128)(2,1)S(1)} %collective-permute-done.21.refs_11_), channel_id=1, source_target_pairs={{0,4},{4,0},{8,12},{12,8},{16,20},{20,16},{24,28},{28,24},{32,36},... | collective-permute-start | bytes 1769480 | tf_op jit(solution)/shard_map/ppermute | solution.py:114
  122.9 11.4 %shard_map.106 = (bf16[2,36,512]{2,1,0:T(8,128)(2,1)S(1)}, bf16[2,36,512]{2,1,0:T(8,128)(2,1)S(1)}, bf16[2,36,512]{2,1,0:T(8,128)(2,1)S(1)}, bf16[2,36,512]{2,1,...) custom-call(bf16[36,512]{1,0:T(8,128)(2,1)S(1)} %get-tuple-element.51.refs_0_, ...), custom_call_target="tpu_custom_call" | custom-call | flops 3800000000 | bytes 8000000 | tf_op jit(solution)/shard_map/pallas_call | solution.py:474
  134.7 3.6 %collective-permute-start.27 = (bf16[2,36,512]{2,1,0:T(8,128)(2,1)S(1)}, bf16[2,36,512]{2,1,0:T(8,128)(2,1)S(1)}, u32[]{:S(2)}, u32[]{:S(2)}) collective-permute-start(bf16[2,36,512]{2,1,0:T(8,128)(2,1)S(1)} %get-tuple-element.68), channel_id=1, source_target_pairs={{0,448},{4,452},{8,456},{12,460},{16,464},{20,468},{24,472},{28,47... | collective-permute-start | bytes 221192 | tf_op jit(solution)/shard_map/ppermute | solution.py:82
  138.4 3.1 %collective-permute-start.28 = (bf16[2,36,512]{2,1,0:T(8,128)(2,1)S(1)}, bf16[2,36,512]{2,1,0:T(8,128)(2,1)S(1)}, u32[]{:S(2)}, u32[]{:S(2)}) collective-permute-start(bf16[2,36,512]{2,1,0:T(8,128)(2,1)S(1)} %get-tuple-element.69), channel_id=1, source_target_pairs={{0,508},{4,448},{8,452},{12,456},{16,460},{20,464},{24,468},{28,47... | collective-permute-start | bytes 221192 | tf_op jit(solution)/shard_map/ppermute | solution.py:82
  141.5 3.6 %collective-permute-done.28.refs_3_ = bf16[2,36,512]{2,1,0:T(8,128)(2,1)S(1)} collective-permute-done((bf16[2,36,512]{2,1,0:T(8,128)(2,1)S(1)}, bf16[2,36,512]{2,1,0:T(8,128)(2,1)S(1)}, u32[]{:S(2)}, u32[]{:S(2)}) %collective-permute-start.28) | collective-permute-done | bytes 73760 | tf_op jit(solution)/shard_map/ppermute | solution.py:82
  145.1 6.8 %shard_map.107 = (bf16[144,512]{1,0:T(8,128)(2,1)S(1)}, bf16[8,2,32,512]{3,2,1,0:T(8,128)(2,1)S(1)}, bf16[8,2,32,512]{3,2,1,0:T(8,128)(2,1)S(1)}) custom-call(bf16[2,36,512]{2,1,0:T(8,128)(2,1)S(1)} %get-tuple-element.66.refs_0_, bf16[2,36,512]{2,1,0:T(8,128)(2,1)S(1)} %collective-permute-done.26.refs_1_, ...), custom_call_target="tpu_custom_call" | custom-call | flops 2000000000 | bytes 8000000 | tf_op jit(solution)/shard_map/pallas_call | solution.py:486
  152.0 3.3 %collective-permute-start.29 = (bf16[8,2,32,512]{3,2,1,0:T(8,128)(2,1)S(1)}, bf16[8,2,32,512]{3,2,1,0:T(8,128)(2,1)S(1)}, u32[]{:S(2)}, u32[]{:S(2)}) collective-permute-start(bf16[8,2,32,512]{3,2,1,0:T(8,128)(2,1)S(1)} %get-tuple-element.79), channel_id=1, source_target_pairs={{0,4},{4,0},{8,12},{12,8},{16,20},{20,16},{24,28},{28,24},{32,36},... | collective-permute-start | bytes 1572872 | tf_op jit(solution)/shard_map/ppermute | solution.py:114
  157.8 3.5 %all-to-all-start = ((bf16[8,64,512]{2,1,0:T(8,128)(2,1)}), bf16[8,64,512]{2,1,0:T(8,128)(2,1)S(1)}, u32[]{:S(2)}, u32[]{:S(2)}) async-start(bf16[8,64,512]{2,1,0:T(8,128)(2,1)} %bitcast.14), calls=%async_computation | async-start | bytes 1048576 | tf_op jit(solution)/shard_map/all_to_all | solution.py:412
  161.3 8.4 %all-to-all-done = bf16[8,64,512]{2,1,0:T(8,128)(2,1)S(1)} async-done(((bf16[8,64,512]{2,1,0:T(8,128)(2,1)}), bf16[8,64,512]{2,1,0:T(8,128)(2,1)S(1)}, u32[]{:S(2)}, u32[]{:S(2)}) %all-to-all-start) | async-done | bytes 524320 | tf_op jit(solution)/shard_map/all_to_all | solution.py:412
  170.5 6.5 %all-to-all-start.1 = ((bf16[8,8,512]{2,1,0:T(8,128)(2,1)}), bf16[8,8,512]{2,1,0:T(8,128)(2,1)S(1)}, u32[]{:S(2)}, u32[]{:S(2)}) async-start(bf16[8,8,512]{2,1,0:T(8,128)(2,1)} %copy.45), calls=%async_computation.1 | async-start | bytes 131072 | tf_op jit(solution)/shard_map/all_to_all | solution.py:412
  178.8 5.4 %all-to-all-done.1 = bf16[8,8,512]{2,1,0:T(8,128)(2,1)S(1)} async-done(((bf16[8,8,512]{2,1,0:T(8,128)(2,1)}), bf16[8,8,512]{2,1,0:T(8,128)(2,1)S(1)}, u32[]{:S(2)}, u32[]{:S(2)}) %all-to-all-start.1) | async-done | bytes 65568 | tf_op jit(solution)/shard_map/all_to_all | solution.py:412
  (97 shorter events, 31.7 us)
Async XLA Ops:
  2.6 30.8 %collective-permute-start.2 = (bf16[128,768]{1,0:T(8,128)(2,1)}, bf16[128,768]{1,0:T(8,128)(2,1)S(1)}, u32[]{:S(2)}, u32[]{:S(2)}) collective-permute-start(bf16[128,768]{1,0:T(8,128)(2,1)} %get-tuple-element.42), channel_id=1, source_target_pairs={{0,258},{1,259},{2,256},{3,257},{64,322},{65,323},{66,320},{67,321... | collective-permute-start | bytes 589832 | tf_op jit(solution)/shard_map/ppermute | solution.py:108
  14.1 19.3 %collective-permute-start.1 = (bf16[128,768]{1,0:T(8,128)(2,1)}, bf16[128,768]{1,0:T(8,128)(2,1)S(1)}, u32[]{:S(2)}, u32[]{:S(2)}) collective-permute-start(bf16[128,768]{1,0:T(8,128)(2,1)} %get-tuple-element.42), channel_id=1, source_target_pairs={{0,3},{1,0},{2,1},{3,2},{64,67},{65,64},{66,65},{67,66},{128,131},... | collective-permute-start | bytes 589832 | tf_op jit(solution)/shard_map/ppermute | solution.py:107
  16.0 17.4 %collective-permute-start = (bf16[128,768]{1,0:T(8,128)(2,1)}, bf16[128,768]{1,0:T(8,128)(2,1)S(1)}, u32[]{:S(2)}, u32[]{:S(2)}) collective-permute-start(bf16[128,768]{1,0:T(8,128)(2,1)} %get-tuple-element.42), channel_id=1, source_target_pairs={{0,259},{1,256},{2,257},{3,258},{64,323},{65,320},{66,321},{67,322... | collective-permute-start | bytes 589832 | tf_op jit(solution)/shard_map/ppermute | solution.py:106
  20.9 9.2 %collective-permute-start.5 = (bf16[36,512]{1,0:T(8,128)(2,1)S(1)}, bf16[36,512]{1,0:T(8,128)(2,1)S(1)}, u32[]{:S(2)}, u32[]{:S(2)}) collective-permute-start(bf16[36,512]{1,0:T(8,128)(2,1)S(1)} %get-tuple-element.80), channel_id=1, source_target_pairs={{0,68},{4,72},{8,76},{12,80},{16,84},{20,88},{24,92},{28,96},{32,1... | collective-permute-start | bytes 110600 | tf_op jit(solution)/shard_map/ppermute | solution.py:82
  26.5 6.9 %collective-permute-start.4 = (bf16[36,512]{1,0:T(8,128)(2,1)S(1)}, bf16[36,512]{1,0:T(8,128)(2,1)S(1)}, u32[]{:S(2)}, u32[]{:S(2)}) collective-permute-start(bf16[36,512]{1,0:T(8,128)(2,1)S(1)} %get-tuple-element.81), channel_id=1, source_target_pairs={{0,64},{4,68},{8,72},{12,76},{16,80},{20,84},{24,88},{28,92},{32,9... | collective-permute-start | bytes 110600 | tf_op jit(solution)/shard_map/ppermute | solution.py:82
  30.0 3.3 %collective-permute-start.3 = (bf16[36,512]{1,0:T(8,128)(2,1)S(1)}, bf16[36,512]{1,0:T(8,128)(2,1)S(1)}, u32[]{:S(2)}, u32[]{:S(2)}) collective-permute-start(bf16[36,512]{1,0:T(8,128)(2,1)S(1)} %get-tuple-element.82), channel_id=1, source_target_pairs={{0,4},{4,8},{8,12},{12,16},{16,20},{20,24},{24,28},{28,32},{32,36}... | collective-permute-start | bytes 110600 | tf_op jit(solution)/shard_map/ppermute | solution.py:82
  34.2 14.4 %collective-permute-start.6 = (bf16[3,128,768]{2,1,0:T(8,128)(2,1)S(1)}, bf16[3,128,768]{2,1,0:T(8,128)(2,1)S(1)}, u32[]{:S(2)}, u32[]{:S(2)}) collective-permute-start(bf16[3,128,768]{2,1,0:T(8,128)(2,1)S(1)} %shard_map.103.refs_1_.refs_12_), channel_id=1, source_target_pairs={{0,64},{64,128},{128,192},{192,0},{256,320},{320,384},{384,448},{4... | collective-permute-start | bytes 1769480 | tf_op jit(solution)/shard_map/ppermute | solution.py:119
  36.2 7.9 %collective-permute-start.7 = (bf16[128,768]{1,0:T(8,128)(2,1)S(1)}, bf16[128,768]{1,0:T(8,128)(2,1)S(1)}, u32[]{:S(2)}, u32[]{:S(2)}) collective-permute-start(bf16[128,768]{1,0:T(8,128)(2,1)S(1)} %copy-done.10), channel_id=1, source_target_pairs={{0,259},{1,256},{2,257},{3,258},{64,323},{65,320},{66,321},{67,322... | collective-permute-start | bytes 589832 | tf_op jit(solution)/shard_map/ppermute | solution.py:106
  39.8 29.9 %collective-permute-start.9 = (bf16[3,128,768]{2,1,0:T(8,128)(2,1)S(1)}, bf16[3,128,768]{2,1,0:T(8,128)(2,1)S(1)}, u32[]{:S(2)}, u32[]{:S(2)}) collective-permute-start(bf16[3,128,768]{2,1,0:T(8,128)(2,1)S(1)} %shard_map.103.refs_1_.refs_12_), channel_id=1, source_target_pairs={{0,192},{64,0},{128,64},{192,128},{256,448},{320,256},{384,320},{4... | collective-permute-start | bytes 1769480 | tf_op jit(solution)/shard_map/ppermute | solution.py:119
  48.6 23.0 %collective-permute-start.8 = (bf16[3,128,768]{2,1,0:T(8,128)(2,1)S(1)}, bf16[3,128,768]{2,1,0:T(8,128)(2,1)S(1)}, u32[]{:S(2)}, u32[]{:S(2)}) collective-permute-start(bf16[3,128,768]{2,1,0:T(8,128)(2,1)S(1)} %collective-permute-done.6.refs_2_.refs_13_), channel_id=1, source_target_pairs={{0,64},{64,128},{128,192},{192,0},{256,320},{320,384},{384,448},{4... | collective-permute-start | bytes 1769480 | tf_op jit(solution)/shard_map/ppermute | solution.py:119
  50.5 16.1 %collective-permute-start.18 = (bf16[128,768]{1,0:T(8,128)(2,1)S(1)}, bf16[128,768]{1,0:T(8,128)(2,1)S(1)}, u32[]{:S(2)}, u32[]{:S(2)}) collective-permute-start(bf16[128,768]{1,0:T(8,128)(2,1)S(1)} %copy-done.10), channel_id=1, source_target_pairs={{0,258},{1,259},{2,256},{3,257},{64,322},{65,323},{66,320},{67,321... | collective-permute-start | bytes 589832 | tf_op jit(solution)/shard_map/ppermute | solution.py:108
  55.5 18.5 %collective-permute-start.17 = (bf16[128,768]{1,0:T(8,128)(2,1)S(1)}, bf16[128,768]{1,0:T(8,128)(2,1)S(1)}, u32[]{:S(2)}, u32[]{:S(2)}) collective-permute-start(bf16[128,768]{1,0:T(8,128)(2,1)S(1)} %copy-done.10), channel_id=1, source_target_pairs={{0,3},{1,0},{2,1},{3,2},{64,67},{65,64},{66,65},{67,66},{128,131},... | collective-permute-start | bytes 589832 | tf_op jit(solution)/shard_map/ppermute | solution.py:107
  60.0 19.8 %collective-permute-start.10 = (bf16[3,128,768]{2,1,0:T(8,128)(2,1)S(1)}, bf16[3,128,768]{2,1,0:T(8,128)(2,1)S(1)}, u32[]{:S(2)}, u32[]{:S(2)}) collective-permute-start(bf16[3,128,768]{2,1,0:T(8,128)(2,1)S(1)} %shard_map.103.refs_1_.refs_12_), channel_id=1, source_target_pairs={{0,4},{4,0},{8,12},{12,8},{16,20},{20,16},{24,28},{28,24},{32,36},... | collective-permute-start | bytes 1769480 | tf_op jit(solution)/shard_map/ppermute | solution.py:114
  66.7 15.1 %collective-permute-start.11 = (bf16[3,128,768]{2,1,0:T(8,128)(2,1)S(1)}, bf16[3,128,768]{2,1,0:T(8,128)(2,1)S(1)}, u32[]{:S(2)}, u32[]{:S(2)}) collective-permute-start(bf16[3,128,768]{2,1,0:T(8,128)(2,1)S(1)} %collective-permute-done.6.refs_2_.refs_13_), channel_id=1, source_target_pairs={{0,4},{4,0},{8,12},{12,8},{16,20},{20,16},{24,28},{28,24},{32,36},... | collective-permute-start | bytes 1769480 | tf_op jit(solution)/shard_map/ppermute | solution.py:114
  69.7 12.1 %collective-permute-start.13 = (bf16[3,128,768]{2,1,0:T(8,128)(2,1)S(1)}, bf16[3,128,768]{2,1,0:T(8,128)(2,1)S(1)}, u32[]{:S(2)}, u32[]{:S(2)}) collective-permute-start(bf16[3,128,768]{2,1,0:T(8,128)(2,1)S(1)} %collective-permute-done.9.refs_4_.refs_15_), channel_id=1, source_target_pairs={{0,4},{4,0},{8,12},{12,8},{16,20},{20,16},{24,28},{28,24},{32,36},... | collective-permute-start | bytes 1769480 | tf_op jit(solution)/shard_map/ppermute | solution.py:114
  71.6 10.2 %collective-permute-start.12 = (bf16[3,128,768]{2,1,0:T(8,128)(2,1)S(1)}, bf16[3,128,768]{2,1,0:T(8,128)(2,1)S(1)}, u32[]{:S(2)}, u32[]{:S(2)}) collective-permute-start(bf16[3,128,768]{2,1,0:T(8,128)(2,1)S(1)} %collective-permute-done.8.refs_3_.refs_14_), channel_id=1, source_target_pairs={{0,4},{4,0},{8,12},{12,8},{16,20},{20,16},{24,28},{28,24},{32,36},... | collective-permute-start | bytes 1769480 | tf_op jit(solution)/shard_map/ppermute | solution.py:114
  74.8 18.0 %collective-permute-start.20 = (bf16[3,128,768]{2,1,0:T(8,128)(2,1)S(1)}, bf16[3,128,768]{2,1,0:T(8,128)(2,1)S(1)}, u32[]{:S(2)}, u32[]{:S(2)}) collective-permute-start(bf16[3,128,768]{2,1,0:T(8,128)(2,1)S(1)} %shard_map.105.refs_9_), channel_id=1, source_target_pairs={{0,192},{64,0},{128,64},{192,128},{256,448},{320,256},{384,320},{4... | collective-permute-start | bytes 1769480 | tf_op jit(solution)/shard_map/ppermute | solution.py:119
  79.8 32.8 %collective-permute-start.19 = (bf16[3,128,768]{2,1,0:T(8,128)(2,1)S(1)}, bf16[3,128,768]{2,1,0:T(8,128)(2,1)S(1)}, u32[]{:S(2)}, u32[]{:S(2)}) collective-permute-start(bf16[3,128,768]{2,1,0:T(8,128)(2,1)S(1)} %shard_map.105.refs_9_), channel_id=1, source_target_pairs={{0,64},{64,128},{128,192},{192,0},{256,320},{320,384},{384,448},{4... | collective-permute-start | bytes 1769480 | tf_op jit(solution)/shard_map/ppermute | solution.py:119
  92.8 26.1 %collective-permute-start.21 = (bf16[3,128,768]{2,1,0:T(8,128)(2,1)S(1)}, bf16[3,128,768]{2,1,0:T(8,128)(2,1)S(1)}, u32[]{:S(2)}, u32[]{:S(2)}) collective-permute-start(bf16[3,128,768]{2,1,0:T(8,128)(2,1)S(1)} %collective-permute-done.20.refs_12_), channel_id=1, source_target_pairs={{0,192},{64,0},{128,64},{192,128},{256,448},{320,256},{384,320},{4... | collective-permute-start | bytes 1769480 | tf_op jit(solution)/shard_map/ppermute | solution.py:119
  97.8 9.3 %collective-permute-start.14 = (bf16[36,512]{1,0:T(8,128)(2,1)S(1)}, bf16[36,512]{1,0:T(8,128)(2,1)S(1)}, u32[]{:S(2)}, u32[]{:S(2)}) collective-permute-start(bf16[36,512]{1,0:T(8,128)(2,1)S(1)} %get-tuple-element.52), channel_id=1, source_target_pairs={{0,4},{4,8},{8,12},{12,16},{16,20},{20,24},{24,28},{28,32},{32,36}... | collective-permute-start | bytes 110600 | tf_op jit(solution)/shard_map/ppermute | solution.py:82
  103.3 6.8 %collective-permute-start.15 = (bf16[36,512]{1,0:T(8,128)(2,1)S(1)}, bf16[36,512]{1,0:T(8,128)(2,1)S(1)}, u32[]{:S(2)}, u32[]{:S(2)}) collective-permute-start(bf16[36,512]{1,0:T(8,128)(2,1)S(1)} %get-tuple-element.53), channel_id=1, source_target_pairs={{0,64},{4,68},{8,72},{12,76},{16,80},{20,84},{24,88},{28,92},{32,9... | collective-permute-start | bytes 110600 | tf_op jit(solution)/shard_map/ppermute | solution.py:82
  105.2 7.4 %collective-permute-start.16 = (bf16[36,512]{1,0:T(8,128)(2,1)S(1)}, bf16[36,512]{1,0:T(8,128)(2,1)S(1)}, u32[]{:S(2)}, u32[]{:S(2)}) collective-permute-start(bf16[36,512]{1,0:T(8,128)(2,1)S(1)} %get-tuple-element.54), channel_id=1, source_target_pairs={{0,68},{4,72},{8,76},{12,80},{16,84},{20,88},{24,92},{28,96},{32,1... | collective-permute-start | bytes 110600 | tf_op jit(solution)/shard_map/ppermute | solution.py:82
  112.6 8.9 %collective-permute-start.22 = (bf16[3,128,768]{2,1,0:T(8,128)(2,1)S(1)}, bf16[3,128,768]{2,1,0:T(8,128)(2,1)S(1)}, u32[]{:S(2)}, u32[]{:S(2)}) collective-permute-start(bf16[3,128,768]{2,1,0:T(8,128)(2,1)S(1)} %shard_map.105.refs_9_), channel_id=1, source_target_pairs={{0,4},{4,0},{8,12},{12,8},{16,20},{20,16},{24,28},{28,24},{32,36},... | collective-permute-start | bytes 1769480 | tf_op jit(solution)/shard_map/ppermute | solution.py:114
  114.5 7.0 %collective-permute-start.23 = (bf16[3,128,768]{2,1,0:T(8,128)(2,1)S(1)}, bf16[3,128,768]{2,1,0:T(8,128)(2,1)S(1)}, u32[]{:S(2)}, u32[]{:S(2)}) collective-permute-start(bf16[3,128,768]{2,1,0:T(8,128)(2,1)S(1)} %collective-permute-done.19.refs_10_), channel_id=1, source_target_pairs={{0,4},{4,0},{8,12},{12,8},{16,20},{20,16},{24,28},{28,24},{32,36},... | collective-permute-start | bytes 1769480 | tf_op jit(solution)/shard_map/ppermute | solution.py:114
  117.0 4.6 %collective-permute-start.25 = (bf16[3,128,768]{2,1,0:T(8,128)(2,1)S(1)}, bf16[3,128,768]{2,1,0:T(8,128)(2,1)S(1)}, u32[]{:S(2)}, u32[]{:S(2)}) collective-permute-start(bf16[3,128,768]{2,1,0:T(8,128)(2,1)S(1)} %collective-permute-done.20.refs_12_), channel_id=1, source_target_pairs={{0,4},{4,0},{8,12},{12,8},{16,20},{20,16},{24,28},{28,24},{32,36},... | collective-permute-start | bytes 1769480 | tf_op jit(solution)/shard_map/ppermute | solution.py:114
  118.9 4.0 %collective-permute-start.24 = (bf16[3,128,768]{2,1,0:T(8,128)(2,1)S(1)}, bf16[3,128,768]{2,1,0:T(8,128)(2,1)S(1)}, u32[]{:S(2)}, u32[]{:S(2)}) collective-permute-start(bf16[3,128,768]{2,1,0:T(8,128)(2,1)S(1)} %collective-permute-done.21.refs_11_), channel_id=1, source_target_pairs={{0,4},{4,0},{8,12},{12,8},{16,20},{20,16},{24,28},{28,24},{32,36},... | collective-permute-start | bytes 1769480 | tf_op jit(solution)/shard_map/ppermute | solution.py:114
  134.3 7.1 %collective-permute-start.26 = (bf16[2,36,512]{2,1,0:T(8,128)(2,1)S(1)}, bf16[2,36,512]{2,1,0:T(8,128)(2,1)S(1)}, u32[]{:S(2)}, u32[]{:S(2)}) collective-permute-start(bf16[2,36,512]{2,1,0:T(8,128)(2,1)S(1)} %get-tuple-element.67), channel_id=1, source_target_pairs={{0,60},{4,0},{8,4},{12,8},{16,12},{20,16},{24,20},{28,24},{32,28},... | collective-permute-start | bytes 221192 | tf_op jit(solution)/shard_map/ppermute | solution.py:82
  134.7 6.8 %collective-permute-start.27 = (bf16[2,36,512]{2,1,0:T(8,128)(2,1)S(1)}, bf16[2,36,512]{2,1,0:T(8,128)(2,1)S(1)}, u32[]{:S(2)}, u32[]{:S(2)}) collective-permute-start(bf16[2,36,512]{2,1,0:T(8,128)(2,1)S(1)} %get-tuple-element.68), channel_id=1, source_target_pairs={{0,448},{4,452},{8,456},{12,460},{16,464},{20,468},{24,472},{28,47... | collective-permute-start | bytes 221192 | tf_op jit(solution)/shard_map/ppermute | solution.py:82
  138.4 6.8 %collective-permute-start.28 = (bf16[2,36,512]{2,1,0:T(8,128)(2,1)S(1)}, bf16[2,36,512]{2,1,0:T(8,128)(2,1)S(1)}, u32[]{:S(2)}, u32[]{:S(2)}) collective-permute-start(bf16[2,36,512]{2,1,0:T(8,128)(2,1)S(1)} %get-tuple-element.69), channel_id=1, source_target_pairs={{0,508},{4,448},{8,452},{12,456},{16,460},{20,464},{24,468},{28,47... | collective-permute-start | bytes 221192 | tf_op jit(solution)/shard_map/ppermute | solution.py:82
  152.0 4.8 %collective-permute-start.29 = (bf16[8,2,32,512]{3,2,1,0:T(8,128)(2,1)S(1)}, bf16[8,2,32,512]{3,2,1,0:T(8,128)(2,1)S(1)}, u32[]{:S(2)}, u32[]{:S(2)}) collective-permute-start(bf16[8,2,32,512]{3,2,1,0:T(8,128)(2,1)S(1)} %get-tuple-element.79), channel_id=1, source_target_pairs={{0,4},{4,0},{8,12},{12,8},{16,20},{20,16},{24,28},{28,24},{32,36},... | collective-permute-start | bytes 1572872 | tf_op jit(solution)/shard_map/ppermute | solution.py:114
  157.8 11.9 %all-to-all-start = ((bf16[8,64,512]{2,1,0:T(8,128)(2,1)}), bf16[8,64,512]{2,1,0:T(8,128)(2,1)S(1)}, u32[]{:S(2)}, u32[]{:S(2)}) async-start(bf16[8,64,512]{2,1,0:T(8,128)(2,1)} %bitcast.14), calls=%async_computation | async-start | bytes 1048576 | tf_op jit(solution)/shard_map/all_to_all | solution.py:412
  170.5 13.7 %all-to-all-start.1 = ((bf16[8,8,512]{2,1,0:T(8,128)(2,1)}), bf16[8,8,512]{2,1,0:T(8,128)(2,1)S(1)}, u32[]{:S(2)}, u32[]{:S(2)}) async-start(bf16[8,8,512]{2,1,0:T(8,128)(2,1)} %copy.45), calls=%async_computation.1 | async-start | bytes 131072 | tf_op jit(solution)/shard_map/all_to_all | solution.py:412
  (14 other events, 326.9 us)

commit v5 on v4

--- a/solution.py
+++ b/solution.py
@@ -103,9 +103,9 @@
     def even(a, h):
         return (a, h + (1 if a // ring else -1))
 
+    three = lax.ppermute(shard, ("lat", "head"), odd(2))
+    two = lax.ppermute(shard, ("lat", "head"), joint(sizes, even))
     one = lax.ppermute(shard, ("lat", "head"), odd(1))
-    two = lax.ppermute(shard, ("lat", "head"), joint(sizes, even))
-    three = lax.ppermute(shard, ("lat", "head"), odd(2))
     return one, two, three
 
 
@@ -425,6 +425,7 @@
     ends = ends + [ends[-1] + up_weight.shape[2], ends[-1] + 2 * up_weight.shape[2]]
     shards = weight_shards(own)
     early = fetch_heads(shards[0])
+    late = fetch_heads(shards[1])
     ending = send_quads(list(after(quads(cotangent), shards[0])), 1)
     edge = ((jnp.arange(lat_rows) < 3) & (lax.axis_index("lat") == 0)).astype(jnp.int32)
     region = jnp.broadcast_to((shift_labels * 2 + edge[:, None])[None, :, :, None], (level_count, 6, 12, 1))
@@ -435,12 +436,14 @@
     ending = (e0, e1, e2, e3)
     early_block = pack_shards(early)
     early_near = ring_near(early_block)
-    late = fetch_heads(shards[1], (early_block,))
-    early_ring = ring_far(early_near, 1, late[0])
-    early_swaps = [swap_cores(early_block)]
-    late_block = pack_shards(late)
-    late_near = ring_near(late_block, early_ring[2:3], early_ring[1::2])
-    early_all = early_ring + early_swaps + [swap_cores(piece) for piece in early_ring[1:]]
+    early_ring = ring_far(early_near, 1)
+    held = [piece if s in (0, 1, 2, 3) else after(piece, early_ring[2]) for s, piece in enumerate(early_ring)]
+    early_swaps = [swap_cores(piece) for piece in held]
+    early_all = early_ring + early_swaps
+    late_block = pack_shards(lax.optimization_barrier((*late, early_ring[1], early_ring[-1]))[:3])
+    late_near = ring_near(late_block, early_ring[2:3])
+    late_own = swap_cores(late_block)
+    start = after(start, late_own)
 
     width = head_width // HD * PARTS
     stream = jax.ShapeDtypeStruct((tokens, model_width), BF)
@@ -467,10 +470,9 @@
         compiler_params=PARAMS,
         cost_estimate=cost(1_800_000_000),
     )(start, *early_all, *own)
-    late_ring = ring_far(late_near, -1, quarters[0])
+    late_ring = ring_far(late_near, -1, late_own)
     quarters = send_quads(quarters, 1)
-    late_swaps = [swap_cores(piece if s == 2 else after(piece, *quarters[1:])) for s, piece in enumerate(late_ring)]
-    late_all = late_ring + late_swaps
+    late_all = late_ring + [late_own] + [swap_cores(after(p, *quarters[1:]) if s != 1 else p) for s, p in enumerate(late_ring[1:])]
     *pairs, late_keep, late_send = pl.pallas_call(
         partial(second_kernel, pieces, ends, factor),
         out_shape=[pair] * PARTS + [sums] * 2,

time: 188 us -> 182 us (0.968)
  starting transfers between devices: 114 us -> 110 us
  waiting for transfers between devices: 37.8 us -> 35.6 us
    ppermute x6, waiting for transfers between devices: 10 us -> 2.63 us  [along_x(): lax.ppermute(block, 'lat', [(i, i // ring * ring + (i + by) % ring) for i...]
    ppermute x2, waiting for transfers between devices: 0.99 us -> 5.91 us  [fetch_heads(): one = lax.ppermute(shard, ('lat', 'head'), odd(1))]
    ppermute x2, waiting for transfers between devices: 0.01 us -> 3.84 us  [fetch_heads(): two = lax.ppermute(shard, ('lat', 'head'), joint(sizes, even))]
    ppermute x9, waiting for transfers between devices: 10.1 us -> 6.36 us  [send_quads(): out.insert(1, lax.ppermute(pieces[q], ('lat', 'lon'), perm))]
    ppermute x9, starting transfers between devices: 27.3 us -> 24.7 us  [send_quads(): out.insert(1, lax.ppermute(pieces[q], ('lat', 'lon'), perm))]
  transfers between devices with their start and end apart: 32 -> 32, of which waited for: 11 -> 12; matrix products, arithmetic and copies ran while one was open for 1% -> 1% of each run, Pallas kernels for 3% -> 3%
where the time goes in v5:
time: 182 us; the launch traced here: 180 us
  starting transfers between devices  110 us (60%)
  waiting for transfers between devices  35.6 us (20%)
  Pallas kernels  27.2 us (15%)
  local copies, waits for them, and re-layouts  4.31 us (2%)
    ppermute x9, starting transfers between devices, swap_cores(): return lax.ppermute(piece, 'lon', [(i, i ^ 1) for i in range(size)])  27.6 us
    ppermute x9, starting transfers between devices, send_quads(): out.insert(1, lax.ppermute(pieces[q], ('lat', 'lon'), perm))  24.7 us
    ppermute x6, starting transfers between devices, along_x(): lax.ppermute(block, 'lat', [(i, i // ring * ring + (i + by) % ring) for i...  17.5 us
    ppermute x2, starting transfers between devices, fetch_heads(): three = lax.ppermute(shard, ('lat', 'head'), odd(2))  17 us
    all_to_all x2, waiting for transfers between devices, scatter(): parts = lax.all_to_all(parts, axis, 0, 0, axis_index_groups=groups)  13.6 us
    pallas_call x1, Pallas kernels, per_device(): pl.pallas_call(partial(second_kernel, pieces, ends, factor), out_shape=[p...  11.4 us
    all_to_all x2, starting transfers between devices, scatter(): parts = lax.all_to_all(parts, axis, 0, 0, axis_index_groups=groups)  9.5 us
    ppermute x2, starting transfers between devices, fetch_heads(): one = lax.ppermute(shard, ('lat', 'head'), odd(1))  8.42 us
  transfers between devices with their start and end apart: 32, of which 12 were waited for; matrix products, arithmetic and copies ran while one was open for 1% of the time, Pallas kernels for 3%

profile of v5, /device:TPU:1, one launch (start us, length us, event | category | flops | bytes accessed | tf_op | source)
XLA Modules:
  0.0 180.0 jit_solution(8228138654928697814)
XLA Ops:
  2.6 11.5 %collective-permute-start.2 = (bf16[128,768]{1,0:T(8,128)(2,1)}, bf16[128,768]{1,0:T(8,128)(2,1)S(1)}, u32[]{:S(2)}, u32[]{:S(2)}) collective-permute-start(bf16[128,768]{1,0:T(8,128)(2,1)} %get-tuple-element.42), channel_id=1, source_target_pairs={{0,258},{1,259},{2,256},{3,257},{64,322},{65,323},{66,320},{67,321... | collective-permute-start | bytes 589832 | tf_op jit(solution)/shard_map/ppermute | solution.py:106
  16.0 4.6 %collective-permute-start = (bf16[128,768]{1,0:T(8,128)(2,1)}, bf16[128,768]{1,0:T(8,128)(2,1)S(1)}, u32[]{:S(2)}, u32[]{:S(2)}) collective-permute-start(bf16[128,768]{1,0:T(8,128)(2,1)} %get-tuple-element.42), channel_id=1, source_target_pairs={{0,259},{1,256},{2,257},{3,258},{64,323},{65,320},{66,321},{67,322... | collective-permute-start | bytes 589832 | tf_op jit(solution)/shard_map/ppermute | solution.py:108
  20.9 5.6 %collective-permute-start.5 = (bf16[36,512]{1,0:T(8,128)(2,1)S(1)}, bf16[36,512]{1,0:T(8,128)(2,1)S(1)}, u32[]{:S(2)}, u32[]{:S(2)}) collective-permute-start(bf16[36,512]{1,0:T(8,128)(2,1)S(1)} %get-tuple-element.80), channel_id=1, source_target_pairs={{0,68},{4,72},{8,76},{12,80},{16,84},{20,88},{24,92},{28,96},{32,1... | collective-permute-start | bytes 110600 | tf_op jit(solution)/shard_map/ppermute | solution.py:82
  26.5 3.1 %collective-permute-start.4 = (bf16[36,512]{1,0:T(8,128)(2,1)S(1)}, bf16[36,512]{1,0:T(8,128)(2,1)S(1)}, u32[]{:S(2)}, u32[]{:S(2)}) collective-permute-start(bf16[36,512]{1,0:T(8,128)(2,1)S(1)} %get-tuple-element.81), channel_id=1, source_target_pairs={{0,64},{4,68},{8,72},{12,76},{16,80},{20,84},{24,88},{28,92},{32,9... | collective-permute-start | bytes 110600 | tf_op jit(solution)/shard_map/ppermute | solution.py:82
  30.0 2.2 %collective-permute-start.3 = (bf16[36,512]{1,0:T(8,128)(2,1)S(1)}, bf16[36,512]{1,0:T(8,128)(2,1)S(1)}, u32[]{:S(2)}, u32[]{:S(2)}) collective-permute-start(bf16[36,512]{1,0:T(8,128)(2,1)S(1)} %get-tuple-element.82), channel_id=1, source_target_pairs={{0,4},{4,8},{8,12},{12,16},{16,20},{20,24},{24,28},{28,32},{32,36}... | collective-permute-start | bytes 110600 | tf_op jit(solution)/shard_map/ppermute | solution.py:82
  34.2 3.3 %collective-permute-start.10 = (bf16[3,128,768]{2,1,0:T(8,128)(2,1)S(1)}, bf16[3,128,768]{2,1,0:T(8,128)(2,1)S(1)}, u32[]{:S(2)}, u32[]{:S(2)}) collective-permute-start(bf16[3,128,768]{2,1,0:T(8,128)(2,1)S(1)} %shard_map.103.refs_1_.refs_12_), channel_id=1, source_target_pairs={{0,192},{64,0},{128,64},{192,128},{256,448},{320,256},{384,320},{4... | collective-permute-start | bytes 1769480 | tf_op jit(solution)/shard_map/ppermute | solution.py:119
  39.5 5.5 %collective-permute-start.8 = (bf16[128,768]{1,0:T(8,128)(2,1)S(1)}, bf16[128,768]{1,0:T(8,128)(2,1)S(1)}, u32[]{:S(2)}, u32[]{:S(2)}) collective-permute-start(bf16[128,768]{1,0:T(8,128)(2,1)S(1)} %copy-done.10), channel_id=1, source_target_pairs={{0,258},{1,259},{2,256},{3,257},{64,322},{65,323},{66,320},{67,321... | collective-permute-start | bytes 589832 | tf_op jit(solution)/shard_map/ppermute | solution.py:106
  45.0 3.7 %collective-permute-start.7 = (bf16[128,768]{1,0:T(8,128)(2,1)S(1)}, bf16[128,768]{1,0:T(8,128)(2,1)S(1)}, u32[]{:S(2)}, u32[]{:S(2)}) collective-permute-start(bf16[128,768]{1,0:T(8,128)(2,1)S(1)} %copy-done.10), channel_id=1, source_target_pairs={{0,3},{1,0},{2,1},{3,2},{64,67},{65,64},{66,65},{67,66},{128,131},... | collective-permute-start | bytes 589832 | tf_op jit(solution)/shard_map/ppermute | solution.py:107
  48.7 3.9 %collective-permute-start.6 = (bf16[128,768]{1,0:T(8,128)(2,1)S(1)}, bf16[128,768]{1,0:T(8,128)(2,1)S(1)}, u32[]{:S(2)}, u32[]{:S(2)}) collective-permute-start(bf16[128,768]{1,0:T(8,128)(2,1)S(1)} %copy-done.10), channel_id=1, source_target_pairs={{0,259},{1,256},{2,257},{3,258},{64,323},{65,320},{66,321},{67,322... | collective-permute-start | bytes 589832 | tf_op jit(solution)/shard_map/ppermute | solution.py:108
  52.6 3.8 %collective-permute-done.7.refs_1_ = bf16[128,768]{1,0:T(8,128)(2,1)S(1)} collective-permute-done((bf16[128,768]{1,0:T(8,128)(2,1)S(1)}, bf16[128,768]{1,0:T(8,128)(2,1)S(1)}, u32[]{:S(2)}, u32[]{:S(2)}) %collective-permute-start.7) | collective-permute-done | bytes 196640 | tf_op jit(solution)/shard_map/ppermute | solution.py:107
  56.5 5.9 %collective-permute-done.6.refs_0_ = bf16[128,768]{1,0:T(8,128)(2,1)S(1)} collective-permute-done((bf16[128,768]{1,0:T(8,128)(2,1)S(1)}, bf16[128,768]{1,0:T(8,128)(2,1)S(1)}, u32[]{:S(2)}, u32[]{:S(2)}) %collective-permute-start.6) | collective-permute-done | bytes 196640 | tf_op jit(solution)/shard_map/ppermute | solution.py:108
  63.2 5.0 %collective-permute-start.21 = (bf16[3,128,768]{2,1,0:T(8,128)(2,1)S(1)}, bf16[3,128,768]{2,1,0:T(8,128)(2,1)S(1)}, u32[]{:S(2)}, u32[]{:S(2)}) collective-permute-start(bf16[3,128,768]{2,1,0:T(8,128)(2,1)S(1)} %shard_map.104.refs_9_), channel_id=1, source_target_pairs={{0,192},{64,0},{128,64},{192,128},{256,448},{320,256},{384,320},{4... | collective-permute-start | bytes 1769480 | tf_op jit(solution)/shard_map/ppermute | solution.py:119
  70.1 3.4 %collective-permute-start.11 = (bf16[3,128,768]{2,1,0:T(8,128)(2,1)S(1)}, bf16[3,128,768]{2,1,0:T(8,128)(2,1)S(1)}, u32[]{:S(2)}, u32[]{:S(2)}) collective-permute-start(bf16[3,128,768]{2,1,0:T(8,128)(2,1)S(1)} %shard_map.104.refs_9_), channel_id=1, source_target_pairs={{0,4},{4,0},{8,12},{12,8},{16,20},{20,16},{24,28},{28,24},{32,36},... | collective-permute-start | bytes 1769480 | tf_op jit(solution)/shard_map/ppermute | solution.py:114
  75.5 2.4 %collective-permute-start.16 = (bf16[3,128,768]{2,1,0:T(8,128)(2,1)S(1)}, bf16[3,128,768]{2,1,0:T(8,128)(2,1)S(1)}, u32[]{:S(2)}, u32[]{:S(2)}) collective-permute-start(bf16[3,128,768]{2,1,0:T(8,128)(2,1)S(1)} %collective-permute-done.10.refs_4_.refs_15_), channel_id=1, source_target_pairs={{0,4},{4,0},{8,12},{12,8},{16,20},{20,16},{24,28},{28,24},{32,36},... | collective-permute-start | bytes 1769480 | tf_op jit(solution)/shard_map/ppermute | solution.py:114
  79.5 4.1 %collective-permute-start.14 = (bf16[3,128,768]{2,1,0:T(8,128)(2,1)S(1)}, bf16[3,128,768]{2,1,0:T(8,128)(2,1)S(1)}, u32[]{:S(2)}, u32[]{:S(2)}) collective-permute-start(bf16[3,128,768]{2,1,0:T(8,128)(2,1)S(1)} %collective-permute-done.9.refs_2_.refs_13_), channel_id=1, source_target_pairs={{0,4},{4,0},{8,12},{12,8},{16,20},{20,16},{24,28},{28,24},{32,36},... | collective-permute-start | bytes 1769480 | tf_op jit(solution)/shard_map/ppermute | solution.py:114
  84.6 4.3 %collective-permute-start.15 = (bf16[3,128,768]{2,1,0:T(8,128)(2,1)S(1)}, bf16[3,128,768]{2,1,0:T(8,128)(2,1)S(1)}, u32[]{:S(2)}, u32[]{:S(2)}) collective-permute-start(bf16[3,128,768]{2,1,0:T(8,128)(2,1)S(1)} %collective-permute-done.12.refs_3_.refs_14_), channel_id=1, source_target_pairs={{0,4},{4,0},{8,12},{12,8},{16,20},{20,16},{24,28},{28,24},{32,36},... | collective-permute-start | bytes 1769480 | tf_op jit(solution)/shard_map/ppermute | solution.py:114
  90.9 3.4 %collective-permute-start.20 = (bf16[3,128,768]{2,1,0:T(8,128)(2,1)S(1)}, bf16[3,128,768]{2,1,0:T(8,128)(2,1)S(1)}, u32[]{:S(2)}, u32[]{:S(2)}) collective-permute-start(bf16[3,128,768]{2,1,0:T(8,128)(2,1)S(1)} %shard_map.104.refs_9_), channel_id=1, source_target_pairs={{0,64},{64,128},{128,192},{192,0},{256,320},{320,384},{384,448},{4... | collective-permute-start | bytes 1769480 | tf_op jit(solution)/shard_map/ppermute | solution.py:119
  94.3 5.5 %shard_map.105 = (bf16[36,512]{1,0:T(8,128)(2,1)S(1)}, bf16[36,512]{1,0:T(8,128)(2,1)S(1)}, bf16[36,512]{1,0:T(8,128)(2,1)S(1)}, bf16[36,512]{1,0:T(8,128)(2,1)S...) custom-call(bf16[144,512]{1,0:T(8,128)(2,1)S(1)} %reshape_reshape.6., ...), custom_call_target="tpu_custom_call" | custom-call | flops 1800000000 | bytes 8000000 | tf_op jit(solution)/shard_map/pallas_call | solution.py:464
  99.8 2.4 %collective-permute-start.17 = (bf16[36,512]{1,0:T(8,128)(2,1)S(1)}, bf16[36,512]{1,0:T(8,128)(2,1)S(1)}, u32[]{:S(2)}, u32[]{:S(2)}) collective-permute-start(bf16[36,512]{1,0:T(8,128)(2,1)S(1)} %get-tuple-element.54), channel_id=1, source_target_pairs={{0,4},{4,8},{8,12},{12,16},{16,20},{20,24},{24,28},{28,32},{32,36}... | collective-permute-start | bytes 110600 | tf_op jit(solution)/shard_map/ppermute | solution.py:82
  106.1 2.4 %collective-permute-start.24 = (bf16[3,128,768]{2,1,0:T(8,128)(2,1)S(1)}, bf16[3,128,768]{2,1,0:T(8,128)(2,1)S(1)}, u32[]{:S(2)}, u32[]{:S(2)}) collective-permute-start(bf16[3,128,768]{2,1,0:T(8,128)(2,1)S(1)} %collective-permute-done.22.refs_11_), channel_id=1, source_target_pairs={{0,4},{4,0},{8,12},{12,8},{16,20},{20,16},{24,28},{28,24},{32,36},... | collective-permute-start | bytes 1769480 | tf_op jit(solution)/shard_map/ppermute | solution.py:114
  109.1 2.7 %collective-permute-done.19.refs_3_ = bf16[36,512]{1,0:T(8,128)(2,1)S(1)} collective-permute-done((bf16[36,512]{1,0:T(8,128)(2,1)S(1)}, bf16[36,512]{1,0:T(8,128)(2,1)S(1)}, u32[]{:S(2)}, u32[]{:S(2)}) %collective-permute-start.19) | collective-permute-done | bytes 36896 | tf_op jit(solution)/shard_map/ppermute | solution.py:82
  111.9 2.9 %collective-permute-start.23 = (bf16[3,128,768]{2,1,0:T(8,128)(2,1)S(1)}, bf16[3,128,768]{2,1,0:T(8,128)(2,1)S(1)}, u32[]{:S(2)}, u32[]{:S(2)}) collective-permute-start(bf16[3,128,768]{2,1,0:T(8,128)(2,1)S(1)} %collective-permute-done.20.refs_10_), channel_id=1, source_target_pairs={{0,4},{4,0},{8,12},{12,8},{16,20},{20,16},{24,28},{28,24},{32,36},... | collective-permute-start | bytes 1769480 | tf_op jit(solution)/shard_map/ppermute | solution.py:114
  114.8 2.1 %collective-permute-start.25 = (bf16[3,128,768]{2,1,0:T(8,128)(2,1)S(1)}, bf16[3,128,768]{2,1,0:T(8,128)(2,1)S(1)}, u32[]{:S(2)}, u32[]{:S(2)}) collective-permute-start(bf16[3,128,768]{2,1,0:T(8,128)(2,1)S(1)} %collective-permute-done.21.refs_12_), channel_id=1, source_target_pairs={{0,4},{4,0},{8,12},{12,8},{16,20},{20,16},{24,28},{28,24},{32,36},... | collective-permute-start | bytes 1769480 | tf_op jit(solution)/shard_map/ppermute | solution.py:114
  118.7 11.4 %shard_map.106 = (bf16[2,36,512]{2,1,0:T(8,128)(2,1)S(1)}, bf16[2,36,512]{2,1,0:T(8,128)(2,1)S(1)}, bf16[2,36,512]{2,1,0:T(8,128)(2,1)S(1)}, bf16[2,36,512]{2,1,...) custom-call(bf16[36,512]{1,0:T(8,128)(2,1)S(1)} %get-tuple-element.53.refs_0_, ...), custom_call_target="tpu_custom_call" | custom-call | flops 3800000000 | bytes 8000000 | tf_op jit(solution)/shard_map/pallas_call | solution.py:476
  130.2 2.8 %collective-permute-start.27 = (bf16[2,36,512]{2,1,0:T(8,128)(2,1)S(1)}, bf16[2,36,512]{2,1,0:T(8,128)(2,1)S(1)}, u32[]{:S(2)}, u32[]{:S(2)}) collective-permute-start(bf16[2,36,512]{2,1,0:T(8,128)(2,1)S(1)} %get-tuple-element.68), channel_id=1, source_target_pairs={{0,448},{4,452},{8,456},{12,460},{16,464},{20,468},{24,472},{28,47... | collective-permute-start | bytes 221192 | tf_op jit(solution)/shard_map/ppermute | solution.py:82
  133.0 4.6 %collective-permute-start.28 = (bf16[2,36,512]{2,1,0:T(8,128)(2,1)S(1)}, bf16[2,36,512]{2,1,0:T(8,128)(2,1)S(1)}, u32[]{:S(2)}, u32[]{:S(2)}) collective-permute-start(bf16[2,36,512]{2,1,0:T(8,128)(2,1)S(1)} %get-tuple-element.69), channel_id=1, source_target_pairs={{0,508},{4,448},{8,452},{12,456},{16,460},{20,464},{24,468},{28,47... | collective-permute-start | bytes 221192 | tf_op jit(solution)/shard_map/ppermute | solution.py:82
  139.6 6.8 %shard_map.107 = (bf16[144,512]{1,0:T(8,128)(2,1)S(1)}, bf16[8,2,32,512]{3,2,1,0:T(8,128)(2,1)S(1)}, bf16[8,2,32,512]{3,2,1,0:T(8,128)(2,1)S(1)}) custom-call(bf16[2,36,512]{2,1,0:T(8,128)(2,1)S(1)} %get-tuple-element.66.refs_0_, bf16[2,36,512]{2,1,0:T(8,128)(2,1)S(1)} %collective-permute-done.26.refs_1_, ...), custom_call_target="tpu_custom_call" | custom-call | flops 2000000000 | bytes 8000000 | tf_op jit(solution)/shard_map/pallas_call | solution.py:488
  146.5 4.1 %collective-permute-start.29 = (bf16[8,2,32,512]{3,2,1,0:T(8,128)(2,1)S(1)}, bf16[8,2,32,512]{3,2,1,0:T(8,128)(2,1)S(1)}, u32[]{:S(2)}, u32[]{:S(2)}) collective-permute-start(bf16[8,2,32,512]{3,2,1,0:T(8,128)(2,1)S(1)} %get-tuple-element.79), channel_id=1, source_target_pairs={{0,4},{4,0},{8,12},{12,8},{16,20},{20,16},{24,28},{28,24},{32,36},... | collective-permute-start | bytes 1572872 | tf_op jit(solution)/shard_map/ppermute | solution.py:114
  153.0 3.5 %all-to-all-start = ((bf16[8,64,512]{2,1,0:T(8,128)(2,1)}), bf16[8,64,512]{2,1,0:T(8,128)(2,1)S(1)}, u32[]{:S(2)}, u32[]{:S(2)}) async-start(bf16[8,64,512]{2,1,0:T(8,128)(2,1)} %bitcast.14), calls=%async_computation | async-start | bytes 1048576 | tf_op jit(solution)/shard_map/all_to_all | solution.py:412
  156.6 8.2 %all-to-all-done = bf16[8,64,512]{2,1,0:T(8,128)(2,1)S(1)} async-done(((bf16[8,64,512]{2,1,0:T(8,128)(2,1)}), bf16[8,64,512]{2,1,0:T(8,128)(2,1)S(1)}, u32[]{:S(2)}, u32[]{:S(2)}) %all-to-all-start) | async-done | bytes 524320 | tf_op jit(solution)/shard_map/all_to_all | solution.py:412
  165.6 6.0 %all-to-all-start.1 = ((bf16[8,8,512]{2,1,0:T(8,128)(2,1)}), bf16[8,8,512]{2,1,0:T(8,128)(2,1)S(1)}, u32[]{:S(2)}, u32[]{:S(2)}) async-start(bf16[8,8,512]{2,1,0:T(8,128)(2,1)} %copy.45), calls=%async_computation.1 | async-start | bytes 131072 | tf_op jit(solution)/shard_map/all_to_all | solution.py:412
  173.3 5.4 %all-to-all-done.1 = bf16[8,8,512]{2,1,0:T(8,128)(2,1)S(1)} async-done(((bf16[8,8,512]{2,1,0:T(8,128)(2,1)}), bf16[8,8,512]{2,1,0:T(8,128)(2,1)S(1)}, u32[]{:S(2)}, u32[]{:S(2)}) %all-to-all-start.1) | async-done | bytes 65568 | tf_op jit(solution)/shard_map/all_to_all | solution.py:412
  (97 shorter events, 32.3 us)
Async XLA Ops:
  2.6 30.8 %collective-permute-start.2 = (bf16[128,768]{1,0:T(8,128)(2,1)}, bf16[128,768]{1,0:T(8,128)(2,1)S(1)}, u32[]{:S(2)}, u32[]{:S(2)}) collective-permute-start(bf16[128,768]{1,0:T(8,128)(2,1)} %get-tuple-element.42), channel_id=1, source_target_pairs={{0,258},{1,259},{2,256},{3,257},{64,322},{65,323},{66,320},{67,321... | collective-permute-start | bytes 589832 | tf_op jit(solution)/shard_map/ppermute | solution.py:106
  14.1 19.3 %collective-permute-start.1 = (bf16[128,768]{1,0:T(8,128)(2,1)}, bf16[128,768]{1,0:T(8,128)(2,1)S(1)}, u32[]{:S(2)}, u32[]{:S(2)}) collective-permute-start(bf16[128,768]{1,0:T(8,128)(2,1)} %get-tuple-element.42), channel_id=1, source_target_pairs={{0,3},{1,0},{2,1},{3,2},{64,67},{65,64},{66,65},{67,66},{128,131},... | collective-permute-start | bytes 589832 | tf_op jit(solution)/shard_map/ppermute | solution.py:107
  16.0 17.4 %collective-permute-start = (bf16[128,768]{1,0:T(8,128)(2,1)}, bf16[128,768]{1,0:T(8,128)(2,1)S(1)}, u32[]{:S(2)}, u32[]{:S(2)}) collective-permute-start(bf16[128,768]{1,0:T(8,128)(2,1)} %get-tuple-element.42), channel_id=1, source_target_pairs={{0,259},{1,256},{2,257},{3,258},{64,323},{65,320},{66,321},{67,322... | collective-permute-start | bytes 589832 | tf_op jit(solution)/shard_map/ppermute | solution.py:108
  20.9 9.2 %collective-permute-start.5 = (bf16[36,512]{1,0:T(8,128)(2,1)S(1)}, bf16[36,512]{1,0:T(8,128)(2,1)S(1)}, u32[]{:S(2)}, u32[]{:S(2)}) collective-permute-start(bf16[36,512]{1,0:T(8,128)(2,1)S(1)} %get-tuple-element.80), channel_id=1, source_target_pairs={{0,68},{4,72},{8,76},{12,80},{16,84},{20,88},{24,92},{28,96},{32,1... | collective-permute-start | bytes 110600 | tf_op jit(solution)/shard_map/ppermute | solution.py:82
  26.5 6.9 %collective-permute-start.4 = (bf16[36,512]{1,0:T(8,128)(2,1)S(1)}, bf16[36,512]{1,0:T(8,128)(2,1)S(1)}, u32[]{:S(2)}, u32[]{:S(2)}) collective-permute-start(bf16[36,512]{1,0:T(8,128)(2,1)S(1)} %get-tuple-element.81), channel_id=1, source_target_pairs={{0,64},{4,68},{8,72},{12,76},{16,80},{20,84},{24,88},{28,92},{32,9... | collective-permute-start | bytes 110600 | tf_op jit(solution)/shard_map/ppermute | solution.py:82
  30.0 3.3 %collective-permute-start.3 = (bf16[36,512]{1,0:T(8,128)(2,1)S(1)}, bf16[36,512]{1,0:T(8,128)(2,1)S(1)}, u32[]{:S(2)}, u32[]{:S(2)}) collective-permute-start(bf16[36,512]{1,0:T(8,128)(2,1)S(1)} %get-tuple-element.82), channel_id=1, source_target_pairs={{0,4},{4,8},{8,12},{12,16},{16,20},{20,24},{24,28},{28,32},{32,36}... | collective-permute-start | bytes 110600 | tf_op jit(solution)/shard_map/ppermute | solution.py:82
  34.2 28.2 %collective-permute-start.10 = (bf16[3,128,768]{2,1,0:T(8,128)(2,1)S(1)}, bf16[3,128,768]{2,1,0:T(8,128)(2,1)S(1)}, u32[]{:S(2)}, u32[]{:S(2)}) collective-permute-start(bf16[3,128,768]{2,1,0:T(8,128)(2,1)S(1)} %shard_map.103.refs_1_.refs_12_), channel_id=1, source_target_pairs={{0,192},{64,0},{128,64},{192,128},{256,448},{320,256},{384,320},{4... | collective-permute-start | bytes 1769480 | tf_op jit(solution)/shard_map/ppermute | solution.py:119
  37.5 24.9 %collective-permute-start.9 = (bf16[3,128,768]{2,1,0:T(8,128)(2,1)S(1)}, bf16[3,128,768]{2,1,0:T(8,128)(2,1)S(1)}, u32[]{:S(2)}, u32[]{:S(2)}) collective-permute-start(bf16[3,128,768]{2,1,0:T(8,128)(2,1)S(1)} %shard_map.103.refs_1_.refs_12_), channel_id=1, source_target_pairs={{0,64},{64,128},{128,192},{192,0},{256,320},{320,384},{384,448},{4... | collective-permute-start | bytes 1769480 | tf_op jit(solution)/shard_map/ppermute | solution.py:119
  39.5 13.1 %collective-permute-start.8 = (bf16[128,768]{1,0:T(8,128)(2,1)S(1)}, bf16[128,768]{1,0:T(8,128)(2,1)S(1)}, u32[]{:S(2)}, u32[]{:S(2)}) collective-permute-start(bf16[128,768]{1,0:T(8,128)(2,1)S(1)} %copy-done.10), channel_id=1, source_target_pairs={{0,258},{1,259},{2,256},{3,257},{64,322},{65,323},{66,320},{67,321... | collective-permute-start | bytes 589832 | tf_op jit(solution)/shard_map/ppermute | solution.py:106
  45.0 11.4 %collective-permute-start.7 = (bf16[128,768]{1,0:T(8,128)(2,1)S(1)}, bf16[128,768]{1,0:T(8,128)(2,1)S(1)}, u32[]{:S(2)}, u32[]{:S(2)}) collective-permute-start(bf16[128,768]{1,0:T(8,128)(2,1)S(1)} %copy-done.10), channel_id=1, source_target_pairs={{0,3},{1,0},{2,1},{3,2},{64,67},{65,64},{66,65},{67,66},{128,131},... | collective-permute-start | bytes 589832 | tf_op jit(solution)/shard_map/ppermute | solution.py:107
  48.7 13.6 %collective-permute-start.6 = (bf16[128,768]{1,0:T(8,128)(2,1)S(1)}, bf16[128,768]{1,0:T(8,128)(2,1)S(1)}, u32[]{:S(2)}, u32[]{:S(2)}) collective-permute-start(bf16[128,768]{1,0:T(8,128)(2,1)S(1)} %copy-done.10), channel_id=1, source_target_pairs={{0,259},{1,256},{2,257},{3,258},{64,323},{65,320},{66,321},{67,322... | collective-permute-start | bytes 589832 | tf_op jit(solution)/shard_map/ppermute | solution.py:108
  63.2 16.4 %collective-permute-start.21 = (bf16[3,128,768]{2,1,0:T(8,128)(2,1)S(1)}, bf16[3,128,768]{2,1,0:T(8,128)(2,1)S(1)}, u32[]{:S(2)}, u32[]{:S(2)}) collective-permute-start(bf16[3,128,768]{2,1,0:T(8,128)(2,1)S(1)} %shard_map.104.refs_9_), channel_id=1, source_target_pairs={{0,192},{64,0},{128,64},{192,128},{256,448},{320,256},{384,320},{4... | collective-permute-start | bytes 1769480 | tf_op jit(solution)/shard_map/ppermute | solution.py:119
  68.2 16.4 %collective-permute-start.12 = (bf16[3,128,768]{2,1,0:T(8,128)(2,1)S(1)}, bf16[3,128,768]{2,1,0:T(8,128)(2,1)S(1)}, u32[]{:S(2)}, u32[]{:S(2)}) collective-permute-start(bf16[3,128,768]{2,1,0:T(8,128)(2,1)S(1)} %collective-permute-done.9.refs_2_.refs_13_), channel_id=1, source_target_pairs={{0,64},{64,128},{128,192},{192,0},{256,320},{320,384},{384,448},{4... | collective-permute-start | bytes 1769480 | tf_op jit(solution)/shard_map/ppermute | solution.py:119
  70.1 18.8 %collective-permute-start.11 = (bf16[3,128,768]{2,1,0:T(8,128)(2,1)S(1)}, bf16[3,128,768]{2,1,0:T(8,128)(2,1)S(1)}, u32[]{:S(2)}, u32[]{:S(2)}) collective-permute-start(bf16[3,128,768]{2,1,0:T(8,128)(2,1)S(1)} %shard_map.104.refs_9_), channel_id=1, source_target_pairs={{0,4},{4,0},{8,12},{12,8},{16,20},{20,16},{24,28},{28,24},{32,36},... | collective-permute-start | bytes 1769480 | tf_op jit(solution)/shard_map/ppermute | solution.py:114
  73.5 17.3 %collective-permute-start.13 = (bf16[3,128,768]{2,1,0:T(8,128)(2,1)S(1)}, bf16[3,128,768]{2,1,0:T(8,128)(2,1)S(1)}, u32[]{:S(2)}, u32[]{:S(2)}) collective-permute-start(bf16[3,128,768]{2,1,0:T(8,128)(2,1)S(1)} %shard_map.103.refs_1_.refs_12_), channel_id=1, source_target_pairs={{0,4},{4,0},{8,12},{12,8},{16,20},{20,16},{24,28},{28,24},{32,36},... | collective-permute-start | bytes 1769480 | tf_op jit(solution)/shard_map/ppermute | solution.py:114
  75.5 18.8 %collective-permute-start.16 = (bf16[3,128,768]{2,1,0:T(8,128)(2,1)S(1)}, bf16[3,128,768]{2,1,0:T(8,128)(2,1)S(1)}, u32[]{:S(2)}, u32[]{:S(2)}) collective-permute-start(bf16[3,128,768]{2,1,0:T(8,128)(2,1)S(1)} %collective-permute-done.10.refs_4_.refs_15_), channel_id=1, source_target_pairs={{0,4},{4,0},{8,12},{12,8},{16,20},{20,16},{24,28},{28,24},{32,36},... | collective-permute-start | bytes 1769480 | tf_op jit(solution)/shard_map/ppermute | solution.py:114
  79.5 14.7 %collective-permute-start.14 = (bf16[3,128,768]{2,1,0:T(8,128)(2,1)S(1)}, bf16[3,128,768]{2,1,0:T(8,128)(2,1)S(1)}, u32[]{:S(2)}, u32[]{:S(2)}) collective-permute-start(bf16[3,128,768]{2,1,0:T(8,128)(2,1)S(1)} %collective-permute-done.9.refs_2_.refs_13_), channel_id=1, source_target_pairs={{0,4},{4,0},{8,12},{12,8},{16,20},{20,16},{24,28},{28,24},{32,36},... | collective-permute-start | bytes 1769480 | tf_op jit(solution)/shard_map/ppermute | solution.py:114
  84.6 9.7 %collective-permute-start.15 = (bf16[3,128,768]{2,1,0:T(8,128)(2,1)S(1)}, bf16[3,128,768]{2,1,0:T(8,128)(2,1)S(1)}, u32[]{:S(2)}, u32[]{:S(2)}) collective-permute-start(bf16[3,128,768]{2,1,0:T(8,128)(2,1)S(1)} %collective-permute-done.12.refs_3_.refs_14_), channel_id=1, source_target_pairs={{0,4},{4,0},{8,12},{12,8},{16,20},{20,16},{24,28},{28,24},{32,36},... | collective-permute-start | bytes 1769480 | tf_op jit(solution)/shard_map/ppermute | solution.py:114
  88.9 17.1 %collective-permute-start.22 = (bf16[3,128,768]{2,1,0:T(8,128)(2,1)S(1)}, bf16[3,128,768]{2,1,0:T(8,128)(2,1)S(1)}, u32[]{:S(2)}, u32[]{:S(2)}) collective-permute-start(bf16[3,128,768]{2,1,0:T(8,128)(2,1)S(1)} %collective-permute-done.21.refs_12_), channel_id=1, source_target_pairs={{0,192},{64,0},{128,64},{192,128},{256,448},{320,256},{384,320},{4... | collective-permute-start | bytes 1769480 | tf_op jit(solution)/shard_map/ppermute | solution.py:119
  90.9 21.0 %collective-permute-start.20 = (bf16[3,128,768]{2,1,0:T(8,128)(2,1)S(1)}, bf16[3,128,768]{2,1,0:T(8,128)(2,1)S(1)}, u32[]{:S(2)}, u32[]{:S(2)}) collective-permute-start(bf16[3,128,768]{2,1,0:T(8,128)(2,1)S(1)} %shard_map.104.refs_9_), channel_id=1, source_target_pairs={{0,64},{64,128},{128,192},{192,0},{256,320},{320,384},{384,448},{4... | collective-permute-start | bytes 1769480 | tf_op jit(solution)/shard_map/ppermute | solution.py:119
  99.8 8.7 %collective-permute-start.17 = (bf16[36,512]{1,0:T(8,128)(2,1)S(1)}, bf16[36,512]{1,0:T(8,128)(2,1)S(1)}, u32[]{:S(2)}, u32[]{:S(2)}) collective-permute-start(bf16[36,512]{1,0:T(8,128)(2,1)S(1)} %get-tuple-element.54), channel_id=1, source_target_pairs={{0,4},{4,8},{8,12},{12,16},{16,20},{20,24},{24,28},{28,32},{32,36}... | collective-permute-start | bytes 110600 | tf_op jit(solution)/shard_map/ppermute | solution.py:82
  102.2 6.9 %collective-permute-start.18 = (bf16[36,512]{1,0:T(8,128)(2,1)S(1)}, bf16[36,512]{1,0:T(8,128)(2,1)S(1)}, u32[]{:S(2)}, u32[]{:S(2)}) collective-permute-start(bf16[36,512]{1,0:T(8,128)(2,1)S(1)} %get-tuple-element.55), channel_id=1, source_target_pairs={{0,64},{4,68},{8,72},{12,76},{16,80},{20,84},{24,88},{28,92},{32,9... | collective-permute-start | bytes 110600 | tf_op jit(solution)/shard_map/ppermute | solution.py:82
  104.1 7.7 %collective-permute-start.19 = (bf16[36,512]{1,0:T(8,128)(2,1)S(1)}, bf16[36,512]{1,0:T(8,128)(2,1)S(1)}, u32[]{:S(2)}, u32[]{:S(2)}) collective-permute-start(bf16[36,512]{1,0:T(8,128)(2,1)S(1)} %get-tuple-element.56), channel_id=1, source_target_pairs={{0,68},{4,72},{8,76},{12,80},{16,84},{20,88},{24,92},{28,96},{32,1... | collective-permute-start | bytes 110600 | tf_op jit(solution)/shard_map/ppermute | solution.py:82
  106.1 10.8 %collective-permute-start.24 = (bf16[3,128,768]{2,1,0:T(8,128)(2,1)S(1)}, bf16[3,128,768]{2,1,0:T(8,128)(2,1)S(1)}, u32[]{:S(2)}, u32[]{:S(2)}) collective-permute-start(bf16[3,128,768]{2,1,0:T(8,128)(2,1)S(1)} %collective-permute-done.22.refs_11_), channel_id=1, source_target_pairs={{0,4},{4,0},{8,12},{12,8},{16,20},{20,16},{24,28},{28,24},{32,36},... | collective-permute-start | bytes 1769480 | tf_op jit(solution)/shard_map/ppermute | solution.py:114
  111.9 5.0 %collective-permute-start.23 = (bf16[3,128,768]{2,1,0:T(8,128)(2,1)S(1)}, bf16[3,128,768]{2,1,0:T(8,128)(2,1)S(1)}, u32[]{:S(2)}, u32[]{:S(2)}) collective-permute-start(bf16[3,128,768]{2,1,0:T(8,128)(2,1)S(1)} %collective-permute-done.20.refs_10_), channel_id=1, source_target_pairs={{0,4},{4,0},{8,12},{12,8},{16,20},{20,16},{24,28},{28,24},{32,36},... | collective-permute-start | bytes 1769480 | tf_op jit(solution)/shard_map/ppermute | solution.py:114
  114.8 3.9 %collective-permute-start.25 = (bf16[3,128,768]{2,1,0:T(8,128)(2,1)S(1)}, bf16[3,128,768]{2,1,0:T(8,128)(2,1)S(1)}, u32[]{:S(2)}, u32[]{:S(2)}) collective-permute-start(bf16[3,128,768]{2,1,0:T(8,128)(2,1)S(1)} %collective-permute-done.21.refs_12_), channel_id=1, source_target_pairs={{0,4},{4,0},{8,12},{12,8},{16,20},{20,16},{24,28},{28,24},{32,36},... | collective-permute-start | bytes 1769480 | tf_op jit(solution)/shard_map/ppermute | solution.py:114
  130.1 7.5 %collective-permute-start.26 = (bf16[2,36,512]{2,1,0:T(8,128)(2,1)S(1)}, bf16[2,36,512]{2,1,0:T(8,128)(2,1)S(1)}, u32[]{:S(2)}, u32[]{:S(2)}) collective-permute-start(bf16[2,36,512]{2,1,0:T(8,128)(2,1)S(1)} %get-tuple-element.67), channel_id=1, source_target_pairs={{0,60},{4,0},{8,4},{12,8},{16,12},{20,16},{24,20},{28,24},{32,28},... | collective-permute-start | bytes 221192 | tf_op jit(solution)/shard_map/ppermute | solution.py:82
  130.2 7.4 %collective-permute-start.27 = (bf16[2,36,512]{2,1,0:T(8,128)(2,1)S(1)}, bf16[2,36,512]{2,1,0:T(8,128)(2,1)S(1)}, u32[]{:S(2)}, u32[]{:S(2)}) collective-permute-start(bf16[2,36,512]{2,1,0:T(8,128)(2,1)S(1)} %get-tuple-element.68), channel_id=1, source_target_pairs={{0,448},{4,452},{8,456},{12,460},{16,464},{20,468},{24,472},{28,47... | collective-permute-start | bytes 221192 | tf_op jit(solution)/shard_map/ppermute | solution.py:82
  133.0 6.7 %collective-permute-start.28 = (bf16[2,36,512]{2,1,0:T(8,128)(2,1)S(1)}, bf16[2,36,512]{2,1,0:T(8,128)(2,1)S(1)}, u32[]{:S(2)}, u32[]{:S(2)}) collective-permute-start(bf16[2,36,512]{2,1,0:T(8,128)(2,1)S(1)} %get-tuple-element.69), channel_id=1, source_target_pairs={{0,508},{4,448},{8,452},{12,456},{16,460},{20,464},{24,468},{28,47... | collective-permute-start | bytes 221192 | tf_op jit(solution)/shard_map/ppermute | solution.py:82
  146.5 5.6 %collective-permute-start.29 = (bf16[8,2,32,512]{3,2,1,0:T(8,128)(2,1)S(1)}, bf16[8,2,32,512]{3,2,1,0:T(8,128)(2,1)S(1)}, u32[]{:S(2)}, u32[]{:S(2)}) collective-permute-start(bf16[8,2,32,512]{3,2,1,0:T(8,128)(2,1)S(1)} %get-tuple-element.79), channel_id=1, source_target_pairs={{0,4},{4,0},{8,12},{12,8},{16,20},{20,16},{24,28},{28,24},{32,36},... | collective-permute-start | bytes 1572872 | tf_op jit(solution)/shard_map/ppermute | solution.py:114
  153.0 11.7 %all-to-all-start = ((bf16[8,64,512]{2,1,0:T(8,128)(2,1)}), bf16[8,64,512]{2,1,0:T(8,128)(2,1)S(1)}, u32[]{:S(2)}, u32[]{:S(2)}) async-start(bf16[8,64,512]{2,1,0:T(8,128)(2,1)} %bitcast.14), calls=%async_computation | async-start | bytes 1048576 | tf_op jit(solution)/shard_map/all_to_all | solution.py:412
  165.6 13.2 %all-to-all-start.1 = ((bf16[8,8,512]{2,1,0:T(8,128)(2,1)}), bf16[8,8,512]{2,1,0:T(8,128)(2,1)S(1)}, u32[]{:S(2)}, u32[]{:S(2)}) async-start(bf16[8,8,512]{2,1,0:T(8,128)(2,1)} %copy.45), calls=%async_computation.1 | async-start | bytes 131072 | tf_op jit(solution)/shard_map/all_to_all | solution.py:412
  (14 other events, 377.7 us)
